TPU v7x, 32 devices: a whole 2x2x4 slice. The times are simulated.
32 devices in a mesh: fsdp: 16 (over z, y, core), tp: 2 (over x).
Axes of the slice: x: 2, y: 2, z: 4, core: 2. Of those that a mesh axis runs over, the one named last changes fastest.
Arguments:
- points: bfloat16 [192, 512], P('fsdp'), may hold values from -6 to 6
- missing: int32 [192, 512], P('fsdp'), may hold values 0 or 1
- tok_hidden_w: bfloat16 [2, 640, 64], P('tp', 'fsdp'), may hold values from -0.75 to 0.75
- tok_hidden_b: bfloat16 [2, 640], P('tp', 'fsdp'), may hold values from -3 to 3
- tok_out_w: bfloat16 [1280, 1280], P('fsdp', 'tp'), may hold values from -0.15625 to 0.15625
- tok_res_w: bfloat16 [1280, 64], P('fsdp', 'tp'), may hold values from -0.75 to 0.75
- tok_out_b: bfloat16 [1280], P('fsdp'), may hold values from -3 to 3
- attn_gain: bfloat16 [1280], P('fsdp'), may hold values from 0.25 to 1.75
- qkv_w: bfloat16 [1280, 3, 1280], P('fsdp', None, 'tp'), may hold values from -0.15625 to 0.15625
- attn_out_w: bfloat16 [1280, 1280], P('fsdp', 'tp'), may hold values from -0.3125 to 0.3125
- mlp_gain: bfloat16 [1280], P('fsdp'), may hold values from 0.25 to 1.75
- mlp_in_w: bfloat16 [1280, 5120], P('fsdp', 'tp'), may hold values from -0.15625 to 0.15625
- mlp_in_b: bfloat16 [2, 2560], P('tp', 'fsdp'), may hold values from -3 to 3
- mlp_out_w: bfloat16 [1280, 5120], P('fsdp', 'tp'), may hold values from -0.078125 to 0.078125
- mlp_out_b: bfloat16 [1280], P('fsdp'), may hold values from -3 to 3
- cotangent: bfloat16 [3072, 1280], P('fsdp'), may hold values from -6 to 6
Outputs:
- output: bfloat16 [3072, 1280], P('fsdp')
- points_grad: float32 [192, 512], P('fsdp')
- grad_tok_hidden_w: float32 [2, 640, 64], P('tp', 'fsdp')
- grad_tok_hidden_b: float32 [2, 640], P('tp', 'fsdp')
- grad_tok_out_w: float32 [1280, 1280], P('fsdp', 'tp')
- grad_tok_res_w: float32 [1280, 64], P('fsdp', 'tp')
- grad_tok_out_b: float32 [1280], P('fsdp')
- grad_attn_gain: float32 [1280], P('fsdp')
- grad_qkv_w: float32 [1280, 3, 1280], P('fsdp', None, 'tp')
- grad_attn_out_w: float32 [1280, 1280], P('fsdp', 'tp')
- grad_mlp_gain: float32 [1280], P('fsdp')
- grad_mlp_in_w: float32 [1280, 5120], P('fsdp', 'tp')
- grad_mlp_in_b: float32 [2, 2560], P('tp', 'fsdp')
- grad_mlp_out_w: float32 [1280, 5120], P('fsdp', 'tp')
- grad_mlp_out_b: float32 [1280], P('fsdp')
Inputs may be any that keep to these rules, and one draw needn't show every extreme that they name: 1 marks a missing point, 0 an observed one.
All inputs are finite; a program needn't handle non-finite values. No bound on the sum of `missing` on one device may be relied on, other than what follows from the above.
Results may differ from a plain program's by a relative error of at most 0.02.
Values may be sent and summed in bfloat16 or wider, within the bound.
A program may use at most 192 MiB of HBM per device.

v0:
```python
import math

import jax
import jax.numpy as jnp
from jax import lax
from jax.sharding import PartitionSpec as P

D = 1280
HEAD_DIM = 80
PL = 32
CTXLEN = 16


def dot_plain(left, right):
    return jnp.dot(left, right, preferred_element_type=jnp.float32)


def dot_last(left, right):
    return lax.dot_general(
        left, right, (((1,), (1,)), ((), ())), preferred_element_type=jnp.float32
    )


def dot_rows(left, right):
    return lax.dot_general(
        left, right, (((0,), (0,)), ((), ())), preferred_element_type=jnp.float32
    )


def silu_slope(values):
    sigma = jax.nn.sigmoid(values)
    return sigma * (1.0 + values * (1.0 - sigma))


def rotary_tables():
    positions = jnp.arange(CTXLEN, dtype=jnp.float32)
    freqs = 10000.0 ** (-2.0 * jnp.arange(HEAD_DIM // 2, dtype=jnp.float32) / HEAD_DIM)
    angles = positions[:, None] * freqs[None, :]
    return (jnp.cos(angles)[None, :, None, :], jnp.sin(angles)[None, :, None, :])


def rotate(vector, cosine, sine):
    half = vector.shape[-1] // 2
    first = vector[..., :half]
    second = vector[..., half:]
    return jnp.concatenate(
        [first * cosine - second * sine, second * cosine + first * sine], axis=-1
    )


def rotate_back(vector, cosine, sine):
    half = vector.shape[-1] // 2
    first = vector[..., :half]
    second = vector[..., half:]
    return jnp.concatenate(
        [first * cosine + second * sine, second * cosine - first * sine], axis=-1
    )


def norm_stats(values):
    factor = lax.rsqrt(jnp.mean(values * values, axis=-1, keepdims=True) + 1e-06)
    return (factor, values * factor)


def norm_back(grad, normal, factor, gain):
    scaled = grad * gain
    inner = jnp.mean(scaled * normal, axis=-1, keepdims=True)
    return (factor * (scaled - normal * inner), jnp.sum(grad * normal, axis=0))


def body(
    points,
    missing,
    tok_hidden_w,
    tok_hidden_b,
    tok_out_w,
    tok_res_w,
    tok_out_b,
    attn_gain,
    qkv_w,
    attn_out_w,
    mlp_gain,
    mlp_in_w,
    mlp_in_b,
    mlp_out_w,
    mlp_out_b,
    cotangent,
):
    gathered = (
        lax.all_gather(tok_hidden_w, "fsdp", axis=1, tiled=True),
        lax.all_gather(tok_hidden_b, "fsdp", axis=1, tiled=True),
        lax.all_gather(tok_out_w, "fsdp", axis=0, tiled=True),
        lax.all_gather(tok_res_w, "fsdp", axis=0, tiled=True),
        lax.all_gather(tok_out_b, "fsdp", axis=0, tiled=True),
        lax.all_gather(attn_gain, "fsdp", axis=0, tiled=True),
        lax.all_gather(qkv_w, "fsdp", axis=0, tiled=True),
        lax.all_gather(attn_out_w, "fsdp", axis=0, tiled=True),
        lax.all_gather(mlp_gain, "fsdp", axis=0, tiled=True),
        lax.all_gather(mlp_in_w, "fsdp", axis=0, tiled=True),
        lax.all_gather(mlp_in_b, "fsdp", axis=1, tiled=True),
        lax.all_gather(mlp_out_w, "fsdp", axis=0, tiled=True),
        lax.all_gather(mlp_out_b, "fsdp", axis=0, tiled=True),
    )
    (
        hidden_full,
        hidden_bias,
        token_full,
        residual_full,
        token_bias,
        first_gain,
        project_full,
        attend_full,
        second_gain,
        inner_full,
        inner_bias,
        outer_full,
        outer_bias,
    ) = gathered
    contexts = points.shape[0]
    rows = contexts * CTXLEN
    tensor_rank = lax.axis_index("tp")
    kept_mask = (1 - missing).astype(jnp.float32).reshape(rows, PL)
    absent = missing.astype(jnp.float32).reshape(rows, PL)
    observed = points.astype(jnp.float32).reshape(rows, PL) * kept_mask
    features = jnp.concatenate([observed, absent], axis=1).astype(jnp.bfloat16)
    half_features = jnp.where(tensor_rank == 0, observed, absent).astype(jnp.bfloat16)
    hidden_matrix = hidden_full.reshape(-1, 2 * PL)
    pre_tok = dot_last(features, hidden_matrix) + hidden_bias.reshape(-1).astype(jnp.float32)
    hidden_tok = jax.nn.silu(pre_tok).astype(jnp.bfloat16)
    partial_tok = dot_last(hidden_tok, token_full) + dot_last(half_features, residual_full)
    embedded = lax.psum(partial_tok.astype(jnp.bfloat16), "tp").astype(jnp.float32)
    state_zero = embedded + token_bias.astype(jnp.float32)
    factor_one, normal_one = norm_stats(state_zero)
    normed_one = (normal_one * first_gain.astype(jnp.float32)).astype(jnp.bfloat16)
    local_width = project_full.shape[2]
    local_heads = local_width // HEAD_DIM
    project_matrix = project_full.reshape(D, 3 * local_width)
    projected = dot_plain(normed_one, project_matrix).reshape(
        contexts, CTXLEN, 3, local_heads, HEAD_DIM
    )
    cosine, sine = rotary_tables()
    queries = rotate(projected[:, :, 0], cosine, sine).astype(jnp.bfloat16)
    keys_rot = rotate(projected[:, :, 1], cosine, sine).astype(jnp.bfloat16)
    values_b = projected[:, :, 2].astype(jnp.bfloat16)
    scale = 1.0 / math.sqrt(HEAD_DIM)
    causal = jnp.arange(CTXLEN)[:, None] >= jnp.arange(CTXLEN)[None, :]

    def scores_of(left, right):
        raw = jnp.einsum("cihd,cjhd->chij", left, right, preferred_element_type=jnp.float32) * scale
        return jnp.where(causal, raw, -1e30)

    scores = scores_of(queries, keys_rot)
    row_top = jnp.max(scores, axis=-1, keepdims=True)
    log_total = row_top + jnp.log(jnp.sum(jnp.exp(scores - row_top), axis=-1, keepdims=True))
    probs_b = jnp.exp(scores - log_total).astype(jnp.bfloat16)
    attended = jnp.einsum("chij,cjhd->cihd", probs_b, values_b, preferred_element_type=jnp.float32)
    attended = attended.astype(jnp.bfloat16).reshape(rows, local_width)
    branch_attn = lax.psum(dot_last(attended, attend_full).astype(jnp.bfloat16), "tp").astype(
        jnp.float32
    )
    state_one = state_zero + branch_attn
    factor_two, normal_two = norm_stats(state_one)
    normed_two = (normal_two * second_gain.astype(jnp.float32)).astype(jnp.bfloat16)
    pre_mlp = dot_plain(normed_two, inner_full) + inner_bias.reshape(-1).astype(jnp.float32)
    activation = jax.nn.silu(pre_mlp).astype(jnp.bfloat16)
    branch_mlp = lax.psum(dot_last(activation, outer_full).astype(jnp.bfloat16), "tp").astype(
        jnp.float32
    )
    output = (state_one + branch_mlp + outer_bias.astype(jnp.float32)).astype(jnp.bfloat16)
    again = (
        lax.all_gather(tok_hidden_w, "fsdp", axis=1, tiled=True),
        lax.all_gather(tok_hidden_b, "fsdp", axis=1, tiled=True),
        lax.all_gather(tok_out_w, "fsdp", axis=0, tiled=True),
        lax.all_gather(tok_res_w, "fsdp", axis=0, tiled=True),
        lax.all_gather(tok_out_b, "fsdp", axis=0, tiled=True),
        lax.all_gather(attn_gain, "fsdp", axis=0, tiled=True),
        lax.all_gather(qkv_w, "fsdp", axis=0, tiled=True),
        lax.all_gather(attn_out_w, "fsdp", axis=0, tiled=True),
        lax.all_gather(mlp_gain, "fsdp", axis=0, tiled=True),
        lax.all_gather(mlp_in_w, "fsdp", axis=0, tiled=True),
        lax.all_gather(mlp_in_b, "fsdp", axis=1, tiled=True),
        lax.all_gather(mlp_out_w, "fsdp", axis=0, tiled=True),
        lax.all_gather(mlp_out_b, "fsdp", axis=0, tiled=True),
    )
    (
        hidden_full,
        hidden_bias,
        token_full,
        residual_full,
        token_bias,
        first_gain,
        project_full,
        attend_full,
        second_gain,
        inner_full,
        inner_bias,
        outer_full,
        outer_bias,
    ) = again
    hidden_matrix = hidden_full.reshape(-1, 2 * PL)
    project_matrix = project_full.reshape(D, 3 * local_width)
    grad_outer_bias = jnp.sum(cotangent, axis=0, dtype=jnp.float32)
    grad_outer = dot_rows(cotangent, activation)
    d_pre = (dot_plain(cotangent, outer_full) * silu_slope(pre_mlp)).astype(jnp.bfloat16)
    grad_inner_bias = jnp.sum(d_pre, axis=0, dtype=jnp.float32).reshape(1, -1)
    grad_inner = dot_rows(normed_two, d_pre)
    d_normed_two = lax.psum(dot_last(d_pre, inner_full).astype(jnp.bfloat16), "tp").astype(
        jnp.float32
    )
    through_two, grad_second_gain = norm_back(
        d_normed_two, normal_two, factor_two, second_gain.astype(jnp.float32)
    )
    d_state_one = cotangent.astype(jnp.float32) + through_two
    d_branch = d_state_one.astype(jnp.bfloat16)
    grad_attend = dot_rows(d_branch, attended)
    d_attended = (
        dot_plain(d_branch, attend_full)
        .astype(jnp.bfloat16)
        .reshape(contexts, CTXLEN, local_heads, HEAD_DIM)
    )
    probs = jnp.exp(scores_of(queries, keys_rot) - log_total)
    probs_b = probs.astype(jnp.bfloat16)
    d_probs = jnp.einsum(
        "cihd,cjhd->chij", d_attended, values_b, preferred_element_type=jnp.float32
    )
    d_values = jnp.einsum(
        "chij,cihd->cjhd", probs_b, d_attended, preferred_element_type=jnp.float32
    ).astype(jnp.bfloat16)
    row_inner = jnp.sum(probs * d_probs, axis=-1, keepdims=True)
    d_scores = (probs * (d_probs - row_inner)).astype(jnp.bfloat16)
    d_queries = (
        jnp.einsum("chij,cjhd->cihd", d_scores, keys_rot, preferred_element_type=jnp.float32)
        * scale
    )
    d_keys = (
        jnp.einsum("chij,cihd->cjhd", d_scores, queries, preferred_element_type=jnp.float32) * scale
    )
    d_queries = rotate_back(d_queries, cosine, sine).astype(jnp.bfloat16)
    d_keys = rotate_back(d_keys, cosine, sine).astype(jnp.bfloat16)
    d_projected = jnp.stack([d_queries, d_keys, d_values], axis=2).reshape(rows, 3 * local_width)
    grad_project = dot_rows(normed_one, d_projected).reshape(D, 3, local_width)
    d_normed_one = lax.psum(
        dot_last(d_projected, project_matrix).astype(jnp.bfloat16), "tp"
    ).astype(jnp.float32)
    through_one, grad_first_gain = norm_back(
        d_normed_one, normal_one, factor_one, first_gain.astype(jnp.float32)
    )
    d_state_zero = d_state_one + through_one
    grad_token_bias = jnp.sum(d_state_zero, axis=0)
    d_embedded = d_state_zero.astype(jnp.bfloat16)
    grad_token = dot_rows(d_embedded, hidden_tok)
    grad_residual = dot_rows(d_embedded, half_features)
    d_pre_tok = (dot_plain(d_embedded, token_full) * silu_slope(pre_tok)).astype(jnp.bfloat16)
    grad_hidden_bias = jnp.sum(d_pre_tok, axis=0, dtype=jnp.float32).reshape(1, -1)
    grad_hidden = dot_rows(d_pre_tok, features).reshape(1, -1, 2 * PL)
    through_hidden = dot_plain(d_pre_tok, hidden_matrix)[:, :PL]
    through_residual = dot_plain(d_embedded, residual_full)
    point_terms = through_hidden + jnp.where(tensor_rank == 0, through_residual, 0.0)
    point_sums = lax.psum(point_terms, "tp")
    points_grad = (point_sums * kept_mask).reshape(contexts, CTXLEN * PL)
    owned = (
        lax.psum_scatter(grad_hidden, "fsdp", scatter_dimension=1, tiled=True),
        lax.psum_scatter(grad_hidden_bias, "fsdp", scatter_dimension=1, tiled=True),
        lax.psum_scatter(grad_token, "fsdp", scatter_dimension=0, tiled=True),
        lax.psum_scatter(grad_residual, "fsdp", scatter_dimension=0, tiled=True),
        lax.psum_scatter(grad_token_bias, "fsdp", scatter_dimension=0, tiled=True),
        lax.psum_scatter(grad_first_gain, "fsdp", scatter_dimension=0, tiled=True),
        lax.psum_scatter(grad_project, "fsdp", scatter_dimension=0, tiled=True),
        lax.psum_scatter(grad_attend, "fsdp", scatter_dimension=0, tiled=True),
        lax.psum_scatter(grad_second_gain, "fsdp", scatter_dimension=0, tiled=True),
        lax.psum_scatter(grad_inner, "fsdp", scatter_dimension=0, tiled=True),
        lax.psum_scatter(grad_inner_bias, "fsdp", scatter_dimension=1, tiled=True),
        lax.psum_scatter(grad_outer, "fsdp", scatter_dimension=0, tiled=True),
        lax.psum_scatter(grad_outer_bias, "fsdp", scatter_dimension=0, tiled=True),
    )
    return (
        output,
        points_grad,
        owned[0],
        owned[1],
        owned[2],
        owned[3],
        owned[4],
        owned[5],
        owned[6],
        owned[7],
        owned[8],
        owned[9],
        owned[10],
        owned[11],
        owned[12],
    )


def solution(mesh):
    placed = (
        P("fsdp", None),
        P("fsdp", None),
        P("tp", "fsdp", None),
        P("tp", "fsdp"),
        P("fsdp", "tp"),
        P("fsdp", "tp"),
        P("fsdp"),
        P("fsdp"),
        P("fsdp", None, "tp"),
        P("fsdp", "tp"),
        P("fsdp"),
        P("fsdp", "tp"),
        P("tp", "fsdp"),
        P("fsdp", "tp"),
        P("fsdp"),
        P("fsdp", None),
    )
    return jax.shard_map(
        body,
        mesh=mesh,
        in_specs=placed,
        out_specs=(
            P("fsdp", None),
            P("fsdp", None),
            P("tp", "fsdp", None),
            P("tp", "fsdp"),
            P("fsdp", "tp"),
            P("fsdp", "tp"),
            P("fsdp"),
            P("fsdp"),
            P("fsdp", None, "tp"),
            P("fsdp", "tp"),
            P("fsdp"),
            P("fsdp", "tp"),
            P("tp", "fsdp"),
            P("fsdp", "tp"),
            P("fsdp"),
        ),
        check_vma=False,
    )
```

profile of v0, /device:TPU:0, one launch (start us, length us, event | category | flops | bytes accessed | tf_op | source)
XLA Modules:
  0.0 1227.0 jit_solution(17082060551213386069)
XLA Ops:
  8.0 1.3 fusion.55
  11.9 0.9 dynamic-update-slice.3
  12.8 0.8 dynamic-update-slice.2
  13.7 0.8 dynamic-update-slice.1
  14.5 0.8 dynamic-update-slice.5
  15.6 0.8 dynamic-update-slice
  16.4 63.1 %all-reduce.13 = (bf16[2560]{0:T(1024)(128)(2,1)S(1)}, bf16[1280]{0:T(1024)(128)(2,1)S(1)}, bf16[640]{0:T(1024)(128)(2,1)S(1)}, bf16[1280]{0:T(1024)(128)(2,1)S(...) all-reduce(bf16[2560]{0:T(1024)(128)(2,1)S(1)} %dynamic-update-slic, ...), channel_id=1, replica_groups=mesh['fsdp'=16,'tp'=2] {'fsdp'}, use_global_device_ids=true, to_apply=%add.4 | all-reduce | flops 8320 | bytes 33280
  79.5 0.8 subtract_convert_fusion.4
  80.5 0.8 reshape.238
  81.6 17.8 %all-gather = bf16[16,80,32]{1,2,0:T(8,128)(2,1)S(1)} all-gather(bf16[1,80,32]{1,2,0:T(8,128)(2,1)} %bitcast.114), channel_id=1, replica_groups=mesh['fsdp'=16,'tp'=2] {'fsdp'}, dimensions={0}, use_global_device_ids=true | all-gather | bytes 87040 | tf_op jit(solution)/shard_map/all_gather | solution.py:93
  99.6 19.7 %all_gather.48 = bf16[1,640,64]{2,1,0:T(8,128)(2,1)S(1)} all-gather(bf16[1,40,64]{2,1,0:T(8,128)(2,1)} %param.18), channel_id=1, replica_groups=mesh['fsdp'=16,'tp'=2] {'fsdp'}, dimensions={1}, use_global_device_ids=true | all-gather | bytes 87040 | tf_op jit(solution)/shard_map/all_gather | solution.py:90
  120.3 2.3 fusion.52
  122.6 1.1 fusion.1
  125.2 23.8 %all-reduce.20.cloned.1.call-done = bf16[192,1280]{1,0:T(8,128)(2,1)} async-done(((bf16[192,1280]{1,0:T(8,128)(2,1)}), bf16[192,1280]{1,0:T(8,128)(2,1)}) %all-reduce.20.cloned.1.call-update) | async-done | bytes 491536 | tf_op jit(solution)/shard_map/psum | solution.py:131
  149.1 1.2 multiply_reduce_fusion.1
  150.3 1.2 multiply_convert_fusion.2
  151.5 54.2 %all-gather.9.cloned.1.call-done = bf16[1280,3,640]{2,0,1:T(8,128)(2,1)} async-done(((bf16[80,3,640]{2,0,1:T(8,128)(2,1)}), bf16[1280,3,640]{2,0,1:T(8,128)(2,1)}) %all-gather.9.cloned.1.call-update) | async-done | bytes 4915216 | tf_op jit(solution)/shard_map/all_gather | solution.py:96
  205.7 8.2 copy.61
  213.9 3.8 fusion.57
  220.2 26.0 %all-gather.11.cloned.1.call-done = bf16[1280,640]{1,0:T(8,128)(2,1)} async-done(((bf16[80,640]{1,0:T(8,128)(2,1)}), bf16[1280,640]{1,0:T(8,128)(2,1)}) %all-gather.11.cloned.1.call-update) | async-done | bytes 1638416 | tf_op jit(solution)/shard_map/all_gather | solution.py:97
  246.2 2.9 convolution_convert_fusion.3
  250.7 25.4 %all-reduce.22.cloned.1.call-done = bf16[192,1280]{1,0:T(8,128)(2,1)} async-done(((bf16[192,1280]{1,0:T(8,128)(2,1)}), bf16[192,1280]{1,0:T(8,128)(2,1)}) %all-reduce.22.cloned.1.call-update) | async-done | bytes 491536 | tf_op jit(solution)/shard_map/psum | solution.py:158
  276.1 1.3 multiply_reduce_fusion
  277.4 64.2 %all-gather.13.cloned.1.call-done = bf16[1280,2560]{1,0:T(8,128)(2,1)} async-done(((bf16[80,2560]{1,0:T(8,128)(2,1)}), bf16[1280,2560]{1,0:T(8,128)(2,1)}) %all-gather.13.cloned.1.call-update) | async-done | bytes 6553616 | tf_op jit(solution)/shard_map/all_gather | solution.py:99
  341.6 5.9 convolution_add_fusion
  347.5 58.4 %all-gather.15.cloned.1.call-done = bf16[1280,2560]{1,0:T(8,128)(2,1)} async-done(((bf16[80,2560]{1,0:T(8,128)(2,1)}), bf16[1280,2560]{1,0:T(8,128)(2,1)}) %all-gather.15.cloned.1.call-update) | async-done | bytes 6553616 | tf_op jit(solution)/shard_map/all_gather | solution.py:101
  405.9 5.7 convert_reduce_fusion
  411.6 0.9 copy-done.16
  412.5 3.0 convolution_convert_fusion.1
  415.7 6.6 convolution_convert_fusion.2
  422.3 19.9 %all-reduce.24.cloned.1.call-done = bf16[192,1280]{1,0:T(8,128)(2,1)} async-done(((bf16[192,1280]{1,0:T(8,128)(2,1)}), bf16[192,1280]{1,0:T(8,128)(2,1)}) %all-reduce.24.cloned.1.call-update) | async-done | bytes 491536 | tf_op jit(solution)/shard_map/psum | solution.py:207
  442.2 2.2 fusion.17
  444.9 3.0 convolution_convert_fusion.6
  447.9 1.4 reshape.231
  449.7 1.6 multiply_reduce_fusion.2
  453.9 0.9 reshape.232
  454.9 4.4 convolution_convert_fusion
  459.4 1.5 reshape_bitcast_fusion
  461.0 37.3 %all-reduce.26.cloned.1.call-done = (bf16[192,1280]{1,0:T(8,128)(2,1)}, bf16[192,1280]{1,0:T(8,128)(2,1)}) async-done(((bf16[192,1280]{1,0:T(8,128)(2,1)}, bf16[192,1280]{1,0:T(8,128)(2,1)}), (bf16[192,1280]{1,0:T(8,128)(2,1)}, bf16[192,1280]{1,0:T(8,128)(2,1)})) %all-reduce.26.cloned.1.call-update) | async-done | bytes 983056 | tf_op jit(solution)/shard_map/psum | solution.py:166
  498.2 1.5 fusion.18
  499.8 2.9 fusion.53
  502.7 1.2 fusion.58
  504.1 2.1 convert_reduce_fusion.2
  506.9 1.0 fusion.41
  508.2 3.7 fusion.33
  511.9 1.0 copy-done.13
  512.9 2.4 fusion.51
  515.4 1.0 copy-done.11
  516.3 5.2 fusion.20
  521.7 7.9 fusion.50
  529.6 8.5 convolution_bitcast_fusion
  538.2 14.0 %copy.84 = f32[1280,2560]{1,0:T(8,128)} copy(f32[1280,2560]{0,1:T(8,128)} %convolution_bitcast_fusion) | data formatting | bytes 26214400
  553.6 7.1 reduce-scatter.28.cloned.1.call-done
  560.7 1.5 copy.83
  562.7 8.4 psum.47
  571.2 0.7 reshape.233
  571.9 57.8 %all-reduce.12 = (f32[1,640]{1,0:T(1,128)S(1)}, f32[1280]{0:T(1024)S(1)}, f32[1280]{0:T(1024)S(1)}, f32[1280]{0:T(1024)S(1)}, f32[1280]{0:T(1024)S(1)}) all-reduce(f32[1,640]{1,0:T(1,128)S(1)} %reshape.235, f32[1280]{0:T(1024)S(1)} %get-tuple-element.77, ...), channel_id=3, replica_groups=mesh['fsdp'=16,'tp'=2] {'fsdp'}, use_global_device_ids=true, to_apply=%region_15.16.clone | all-reduce | flops 5760 | bytes 46080
  632.6 1.5 copy.81
  634.0 41.9 %reduce-scatter.32.cloned.1.call-done = f32[1,40,64]{2,0,1:T(1,128)} async-done(((f32[1,640,64]{2,0,1:T(1,128)}), f32[1,40,64]{2,0,1:T(1,128)}) %reduce-scatter.32.cloned.1.call-update) | async-done | bytes 10256
  676.0 70.8 %reduce-scatter.22.cloned.1.call-done = f32[80,640]{1,0:T(8,128)} async-done(((f32[1280,640]{1,0:T(8,128)}), f32[80,640]{1,0:T(8,128)}) %reduce-scatter.22.cloned.1.call-update) | async-done | bytes 204816 | tf_op jit(solution)/shard_map/reduce_scatter | solution.py:269
  746.7 70.0 %reduce-scatter.18.cloned.1.call-done = f32[80,640]{1,0:T(8,128)} async-done(((f32[1280,640]{1,0:T(8,128)}), f32[80,640]{1,0:T(8,128)}) %reduce-scatter.18.cloned.1.call-update) | async-done | bytes 204816 | tf_op jit(solution)/shard_map/reduce_scatter | solution.py:264
  816.7 118.5 %reduce-scatter.20.cloned.1.call-done = f32[80,3,640]{2,0,1:T(8,128)} async-done(((f32[1280,3,640]{2,0,1:T(8,128)}), f32[80,3,640]{2,0,1:T(8,128)}) %reduce-scatter.20.cloned.1.call-update) | async-done | bytes 614416 | tf_op jit(solution)/shard_map/reduce_scatter | solution.py:268
  935.2 143.2 %reduce-scatter.24.cloned.1.call-done = f32[80,2560]{1,0:T(8,128)} async-done(((f32[1280,2560]{1,0:T(8,128)}), f32[80,2560]{1,0:T(8,128)}) %reduce-scatter.24.cloned.1.call-update) | async-done | bytes 819216 | tf_op jit(solution)/shard_map/reduce_scatter | solution.py:271
  1078.4 142.0 %reduce-scatter.30.cloned.1.call-done = f32[80,2560]{1,0:T(8,128)} async-done(((f32[1280,2560]{1,0:T(8,128)}), f32[80,2560]{1,0:T(8,128)}) %reduce-scatter.30.cloned.1.call-update) | async-done | bytes 819216
  (171 shorter events, 17.1 us)
Async XLA Ops:
  7.2 113.1 %all-gather.7.cloned.1.call-start = ((), (), s32[]{:S(2)}) async-start(), calls=%async_computation.8 | async-start | bytes 1740800 | tf_op jit(solution)/shard_map/all_gather | solution.py:92
  7.9 141.2 %all-reduce.20.cloned.1.call-start = ((), (), s32[]{:S(2)}) async-start(), calls=%async_computation.9 | async-start | bytes 983040 | tf_op jit(solution)/shard_map/psum | solution.py:131
  99.6 23.0 %copy-start.19 = (bf16[1280,32]{0,1:T(8,128)(2,1)}, bf16[1280,32]{0,1:T(8,128)(2,1)S(1)}, u32[]{:S(2)}) copy-start(bf16[1280,32]{0,1:T(8,128)(2,1)S(1)} %reshape.260) | copy-start | bytes 245764
  119.4 0.7 copy-start.14
  119.4 3.2 copy-start.23
  120.0 2.6 copy-start.21
  120.3 3.4 copy-start.12
  123.7 82.0 %all-gather.9.cloned.1.call-start = ((), (), s32[]{:S(2)}) async-start(), calls=%async_computation.10 | async-start | bytes 5222400 | tf_op jit(solution)/shard_map/all_gather | solution.py:96
  124.5 121.8 %all-gather.11.cloned.1.call-start = ((), (), s32[]{:S(2)}) async-start(), calls=%async_computation.11 | async-start | bytes 1740800 | tf_op jit(solution)/shard_map/all_gather | solution.py:97
  125.0 151.0 %all-reduce.22.cloned.1.call-start = ((), (), s32[]{:S(2)}) async-start(), calls=%async_computation.12 | async-start | bytes 983040 | tf_op jit(solution)/shard_map/psum | solution.py:158
  125.1 88.8 %copy-start.25 = (f32[1280]{0:T(1024)}, f32[1280]{0:T(1024)S(1)}, u32[]{:S(2)}) copy-start(f32[1280]{0:T(1024)S(1)} %convert_element_type.147) | copy-start | bytes 15364
  125.2 92.7 %copy-start.27 = (f32[16,40]{1,0:T(8,128)}, f32[16,40]{1,0:T(8,128)S(1)}, u32[]{:S(2)}) copy-start(f32[16,40]{1,0:T(8,128)S(1)} %get-tuple-element.99) | copy-start | bytes 7684
  125.2 92.7 %copy-start.29 = (f32[16,40]{1,0:T(8,128)}, f32[16,40]{1,0:T(8,128)S(1)}, u32[]{:S(2)}) copy-start(f32[16,40]{1,0:T(8,128)S(1)} %get-tuple-element.100) | copy-start | bytes 7684
  150.3 63.6 %copy-start.34 = (f32[192]{0:T(256)}, f32[192]{0:T(256)S(1)}, u32[]{:S(2)}) copy-start(f32[192]{0:T(256)S(1)} %add_rsqrt_fusion.1) | copy-start | bytes 2308
  151.5 62.4 %copy-start.10 = (bf16[192,1280]{1,0:T(8,128)(2,1)}, bf16[192,1280]{1,0:T(8,128)(2,1)S(1)}, u32[]{:S(2)}) copy-start(bf16[192,1280]{1,0:T(8,128)(2,1)S(1)} %multiply_convert_fusion.2) | copy-start | bytes 1474564
  217.7 1.7 copy-start.4
  218.5 1.2 copy-start.5
  218.5 1.2 copy-start.7
  220.2 57.2 %copy-start.9 = (bf16[192,640]{1,0:T(8,128)(2,1)}, bf16[192,640]{1,0:T(8,128)(2,1)S(1)}, u32[]{:S(2)}) copy-start(bf16[192,640]{1,0:T(8,128)(2,1)S(1)} %reshape.230) | copy-start | bytes 737284
  220.2 55.9 %copy-start = (bf16[192,1280]{1,0:T(8,128)(2,1)S(1)}, bf16[192,1280]{1,0:T(8,128)(2,1)}, u32[]{:S(2)}) copy-start(bf16[192,1280]{1,0:T(8,128)(2,1)} %all-reduce.20.cloned.1.call-done) | copy-start | bytes 1474564
  249.1 92.5 %all-gather.13.cloned.1.call-start = ((), (), s32[]{:S(2)}) async-start(), calls=%async_computation.13 | async-start | bytes 6963200 | tf_op jit(solution)/shard_map/all_gather | solution.py:99
  249.7 156.2 %all-gather.15.cloned.1.call-start = ((), (), s32[]{:S(2)}) async-start(), calls=%async_computation.14 | async-start | bytes 6963200 | tf_op jit(solution)/shard_map/all_gather | solution.py:101
  250.5 191.7 %all-reduce.24.cloned.1.call-start = ((), (), s32[]{:S(2)}) async-start(), calls=%async_computation.15 | async-start | bytes 983040 | tf_op jit(solution)/shard_map/psum | solution.py:207
  277.4 167.0 %copy-start.31 = (f32[192]{0:T(256)}, f32[192]{0:T(256)S(1)}, u32[]{:S(2)}) copy-start(f32[192]{0:T(256)S(1)} %add_rsqrt_fusion) | copy-start | bytes 2308
  277.4 128.5 %copy-start.2 = (bf16[192,1280]{1,0:T(8,128)(2,1)S(1)}, bf16[192,1280]{1,0:T(8,128)(2,1)}, u32[]{:S(2)}) copy-start(bf16[192,1280]{1,0:T(8,128)(2,1)} %param.31) | copy-start | bytes 1474564
  405.9 6.6 copy-start.40
  411.6 0.9 copy-start.16
  415.6 26.6 %copy-start.1 = (bf16[192,1280]{1,0:T(8,128)(2,1)S(1)}, bf16[192,1280]{1,0:T(8,128)(2,1)}, u32[]{:S(2)}) copy-start(bf16[192,1280]{1,0:T(8,128)(2,1)} %all-reduce.22.cloned.1.call-done) | copy-start | bytes 1474564
  415.6 82.6 %all-reduce.26.cloned.1.call-start = ((), (), s32[]{:S(2)}) async-start(), calls=%async_computation.24 | async-start | bytes 1966080 | tf_op jit(solution)/shard_map/psum | solution.py:166
  444.4 0.6 copy-start.37
  449.7 1.8 copy-start.6
  449.7 1.8 copy-start.8
  451.5 0.9 copy-start.28
  451.6 0.9 copy-start.30
  454.9 4.5 copy-start.39
  454.9 4.5 copy-start.36
  459.3 39.0 %copy-start.26 = (f32[1280]{0:T(1024)S(1)}, f32[1280]{0:T(1024)}, u32[]{:S(2)}) copy-start(f32[1280]{0:T(1024)} %copy-done.25) | copy-start | bytes 15364
  459.3 39.0 %copy-start.35 = (f32[192]{0:T(256)S(1)}, f32[192]{0:T(256)}, u32[]{:S(2)}) copy-start(f32[192]{0:T(256)} %copy-done.34) | copy-start | bytes 2308
  459.3 40.5 %copy-start.3 = (bf16[192,1280]{1,0:T(8,128)(2,1)S(1)}, bf16[192,1280]{1,0:T(8,128)(2,1)}, u32[]{:S(2)}) copy-start(bf16[192,1280]{1,0:T(8,128)(2,1)} %all-reduce.24.cloned.1.call-done) | copy-start | bytes 1474564
  459.3 40.5 %copy-start.32 = (f32[192]{0:T(256)S(1)}, f32[192]{0:T(256)}, u32[]{:S(2)}) copy-start(f32[192]{0:T(256)} %copy-done.31) | copy-start | bytes 2308
  459.3 40.5 %copy-start.38 = (f32[192]{0:T(256)S(1)}, f32[192]{0:T(256)}, u32[]{:S(2)}) copy-start(f32[192]{0:T(256)} %copy-done.37) | copy-start | bytes 2308
  459.3 101.4 %reduce-scatter.28.cloned.1.call-start = ((), (), s32[]{:S(2)}) async-start(), calls=%async_computation.21 | async-start | bytes 1392640
  460.9 171.7 %reduce-scatter.26.cloned.1.call-start = ((), (), s32[]{:S(2)}) async-start(), calls=%async_computation.20 | async-start | bytes 696320
  499.8 3.0 copy-start.22
  504.0 2.9 copy-start.24
  504.0 171.9 %reduce-scatter.32.cloned.1.call-start = ((), (), s32[]{:S(2)}) async-start(), calls=%async_computation.23 | async-start | bytes 348160
  506.2 0.7 copy-start.17
  507.9 238.8 %reduce-scatter.22.cloned.1.call-start = ((), (), s32[]{:S(2)}) async-start(), calls=%async_computation.18 | async-start | bytes 3481600 | tf_op jit(solution)/shard_map/reduce_scatter | solution.py:269
  511.8 1.0 copy-start.13
  511.8 304.9 %reduce-scatter.18.cloned.1.call-start = ((), (), s32[]{:S(2)}) async-start(), calls=%async_computation.16 | async-start | bytes 3481600 | tf_op jit(solution)/shard_map/reduce_scatter | solution.py:264
  515.3 1.0 copy-start.11
  515.3 419.8 %reduce-scatter.20.cloned.1.call-start = ((), (), s32[]{:S(2)}) async-start(), calls=%async_computation.17 | async-start | bytes 10444800 | tf_op jit(solution)/shard_map/reduce_scatter | solution.py:268
  521.6 556.8 %reduce-scatter.24.cloned.1.call-start = ((), (), s32[]{:S(2)}) async-start(), calls=%async_computation.19 | async-start | bytes 13926400 | tf_op jit(solution)/shard_map/reduce_scatter | solution.py:271
  529.6 690.9 %reduce-scatter.30.cloned.1.call-start = ((), (), s32[]{:S(2)}) async-start(), calls=%async_computation.22 | async-start | bytes 13926400
  552.2 10.0 copy-start.20
  552.2 10.2 copy-start.15
  552.2 10.2 copy-start.18
  552.2 19.7 %copy-start.33 = (f32[1280]{0:T(1024)S(1)}, f32[1280]{0:T(1024)}, u32[]{:S(2)}) copy-start(f32[1280]{0:T(1024)} %get-tuple-element.60) | copy-start | bytes 15364
Sparse Core Ops, SparseCore 0:
  10.2 42.8 all-gather.6
  123.9 25.1 all-reduce.19
  151.3 54.3 all-gather.8
  207.7 38.4 all-gather.10
  249.2 26.7 all-reduce.21
  278.2 63.3 all-gather.12
  343.9 61.9 all-gather.14
  415.7 26.4 all-reduce.23
  459.4 38.7 all-reduce.25
  502.1 58.4 reduce-scatter.27
  564.2 55.2 reduce-scatter.25
  623.8 52.1 reduce-scatter.31
  680.8 65.8 reduce-scatter.21
  751.0 65.7 reduce-scatter.17
  821.9 113.2 reduce-scatter.19
  940.2 138.1 reduce-scatter.23
  1082.9 137.4 reduce-scatter.29
where the time goes:
time: 1230 us
  waiting for transfers between devices  906 us (74%)
  blocking collectives  167 us (14%)
  matrix products  75.1 us (6%)
  local copies, waits for them, and re-layouts  45.8 us (4%)
  between operations  18 us (1%)
  other arithmetic  14.2 us (1%)
    unnamed x21, waiting for transfers between devices  194 us
    reduce_scatter x1, waiting for transfers between devices, body(): lax.psum_scatter(grad_inner, 'fsdp', scatter_dimension=0, tiled=True)  143 us
    unnamed x2, blocking collectives  121 us
    reduce_scatter x1, waiting for transfers between devices, body(): lax.psum_scatter(grad_project, 'fsdp', scatter_dimension=0, tiled=True)  118 us
    reduce_scatter x1, waiting for transfers between devices, body(): lax.psum_scatter(grad_attend, 'fsdp', scatter_dimension=0, tiled=True)  70.8 us
    reduce_scatter x1, waiting for transfers between devices, body(): lax.psum_scatter(grad_token, 'fsdp', scatter_dimension=0, tiled=True)  70 us
    all_gather x1, waiting for transfers between devices, body(): lax.all_gather(mlp_in_w, 'fsdp', axis=0, tiled=True)  64.2 us
    all_gather x1, waiting for transfers between devices, body(): lax.all_gather(mlp_out_w, 'fsdp', axis=0, tiled=True)  58.4 us
  transfers between devices with their start and end apart: 17, of which 15 were waited for; matrix products, arithmetic and copies ran while one was open for 8% of the time, Pallas kernels for 0%

commit v1 on v0

--- a/solution.py
+++ b/solution.py
@@ -2,7 +2,10 @@
 
 import jax
 import jax.numpy as jnp
+import numpy as np
 from jax import lax
+from jax.experimental import pallas as pl
+from jax.experimental.pallas import tpu as pltpu
 from jax.sharding import PartitionSpec as P
 
 D = 1280
@@ -292,6 +295,752 @@
     )
 
 
+MESH = pl.DeviceIdType.MESH
+RING = 8
+TOK = 384
+OWN = 192
+BLOCK = 160
+HALF = 80
+C_TO, C_QKV, C_AT, C_IN, C_OUT, C_ALL = 128, 512, 1536, 1920, 3200, 4480
+CHUNKS = ((0, 512), (512, 512), (1024, 512), (1536, 384), (1920, 640), (2560, 640), (3200, 640), (3840, 640))
+RB_ROW = (0, 80, 240, 400)
+RB_LEN = (80, 160, 160, 160)
+TILE = 256
+TILES = D // TILE
+SCALE = 1.0 / math.sqrt(HEAD_DIM)
+
+
+def iota(shape, dim):
+    return lax.broadcasted_iota(jnp.int32, shape, dim)
+
+
+def layer_kernel(
+    fe_in, cot_in, sp_in, pt_in, win_in, wout_in, rot_c, rot_a, rot_b,
+    out_o, pts_o, go_o, gin_o, gout_o, gsp_o,
+    w, g, rb, fe, cot, spx, part, pre, act, dpre, n1, n2, db, x0, x1,
+    hc, dpe, pret, q_s, k_s, v_s, att, datt, dpj, ps, fs, gspf, gbs, ghs, hidf, hid, vec, bin_s, sums, ptx, ptr,
+    cs, cr, xs, xr,
+    ag_s, ag_r, rs_s, rs_r, ar_s, ar_r, nx_s, nx_r, in_s, in_r, lo_s, fin_s, fin_r, pt_s, pt_r,
+):
+    f32, bf16 = jnp.float32, jnp.bfloat16
+    f = lax.axis_index("fsdp")
+    x = lax.axis_index("tp")
+    chip = lax.div(f, 2)
+    c = f - 2 * chip
+    zz = lax.div(chip, 2)
+    yy = chip - 2 * zz
+    pos = zz + yy * (7 - 2 * zz)
+
+    def chip_at(p):
+        p = lax.rem(p + 2 * RING, RING)
+        h = lax.div(p, 4)
+        return 2 * (p + h * (7 - 2 * p)) + h
+
+    nxt = {"fsdp": 2 * chip_at(pos + 1) + c}
+    prv = {"fsdp": 2 * chip_at(pos - 1) + c}
+    mate = {"fsdp": f + 1 - 2 * c}
+    across = {"tp": 1 - x}
+    other = 1 - c
+    own0 = pl.multiple_of(OWN * c, OWN)
+    oth0 = pl.multiple_of(OWN * other, OWN)
+
+    def m16(v):
+        return pl.multiple_of(v, 16)
+
+    def remote(src, dst, s_sem, r_sem, to):
+        return pltpu.make_async_remote_copy(
+            src_ref=src, dst_ref=dst, send_sem=s_sem, recv_sem=r_sem, device_id=to, device_id_type=MESH
+        )
+
+    sent = []
+
+    def go(copy):
+        copy.start()
+        sent.append(copy)
+
+    barrier = pltpu.get_barrier_semaphore()
+    for to in (nxt, prv, mate, across):
+        pl.semaphore_signal(barrier, inc=1, device_id=to, device_id_type=MESH)
+    pl.semaphore_wait(barrier, 4)
+
+    def piece(k, half):
+        if k == 0:
+            return pt_in.at[half, :, 0:384], 128, 384
+        lo, width = CHUNKS[k]
+        if lo < C_IN:
+            return pt_in.at[half, :, lo - C_TO : lo - C_TO + width], lo, width
+        src, base = (win_in, C_IN) if lo < C_OUT else (wout_in, C_OUT)
+        start = pl.multiple_of(1280 * half + (lo - base), 128)
+        return src.at[:, pl.ds(start, width)], lo, width
+
+    myrow = m16(BLOCK * chip)
+    locals_in = {}
+    for k in range(len(CHUNKS)):
+        if k == 0:
+            r = remote(sp_in, spx, in_s.at[8], in_r.at[8], mate)
+            go(r)
+            sp_copy = pltpu.make_async_copy(sp_in, w.at[pl.ds(myrow, BLOCK), 0:128], lo_s.at[8])
+            sp_copy.start()
+            fe_copy = pltpu.make_async_copy(fe_in, fe.at[pl.ds(own0, OWN)], lo_s.at[9])
+            fe_copy.start()
+            fe_send = remote(fe_in, fe.at[pl.ds(own0, OWN)], in_s.at[9], in_r.at[9], mate)
+            go(fe_send)
+        src, lo, width = piece(k, other)
+        dst = w.at[pl.ds(m16(myrow + HALF * c), HALF), lo : lo + width]
+        go(remote(src, dst, in_s.at[k], in_r.at[k], mate))
+        src, lo, width = piece(k, c)
+        cp = pltpu.make_async_copy(src, dst, lo_s.at[k])
+        cp.start()
+        locals_in[k] = cp
+    cot_copy = pltpu.make_async_copy(cot_in, cot.at[pl.ds(own0, OWN)], lo_s.at[10])
+    cot_copy.start()
+    cot_send = remote(cot_in, cot.at[pl.ds(own0, OWN)], in_s.at[10], in_r.at[10], mate)
+    go(cot_send)
+
+    def own_block_ready(k):
+        locals_in[k].wait()
+        _, lo, width = piece(k, c)
+        arrived = w.at[pl.ds(m16(myrow + HALF * other), HALF), lo : lo + width]
+        remote(arrived, arrived, in_s.at[k], in_r.at[k], mate).wait_recv()
+        if k == 0:
+            sp_copy.wait()
+            remote(spx, spx, in_s.at[8], in_r.at[8], mate).wait_recv()
+            mine = w[pl.ds(myrow, BLOCK), 0:128]
+            theirs = jnp.where(iota((BLOCK, 128), 1) >= 65, spx[...].astype(f32), 0.0)
+            w[pl.ds(myrow, BLOCK), 0:128] = (mine.astype(f32) + theirs).astype(bf16)
+
+    def ag_ref(k, p, s, d):
+        lo, width = CHUNKS[k]
+        row = BLOCK * chip_at(p)
+        if s == 3:
+            return w.at[pl.ds(m16(row + HALF * d), HALF), lo : lo + width]
+        return w.at[pl.ds(m16(row), BLOCK), lo : lo + width]
+
+    def ag_recv(k, s, d):
+        ref = ag_ref(k, pos - 1 - s if d == 0 else pos + 1 + s, s, d)
+        remote(ref, ref, ag_s.at[k, s, d], ag_r.at[k, s, d], nxt if d == 0 else prv).wait_recv()
+
+    def ag_send(k, s):
+        if s == 0:
+            own_block_ready(k)
+        for d in (0, 1):
+            if s > 0:
+                ag_recv(k, s - 1, d)
+            ref = ag_ref(k, pos - s if d == 0 else pos + s, s, d)
+            go(remote(ref, ref, ag_s.at[k, s, d], ag_r.at[k, s, d], nxt if d == 0 else prv))
+
+    def ag_slot(t):
+        for s in (3, 2, 1, 0):
+            if 0 <= t - s < len(CHUNKS):
+                ag_send(t - s, s)
+
+    def ag_done(k):
+        for d in (0, 1):
+            ag_recv(k, 3, d)
+
+    def rs_send(k, s):
+        lo, width = CHUNKS[k]
+        cols = slice(lo, lo + width)
+        for d in (0, 1):
+            block = m16(BLOCK * chip_at(pos + 4 - s if d == 0 else pos - 4 + s))
+            if s == 0:
+                src = g.at[pl.ds(m16(block + HALF * d), HALF), cols]
+            else:
+                rs_recv(k, s - 1, d)
+                first = m16(block + HALF * d) if s == 1 else block
+                rs_add(first, d, RB_ROW[s - 1], RB_LEN[s - 1], cols)
+                src = g.at[pl.ds(block, BLOCK), cols]
+            dst = rb.at[d, RB_ROW[s] : RB_ROW[s] + RB_LEN[s], cols]
+            go(remote(src, dst, rs_s.at[k, s, d], rs_r.at[k, s, d], nxt if d == 0 else prv))
+
+    def rs_recv(k, s, d):
+        lo, width = CHUNKS[k]
+        ref = rb.at[d, RB_ROW[s] : RB_ROW[s] + RB_LEN[s], lo : lo + width]
+        remote(ref, ref, rs_s.at[k, s, d], rs_r.at[k, s, d], nxt if d == 0 else prv).wait_recv()
+
+    def rs_add(row, d, rb_row, length, cols):
+        def step(i, carry):
+            here = pl.ds(m16(row + 16 * i), 16)
+            g[here, cols] = g[here, cols] + rb[d, pl.ds(m16(rb_row + 16 * i), 16), cols]
+            return carry
+
+        lax.fori_loop(0, length // 16, step, 0)
+
+    def grad_ref(k, half):
+        lo, width = CHUNKS[k]
+        if k == 0:
+            return go_o.at[half, :, 0:384]
+        if lo < C_IN:
+            return go_o.at[half, :, lo - C_TO : lo - C_TO + width]
+        dst, base = (gin_o, C_IN) if lo < C_OUT else (gout_o, C_OUT)
+        return dst.at[:, pl.ds(pl.multiple_of(1280 * half + (lo - base), 128), width)]
+
+    def rs_last(k):
+        lo, width = CHUNKS[k]
+        for d in (0, 1):
+            rs_recv(k, 3, d)
+        if k == 0:
+            total = g[pl.ds(myrow, BLOCK), 0:128].astype(f32)
+            total = total + rb[0, 400:560, 0:128].astype(f32) + rb[1, 400:560, 0:128].astype(f32)
+            gsp_o[c, :, :] = total
+            go(remote(gsp_o.at[c], gsp_o.at[c], fin_s.at[8], fin_r.at[8], mate))
+            lo, width = 128, 384
+        cols = slice(lo, lo + width)
+
+        def total_at(start):
+            rows = pl.ds(m16(myrow + start), 16)
+            there = pl.ds(m16(400 + start), 16)
+            return g[rows, cols].astype(f32) + (rb[0, there, cols].astype(f32) + rb[1, there, cols].astype(f32))
+
+        def theirs(i, carry):
+            fs[pl.ds(m16(16 * i), 16), cols] = total_at(HALF * other + 16 * i)
+            return carry
+
+        lax.fori_loop(0, HALF // 16, theirs, 0)
+        go(remote(fs.at[:, cols], grad_ref(k, c), fin_s.at[k], fin_r.at[k], mate))
+        mine_ref = grad_ref(k, c)
+
+        def mine(i, carry):
+            mine_ref[pl.ds(m16(16 * i), 16), :] = total_at(HALF * c + 16 * i)
+            return carry
+
+        lax.fori_loop(0, HALF // 16, mine, 0)
+
+    rs_at = {}
+
+    def rs_start(k):
+        rs_send(k, 0)
+        rs_at[k] = 1
+
+    def rs_tick(only=None):
+        for k in list(rs_at):
+            if only is not None and k not in only:
+                continue
+            s = rs_at[k]
+            if s < 4:
+                rs_send(k, s)
+                rs_at[k] = s + 1
+            else:
+                rs_last(k)
+                del rs_at[k]
+
+    def ar_tile(i):
+        return slice(TILE * i, TILE * i + TILE)
+
+    def ar_begin(a, left, lo, width):
+        b = a % 2
+        if a >= 2:
+            for i in range(TILES):
+                done = cs.at[b, :, ar_tile(i)]
+                remote(done, done, ar_s.at[a - 2, 0, i], ar_r.at[a - 2, 0, i], mate).wait_send()
+        for i in range(TILES):
+            part[:, ar_tile(i)] = dot_last(left[...], w[ar_tile(i), lo : lo + width])
+            cs[b, :, ar_tile(i)] = part[pl.ds(oth0, OWN), ar_tile(i)].astype(bf16)
+            copy = remote(cs.at[b, :, ar_tile(i)], cr.at[b, :, ar_tile(i)], ar_s.at[a, 0, i], ar_r.at[a, 0, i], mate)
+            copy.start()
+            if a >= 3:
+                sent.append(copy)
+
+    def ar_mid(a):
+        b = a % 2
+        if a >= 2:
+            for i in range(TILES):
+                done = xs.at[b, :, ar_tile(i)]
+                remote(done, done, ar_s.at[a - 2, 1, i], ar_r.at[a - 2, 1, i], across).wait_send()
+        for i in range(TILES):
+            here = cr.at[b, :, ar_tile(i)]
+            remote(here, here, ar_s.at[a, 0, i], ar_r.at[a, 0, i], mate).wait_recv()
+            xs[b, :, ar_tile(i)] = (
+                part[pl.ds(own0, OWN), ar_tile(i)] + cr[b, :, ar_tile(i)].astype(f32)
+            ).astype(bf16)
+            copy = remote(
+                xs.at[b, :, ar_tile(i)], xr.at[a % 3, :, ar_tile(i)], ar_s.at[a, 1, i], ar_r.at[a, 1, i], across
+            )
+            copy.start()
+            if a >= 3:
+                sent.append(copy)
+
+    def ar_end(a):
+        for i in range(TILES):
+            here = xr.at[a % 3, :, ar_tile(i)]
+            remote(here, here, ar_s.at[a, 1, i], ar_r.at[a, 1, i], across).wait_recv()
+
+    def summed(a, rows):
+        return xs[a % 2, rows, :].astype(f32) + xr[a % 3, rows, :].astype(f32)
+
+    def own_rows(body, block=32):
+        def step(j, carry):
+            start = pl.multiple_of(block * j, block)
+            body(pl.ds(start, block), pl.ds(m16(own0 + start), block))
+            return carry
+
+        lax.fori_loop(0, OWN // block, step, 0)
+
+    def share(j, ref):
+        rows = ref.at[pl.ds(own0, OWN)]
+        go(remote(rows, rows, nx_s.at[j], nx_r.at[j], mate))
+
+    def shared(j, ref):
+        rows = ref.at[pl.ds(oth0, OWN)]
+        remote(rows, rows, nx_s.at[j], nx_r.at[j], mate).wait_recv()
+
+    def rms(v):
+        return lax.rsqrt(jnp.mean(v * v, axis=-1, keepdims=True) + 1e-06)
+
+    def fold(v):
+        return jnp.sum(v.reshape(v.shape[0] // 8, 8, v.shape[1]), axis=0)
+
+    def tiles_loop(count, body):
+        def step(i, carry):
+            body(pl.ds(pl.multiple_of(TILE * i, TILE), TILE), i)
+            return carry
+
+        lax.fori_loop(0, count, step, 0)
+
+    def grad_block(left, right, lo, width, dst):
+        def body(rows, i):
+            g[rows, dst : dst + width] = dot_rows(left[:, rows], right[:, lo : lo + width]).astype(bf16)
+
+        tiles_loop(TILES, body)
+
+    for t in range(5):
+        ag_slot(t) if t < 4 else None
+    sums[...] = jnp.zeros(sums.shape, f32)
+    ag_done(0)
+    ag_slot(4)
+
+    lane = iota((64, 128), 1)
+    row = iota((64, 128), 0)
+    hidf[320:384, :] = jnp.where((row < PL) & (lane == PL * x + row), 1.0, 0.0)
+    for p in range(RING):
+        hidf[40 * p : 40 * p + 40, :] = w[BLOCK * p : BLOCK * p + 48, 0:128].astype(f32)[:40]
+    hid[...] = hidf[...].astype(bf16)
+    fe_copy.wait()
+    arrived = fe.at[pl.ds(oth0, OWN)]
+    remote(arrived, arrived, in_s.at[9], in_r.at[9], mate).wait_recv()
+    pret[...] = dot_last(fe[...], hid[...])
+    lane = iota((TOK, 384), 1)
+    v = pret[...]
+    hc[...] = jnp.where(
+        lane < 320, v * jax.nn.sigmoid(v), jnp.where(lane < 352, v, jnp.where(lane == 352, 1.0, 0.0))
+    ).astype(bf16)
+    ar_begin(0, hc, C_TO, 384)
+    sel = jnp.where(iota((16, 128), 1) == 97 + iota((16, 128), 0), 1.0, 0.0)
+    sel = jnp.where(iota((16, 128), 0) < 4, sel, 0.0).astype(bf16)
+    vec[...] = dot_last(sel, w[:, 384:512])
+    sel = jnp.where(iota((16, 128), 1) == 65 + iota((16, 128), 0), 1.0, 0.0)
+    sel = jnp.where(iota((16, 128), 0) < 2, sel, 0.0).astype(bf16)
+    for q in range(4):
+        both = dot_last(sel, w[pl.ds(m16(640 * c + 160 * q), 160), 0:128])
+        bin_s[0:1, 320 * q : 320 * q + 160] = both[0:1]
+        bin_s[0:1, 320 * q + 160 : 320 * q + 320] = both[1:2]
+    ar_mid(0)
+    ag_slot(5)
+    ar_end(0)
+
+    def first_norm(rows, mine):
+        v = summed(0, rows) + vec[3:4, :]
+        x0[rows, :] = v
+        n1[mine, :] = (v * rms(v) * vec[0:1, :]).astype(bf16)
+
+    own_rows(first_norm)
+    share(0, n1)
+    ag_done(1)
+    ag_slot(6)
+    ag_done(2)
+    shared(0, n1)
+
+    def project(cols, i):
+        part[:, cols] = dot_plain(n1[...], w[:, pl.ds(pl.multiple_of(C_QKV + TILE * i, TILE), TILE)])
+
+    tiles_loop(4, project)
+
+    def turn(j, carry):
+        rows = pl.ds(m16(16 * j), 16)
+        v = part[rows, 0:1024]
+        v = v * rot_c[...] + pltpu.roll(v, 984, 1) * rot_a[...] + pltpu.roll(v, 40, 1) * rot_b[...]
+        q_s[rows, :] = v[:, 0:384].astype(bf16)
+        k_s[rows, :] = pltpu.roll(v, 704, 1)[:, 0:384].astype(bf16)
+        v_s[rows, :] = v[:, 640:1024].astype(bf16)
+        return carry
+
+    lax.fori_loop(0, TOK // 16, turn, 0)
+
+    def stacked(v):
+        head = iota((128, 384), 1)
+        return jnp.concatenate(
+            [
+                jnp.where((head >= HEAD_DIM * h) & (head < HEAD_DIM * h + HEAD_DIM), v, jnp.zeros_like(v))
+                for h in range(4)
+            ],
+            axis=0,
+        )
+
+    def side(v):
+        return jnp.concatenate([v[128 * h : 128 * h + 128] for h in range(4)], axis=1)
+
+    def attend(b, carry):
+        rows = pl.ds(pl.multiple_of(128 * b, 128), 128)
+        scores = dot_last(stacked(q_s[rows, :]), k_s[rows, :]) * SCALE
+        qi = iota((512, 128), 0) & 127
+        kj = iota((512, 128), 1)
+        allowed = ((qi >> 4) == (kj >> 4)) & (kj <= qi)
+        scores = jnp.where(allowed, scores, -1e30)
+        e = jnp.exp(scores - jnp.max(scores, axis=-1, keepdims=True))
+        probs = e * (1.0 / jnp.sum(e, axis=-1, keepdims=True))
+        ps[pl.ds(pl.multiple_of(512 * b, 512), 512), :] = probs
+        att[rows, :] = dot_plain(side(probs.astype(bf16)), stacked(v_s[rows, :])).astype(bf16)
+        return carry
+
+    lax.fori_loop(0, 3, attend, 0)
+    ag_slot(7)
+    ag_done(3)
+    ar_begin(1, att, C_AT, 384)
+    ag_slot(8)
+    ar_mid(1)
+    ag_done(4)
+    ag_slot(9)
+    ar_end(1)
+
+    def second_norm(rows, mine):
+        v = x0[rows, :] + summed(1, rows)
+        x1[rows, :] = v
+        n2[mine, :] = (v * rms(v) * vec[1:2, :]).astype(bf16)
+
+    own_rows(second_norm)
+    share(1, n2)
+    ag_done(5)
+    ag_slot(10)
+    shared(1, n2)
+
+    def inner(cols, i):
+        v = dot_plain(n2[...], w[:, pl.ds(pl.multiple_of(C_IN + TILE * i, 128), TILE)]) + bin_s[0:1, cols]
+        pre[:, cols] = v
+        act[:, cols] = (v * jax.nn.sigmoid(v)).astype(bf16)
+
+    tiles_loop(TILES, inner)
+
+    cot_copy.wait()
+    arrived = cot.at[pl.ds(oth0, OWN)]
+    remote(arrived, arrived, in_s.at[10], in_r.at[10], mate).wait_recv()
+    grad_block(cot, act, 0, 640, 3200)
+    rs_start(6)
+    grad_block(cot, act, 640, 640, 3840)
+    rs_start(7)
+    ag_done(6)
+    ag_done(7)
+
+    def outer_back(cols, i):
+        v = pre[:, cols]
+        s = jax.nn.sigmoid(v)
+        d = dot_plain(cot[...], w[:, pl.ds(pl.multiple_of(C_OUT + TILE * i, 128), TILE)])
+        dpre[:, cols] = (d * (s * (1.0 + v * (1.0 - s)))).astype(bf16)
+
+    tiles_loop(TILES, outer_back)
+    ar_begin(2, dpre, C_IN, 1280)
+    rs_tick()
+    ar_mid(2)
+    grad_block(n2, dpre, 0, 640, 1920)
+    rs_start(4)
+    rs_tick()
+    grad_block(n2, dpre, 640, 640, 2560)
+    rs_start(5)
+    ar_end(2)
+
+    def second_back(rows, mine):
+        dn = summed(2, rows)
+        v = x1[rows, :]
+        r = rms(v)
+        xh = v * r
+        scaled = dn * vec[1:2, :]
+        inside = jnp.mean(scaled * xh, axis=-1, keepdims=True)
+        ct = cot[mine, :].astype(f32)
+        d = ct + r * (scaled - xh * inside)
+        pre[rows, :] = d
+        db[mine, :] = d.astype(bf16)
+        sums[8:16, :] += fold(dn * xh)
+        sums[16:24, :] += fold(ct)
+
+    own_rows(second_back)
+    share(2, db)
+    ar_begin(3, act, C_OUT, 1280)
+    ar_mid(3)
+    shared(2, db)
+
+    def attend_back(cols, i):
+        datt[:, cols] = dot_plain(db[...], w[:, pl.ds(pl.multiple_of(C_AT + 128 * i, 128), 128)]).astype(bf16)
+
+    for i in range(3):
+        attend_back(slice(128 * i, 128 * i + 128), i)
+
+    def attention_back(b, carry):
+        rows = pl.ds(pl.multiple_of(128 * b, 128), 128)
+        probs = ps[pl.ds(pl.multiple_of(512 * b, 512), 512), :]
+        heads_d = stacked(datt[rows, :])
+        dp = dot_last(heads_d, v_s[rows, :])
+        ds = (probs * (dp - jnp.sum(probs * dp, axis=-1, keepdims=True))).astype(bf16)
+        part[rows, 0:384] = dot_plain(side(ds), stacked(k_s[rows, :])) * SCALE
+        part[rows, 320:704] = dot_rows(ds, stacked(q_s[rows, :])) * SCALE
+        part[rows, 640:1024] = dot_rows(probs.astype(bf16), heads_d)
+        return carry
+
+    lax.fori_loop(0, 3, attention_back, 0)
+
+    def turn_back(j, carry):
+        rows = pl.ds(m16(16 * j), 16)
+        v = part[rows, 0:1024]
+        v = v * rot_c[...] - pltpu.roll(v, 984, 1) * rot_a[...] - pltpu.roll(v, 40, 1) * rot_b[...]
+        dpj[rows, :] = v.astype(bf16)
+        return carry
+
+    lax.fori_loop(0, TOK // 16, turn_back, 0)
+    rs_tick()
+    ar_begin(4, dpj, C_QKV, 1024)
+    ar_end(3)
+
+    def finish(rows, mine):
+        out_o[rows, :] = (x1[rows, :] + summed(3, rows) + vec[2:3, :]).astype(bf16)
+
+    own_rows(finish)
+    ar_mid(4)
+    grad_block(db, att, 0, 384, C_AT)
+    rs_start(3)
+    rs_tick()
+    grad_block(n1, dpj, 0, 512, 512)
+    rs_start(1)
+    rs_tick()
+    grad_block(n1, dpj, 512, 512, 1024)
+    rs_start(2)
+    ar_end(4)
+
+    de = act
+
+    def first_back(rows, mine):
+        dn = summed(4, rows)
+        v = x0[rows, :]
+        r = rms(v)
+        xh = v * r
+        scaled = dn * vec[0:1, :]
+        inside = jnp.mean(scaled * xh, axis=-1, keepdims=True)
+        d = pre[rows, :] + r * (scaled - xh * inside)
+        de[mine, :] = d.astype(bf16)
+        sums[0:8, :] += fold(dn * xh)
+
+    own_rows(first_back)
+    share(3, de)
+    rs_tick()
+    shared(3, de)
+
+    v = pret[...]
+    s = jax.nn.sigmoid(v)
+    lane = iota((TOK, 384), 1)
+    d = dot_plain(de[...], w[:, C_TO : C_TO + 384])
+    dpe[...] = jnp.where(lane < 320, d * (s * (1.0 + v * (1.0 - s))), jnp.where(lane < 352, d, 0.0)).astype(bf16)
+    ptx[...] = dot_plain(dpe[...], hid[...])
+    go(remote(ptx.at[pl.ds(oth0, OWN)], ptr.at[0], pt_s.at[0], pt_r.at[0], mate))
+
+    pick = jnp.where(iota((32, 128), 1) == 97 + (iota((32, 128), 0) >> 3), 1.0, 0.0)
+    pick = jnp.where(iota((32, 128), 0) < 24, pick, 0.0).astype(bf16)
+
+    def grad_tok(rows, i):
+        val = dot_rows(de[:, rows], hc[...])
+        g[rows, 128:384] = val[:, 0:256].astype(bf16)
+        g[rows, 384:512] = (val[:, 256:384] + dot_rows(sums[:, rows].astype(bf16), pick)).astype(bf16)
+
+    tiles_loop(TILES, grad_tok)
+    ghs[...] = dot_rows(dpe[...], fe[...])
+    ones = jnp.where((iota((TOK, 128), 1) >= 65) & (iota((TOK, 128), 1) <= 66), 1.0, 0.0).astype(bf16)
+
+    def bias_cols(rows, i):
+        gbs[rows, :] = dot_rows(dpre[:, rows], ones)
+
+    tiles_loop(TILES, bias_cols)
+    gspf[...] = jnp.zeros(gspf.shape, f32)
+    for p in range(RING):
+        gspf[BLOCK * p : BLOCK * p + 40, :] = ghs[40 * p : 40 * p + 40, :]
+    lane = iota((BLOCK, 128), 1)
+    for q in range(4):
+        rows = pl.ds(m16(640 * c + 160 * q), 160)
+        first = jnp.where(lane == 65, gbs[320 * q : 320 * q + 160, :], 0.0)
+        second = jnp.where(lane == 66, gbs[320 * q + 160 : 320 * q + 320, :], 0.0)
+        gspf[rows, :] = gspf[rows, :] + first + second
+
+    def small_cols(rows, i):
+        g[rows, 0:128] = gspf[rows, :].astype(bf16)
+
+    tiles_loop(TILES, small_cols)
+    rs_start(0)
+    remote(ptr.at[0], ptr.at[0], pt_s.at[0], pt_r.at[0], mate).wait_recv()
+    ptr[1] = ptx[pl.ds(own0, OWN), :] + ptr[0]
+    go(remote(ptr.at[1], ptr.at[2], pt_s.at[1], pt_r.at[1], across))
+    while rs_at:
+        rs_tick()
+    remote(ptr.at[2], ptr.at[2], pt_s.at[1], pt_r.at[1], across).wait_recv()
+    pts_o[...] = ptr[1] + ptr[2]
+    for k in range(len(CHUNKS)):
+        there = grad_ref(k, other)
+        remote(there, there, fin_s.at[k], fin_r.at[k], mate).wait_recv()
+    there = gsp_o.at[other]
+    remote(there, there, fin_s.at[8], fin_r.at[8], mate).wait_recv()
+    for copy in sent:
+        copy.wait_send()
+
+
+def rotary_lanes():
+    lanes = np.arange(1024)
+    inside = lanes % HEAD_DIM
+    turned = lanes < 640
+    freqs = 10000.0 ** (-2.0 * (inside % 40) / HEAD_DIM)
+    angles = np.arange(CTXLEN)[:, None] * freqs[None, :]
+    cosine = np.where(turned, np.cos(angles), 1.0)
+    sine = np.where(turned, np.sin(angles), 0.0)
+    lower = np.where(inside < 40, -sine, 0.0)
+    upper = np.where(inside >= 40, sine, 0.0)
+    return [np.asarray(t, np.float32) for t in (cosine, lower, upper)]
+
+
+def fast_body(
+    points, missing, tok_hidden_w, tok_hidden_b, tok_out_w, tok_res_w, tok_out_b, attn_gain, qkv_w, attn_out_w,
+    mlp_gain, mlp_in_w, mlp_in_b, mlp_out_w, mlp_out_b, cotangent,
+):
+    f32, bf16 = jnp.float32, jnp.bfloat16
+    f = lax.axis_index("fsdp")
+    core = lax.rem(f, 2)
+    contexts = points.shape[0]
+    rows = contexts * CTXLEN
+    kept = (1 - missing).astype(bf16)
+    feats = jnp.concatenate(
+        [
+            (points * kept).reshape(rows, PL),
+            missing.astype(bf16).reshape(rows, PL),
+            jnp.ones((rows, 1), bf16),
+            jnp.zeros((rows, 63), bf16),
+        ],
+        axis=1,
+    )
+    hidden = jnp.concatenate([tok_hidden_w[0], tok_hidden_b[0][:, None]], axis=1)
+    small = jnp.pad(hidden, ((0, 120), (0, 63)))
+    lane = lax.broadcasted_iota(jnp.int32, (BLOCK, 128), 1)
+    small = jnp.where(lane == 65 + core, mlp_in_b[0][:, None], small)
+    vectors = jnp.stack([attn_gain, mlp_gain, mlp_out_b, tok_out_b], axis=1)
+    tok = tok_out_w.reshape(HALF, 8, 2, 40)
+    qkv = qkv_w.reshape(HALF, 3, 2, 320)
+
+    def zeros(n):
+        return jnp.zeros((HALF, n), bf16)
+
+    packed = jnp.stack(
+        [
+            jnp.concatenate(
+                [
+                    tok[:, :, h].reshape(HALF, 320),
+                    zeros(16 * h), tok_res_w[:, 16 * h : 16 * h + 16], zeros(16 - 16 * h + 1),
+                    vectors, zeros(27),
+                    qkv[:, :, h].reshape(HALF, 960), zeros(64),
+                    attn_out_w[:, 320 * h : 320 * h + 320], zeros(64),
+                ],
+                axis=1,
+            )
+            for h in (0, 1)
+        ]
+    )
+    any_space = pl.BlockSpec(memory_space=pl.ANY)
+    vmem = pl.BlockSpec(memory_space=pltpu.VMEM)
+
+    def sems(*shape):
+        return pltpu.SemaphoreType.DMA(shape)
+
+    out, pts, go, gin, gout, gsp = pl.pallas_call(
+        layer_kernel,
+        out_shape=(
+            jax.ShapeDtypeStruct((OWN, D), bf16),
+            jax.ShapeDtypeStruct((OWN, 128), f32),
+            jax.ShapeDtypeStruct((2, HALF, 1792), f32),
+            jax.ShapeDtypeStruct((HALF, 2560), f32),
+            jax.ShapeDtypeStruct((HALF, 2560), f32),
+            jax.ShapeDtypeStruct((2, BLOCK, 128), f32),
+        ),
+        in_specs=[any_space] * 6 + [vmem] * 3,
+        out_specs=[vmem] * 6,
+        scratch_shapes=[
+            pltpu.VMEM((D, C_ALL), bf16),
+            pltpu.VMEM((D, C_ALL), bf16),
+            pltpu.VMEM((2, 560, C_ALL), bf16),
+            pltpu.VMEM((TOK, 128), bf16),
+            pltpu.VMEM((TOK, D), bf16),
+            pltpu.VMEM((BLOCK, 128), bf16),
+            pltpu.VMEM((TOK, D), f32),
+            pltpu.VMEM((TOK, D), f32),
+            pltpu.VMEM((TOK, D), bf16),
+            pltpu.VMEM((TOK, D), bf16),
+            pltpu.VMEM((TOK, D), bf16),
+            pltpu.VMEM((TOK, D), bf16),
+            pltpu.VMEM((TOK, D), bf16),
+            pltpu.VMEM((OWN, D), f32),
+            pltpu.VMEM((OWN, D), f32),
+            pltpu.VMEM((TOK, 384), bf16),
+            pltpu.VMEM((TOK, 384), bf16),
+            pltpu.VMEM((TOK, 384), f32),
+            pltpu.VMEM((TOK, 384), bf16),
+            pltpu.VMEM((TOK, 384), bf16),
+            pltpu.VMEM((TOK, 384), bf16),
+            pltpu.VMEM((TOK, 384), bf16),
+            pltpu.VMEM((TOK, 384), bf16),
+            pltpu.VMEM((TOK, 1024), bf16),
+            pltpu.VMEM((1536, 128), f32),
+            pltpu.VMEM((HALF, C_ALL), f32),
+            pltpu.VMEM((D, 128), f32),
+            pltpu.VMEM((D, 128), f32),
+            pltpu.VMEM((TOK, 128), f32),
+            pltpu.VMEM((TOK, 128), f32),
+            pltpu.VMEM((TOK, 128), bf16),
+            pltpu.VMEM((16, D), f32),
+            pltpu.VMEM((8, D), f32),
+            pltpu.VMEM((32, D), f32),
+            pltpu.VMEM((TOK, 128), f32),
+            pltpu.VMEM((3, OWN, 128), f32),
+            pltpu.VMEM((2, OWN, D), bf16),
+            pltpu.VMEM((2, OWN, D), bf16),
+            pltpu.VMEM((2, OWN, D), bf16),
+            pltpu.VMEM((3, OWN, D), bf16),
+            sems(8, 4, 2), sems(8, 4, 2), sems(8, 4, 2), sems(8, 4, 2),
+            sems(5, 2, TILES), sems(5, 2, TILES),
+            sems(4), sems(4), sems(11), sems(11), sems(11), sems(9), sems(9), sems(2), sems(2),
+        ],
+        compiler_params=pltpu.CompilerParams(
+            collective_id=0, has_side_effects=True, vmem_limit_bytes=64 * 1024 * 1024 - 512 * 1024
+        ),
+        cost_estimate=pl.CostEstimate(flops=13 * 10**9, bytes_accessed=10**7, transcendentals=10**6),
+    )(feats, cotangent, small, packed, mlp_in_w, mlp_out_w, *[jnp.asarray(t) for t in rotary_lanes()])
+
+    chip = lax.div(f, 2)
+    points_grad = (pts[:, :PL] * (1 - missing).astype(f32).reshape(rows, PL)).reshape(contexts, CTXLEN * PL)
+    small_own = lax.dynamic_index_in_dim(gsp, core, 0, keepdims=False)
+    small_bias = lax.dynamic_index_in_dim(gsp, lax.div(chip, 4), 0, keepdims=False)
+    bias_col = jnp.where(core == 0, small_bias[:, 65], small_bias[:, 66])
+    grad_tok_out = go[:, :, 0:320].reshape(2, HALF, 8, 40).transpose(1, 2, 0, 3).reshape(HALF, 640)
+    grad_qkv = go[:, :, 384:1344].reshape(2, HALF, 3, 320).transpose(1, 2, 0, 3).reshape(HALF, 3, 640)
+    grad_attn = jnp.concatenate([go[0, :, 1408:1728], go[1, :, 1408:1728]], axis=1)
+    both = go[0, :, 352:356] + go[1, :, 352:356]
+    return (
+        out,
+        points_grad,
+        small_own[None, 0:40, 0:64],
+        small_own[None, 0:40, 64],
+        grad_tok_out,
+        go[0, :, 320:352],
+        go[0, :, 352],
+        both[:, 1],
+        grad_qkv,
+        grad_attn,
+        both[:, 2],
+        gin,
+        bias_col[None, :],
+        gout,
+        both[:, 3],
+    )
+
+
 def solution(mesh):
     placed = (
         P("fsdp", None),
@@ -311,8 +1060,9 @@
         P("fsdp"),
         P("fsdp", None),
     )
+    small_slice = mesh.shape["fsdp"] == 2 * RING and mesh.shape["tp"] == 2
     return jax.shard_map(
-        body,
+        fast_body if small_slice else body,
         mesh=mesh,
         in_specs=placed,
         out_specs=(

time: 1230 us -> 274 us (0.22)
  waiting for transfers between devices: 906 us -> 0 us
  Pallas kernels: 0 us -> 242 us
  blocking collectives: 167 us -> 0 us
  matrix products: 75.1 us -> 0 us
  local copies, waits for them, and re-layouts: 45.8 us -> 21.2 us
  between operations: 18 us -> 0.93 us
    reduce_scatter x4 -> x0, waiting for transfers between devices: 402 us -> none  [the longest x1 143 us: body(): lax.psum_scatter(grad_inner, 'fsdp', scatter_dimension=0, tiled=True)]
    pallas_call x0 -> x1, Pallas kernels: none -> 242 us  [fast_body(): pl.pallas_call(layer_kernel, out_shape=(jax.ShapeDtypeStruct((OWN, D), bf...]
    all_gather x5 -> x0, waiting for transfers between devices: 203 us -> none  [the longest x1 64.2 us: body(): lax.all_gather(mlp_in_w, 'fsdp', axis=0, tiled=True)]
    unnamed x21 -> x0, waiting for transfers between devices: 194 us -> none
    unnamed x2 -> x0, blocking collectives: 121 us -> none
    psum x4 -> x0, waiting for transfers between devices: 106 us -> none  [the longest x1 37.3 us: body(): lax.psum(dot_last(activation, outer_full).astype(jnp.bfloat16), 'tp')]
    dot_general x26 -> x0, matrix products: 73.9 us -> none  [the longest x6 28.8 us: dot_rows(): lax.dot_general(left, right, (((0,), (0,)), ((), ())), preferred_element_...]
    all_gather x2 -> x0, blocking collectives: 37.5 us -> none  [the longest x1 19.7 us: body(): lax.all_gather(tok_hidden_w, 'fsdp', axis=1, tiled=True)]
  transfers between devices with their start and end apart: 17 -> 0, of which waited for: 15 -> 0; matrix products, arithmetic and copies ran while one was open for 8% -> 0% of each run, Pallas kernels for 0% -> 0%
where the time goes in v1:
time: 274 us; the launch traced here: 273 us
  Pallas kernels  242 us (88%)
  local copies, waits for them, and re-layouts  21.2 us (8%)
  other arithmetic  8.8 us (3%)
    pallas_call x1, Pallas kernels, fast_body(): pl.pallas_call(layer_kernel, out_shape=(jax.ShapeDtypeStruct((OWN, D), bf...  242 us

profile of v1, /device:TPU:0, one launch (start us, length us, event | category | flops | bytes accessed | tf_op | source)
XLA Modules:
  0.0 273.0 jit_solution(2790171011351894779)
XLA Ops:
  0.6 0.0 copy-start.4
  0.7 0.0 copy-start.5
  0.7 0.7 reduce
  1.4 0.1 pad.13.clone
  1.5 0.1 pad.14.clone
  1.6 0.7 fusion.12
  2.3 0.8 copy.72
  3.1 0.1 copy.93
  3.2 0.8 fusion.8
  4.0 0.8 copy.80
  4.7 0.8 copy.77
  5.5 0.8 copy.78
  6.3 0.8 copy.79
  7.0 0.1 copy.95
  7.1 1.4 fusion.7.sp_in
  8.6 0.1 reshape.81
  8.7 0.8 subtract_convert_fusion
  9.5 0.1 reshape.82
  9.6 0.7 maximum_maximum_fusion.fe_in
  10.3 0.1 reshape.85
  10.4 1.0 fusion.11
  11.4 0.0 copy-done.5
  11.4 0.2 copy.73
  11.6 0.1 copy.76
  11.7 0.1 copy.83
  11.8 0.0 copy-done.4
  11.8 0.3 reshape.84
  12.2 0.5 fusion.9
  12.7 0.2 copy.94
  12.9 0.2 reshape_squeeze.13
  13.1 0.2 concatenate.19
  13.3 0.2 copy.96
  13.5 0.2 reshape_squeeze.15
  13.7 0.2 concatenate.20
  13.8 0.9 pad_maximum_fusion.pt_in
  14.7 242.1 %shard_map.298 = (bf16[192,1280]{1,0:T(8,128)(2,1)}, f32[192,128]{1,0:T(8,128)}, f32[2,80,1792]{2,1,0:T(8,128)}, f32[80,2560]{1,0:T(8,128)}, f32[80,2560]{1,0:T(8,128)}, /*index=5*/f32[2,160,128]{2,1,0:T(8,128)}) custom-call(bf16[192,128]{1,0:T(8,128)(2,1)} %maximum_maximum_fusion.fe_in, bf16[192,1280]{1,0:T(8,128)(2,1)} %cot_in.1, ...), custom_call_target="tpu_custom_call" | custom-call | flops 12999999488 | bytes 10000000 | tf_op jit(solution)/shard_map/pallas_call | solution.py:953
  256.8 0.0 copy-start
  256.8 1.0 slice_multiply_fusion
  257.8 0.7 reshape.86
  258.5 1.5 slice_reduce_fusion.3
  260.0 0.9 add_bitcast_fusion
  260.9 0.7 slice_reduce_fusion
  261.6 0.9 slice_bitcast_fusion.2
  262.5 0.7 copy.92
  263.2 1.0 dynamic-slice_bitcast_fusion
  264.2 0.8 fusion
  264.9 0.7 slice_reduce_fusion.4
  265.6 0.6 slice_bitcast_fusion.3
  266.2 0.0 copy-done
  266.2 0.2 copy.88
  266.4 0.8 copy.91
  267.3 0.1 slice.89
  267.4 0.8 pad_maximum_fusion.1
  268.1 0.4 reshape.89
  268.5 0.0 copy-start.3
  268.5 0.6 copy.90
  269.1 0.0 copy-start.2
  269.1 1.3 reshape.90
  270.5 0.0 copy-done.3
  270.5 0.8 copy.100
  271.2 0.0 copy-done.2
  271.2 0.9 copy.101
  272.1 0.0 copy-done.1
  272.1 0.9 copy.102
  (12 shorter events, 0.1 us)
Async XLA Ops:
  0.6 11.2 %copy-start.4 = (bf16[80,3,640]{2,0,1:T(8,128)(2,1)S(1)}, bf16[80,3,640]{2,0,1:T(8,128)(2,1)}, u32[]{:S(2)}) copy-start(bf16[80,3,640]{2,0,1:T(8,128)(2,1)} %param.27) | copy-start | bytes 921604
  0.7 10.7 %copy-start.5 = (bf16[80,640]{1,0:T(8,128)(2,1)S(1)}, bf16[80,640]{1,0:T(8,128)(2,1)}, u32[]{:S(2)}) copy-start(bf16[80,640]{1,0:T(8,128)(2,1)} %param.23) | copy-start | bytes 307204
  256.8 9.4 %copy-start = (f32[2,80,1792]{2,1,0:T(8,128)S(1)}, f32[2,80,1792]{2,1,0:T(8,128)}, u32[]{:S(2)}) copy-start(f32[2,80,1792]{2,1,0:T(8,128)} %get-tuple-element.24) | copy-start | bytes 3440644
  268.5 1.9 copy-start.3
  269.1 2.1 copy-start.2
  270.5 1.7 copy-start.1

commit v2 on v0

--- a/solution.py
+++ b/solution.py
@@ -2,7 +2,10 @@
 
 import jax
 import jax.numpy as jnp
+import numpy as np
 from jax import lax
+from jax.experimental import pallas as pl
+from jax.experimental.pallas import tpu as pltpu
 from jax.sharding import PartitionSpec as P
 
 D = 1280
@@ -292,6 +295,860 @@
     )
 
 
+MESH = pl.DeviceIdType.MESH
+TOK = 384
+OWN = 192
+PART = 96
+HALF = 80
+C_SL, C_QKV, C_IN, C_OUT, C_ALL, C_ONE = 0, 768, 1792, 3072, 4352, 2176
+CHUNKS = (
+    (0, 384, 128, 0),
+    (128, 384, 128, 128),
+    (256, 384, 128, 256),
+    (768, 512, 256, 384),
+    (1024, 512, 256, 640),
+    (1792, 640, 256, 896),
+    (2048, 640, 384, 1152),
+    (3072, 640, 256, 1536),
+    (3328, 640, 256, 1792),
+    (3584, 640, 128, 2048),
+)
+GATHER_ORDER = ("zxy", "zyx", "zxy", "zyx", "zxy", "zyx", "zxy", "zyx", "zxy", "zyx")
+SUM_ORDER = ("yxz", "xyz", "yxz", "xyz", "yxz", "xyz", "yxz", "xyz", "yxz", "xyz")
+(
+    FIRST, OWNED, SECOND, THIRD, HERE, SUM, FEATS, COT, COT_HERE, TOKENS, VECTORS, NORM_1, PROJECT, TURN, ATTEND,
+    NORM_2, INNER, GRAD_OUT, OUTER, GRAD_IN, BACK_2, D_ATT, ATTEND_B, TURN_B, FINISH, GRAD_QKV, GRAD_ATT,
+    GRAD_BIAS, BACK_1, D_HID, GRAD_TOK, GRAD_HID, POINTS, SEND, PASS,
+) = range(35)
+PLAN = (
+    (FIRST, 2), (FIRST, 5), (FIRST, 1), (OWNED, 2), (FIRST, 0), (OWNED, 5), (OWNED, 1), (FIRST, 3), (OWNED, 0),
+    (FIRST, 4), (OWNED, 3), (FIRST, 6), (OWNED, 4), (SECOND, 2), (SECOND, 1), (FIRST, 8), (THIRD, 2), (SECOND, 0),
+    (THIRD, 1), (FIRST, 7), (THIRD, 0), (OWNED, 6), (FEATS,), (HERE, 0), (HERE, 2), (SECOND, 5), (HERE, 1), (TOKENS,),
+    (FIRST, 9), (SECOND, 3), (SEND, 0), (PASS, 0), (SECOND, 4), (OWNED, 7), (THIRD, 3), (OWNED, 8), (THIRD, 4),
+    (VECTORS,), (SECOND, 6), (COT,), (NORM_1,), (HERE, 4), (OWNED, 9), (THIRD, 5), (HERE, 3), (PROJECT,), (SECOND, 7),
+    (TURN,), (THIRD, 6), (SECOND, 8), (ATTEND, 0), (ATTEND, 1), (ATTEND, 2), (SEND, 1), (PASS, 1), (THIRD, 7),
+    (HERE, 5), (SECOND, 9), (NORM_2,), (THIRD, 8), (THIRD, 9), (HERE, 6), (INNER,), (COT_HERE,), (GRAD_OUT, 9),
+    (GRAD_OUT, 8), (HERE, 9), (GRAD_OUT, 7), (HERE, 7), (HERE, 8), (OUTER,), (SEND, 2), (PASS, 2), (SUM, 9),
+    (SEND, 3), (GRAD_IN, 6), (SUM, 8), (SUM, 9), (PASS, 3), (BACK_2,), (GRAD_IN, 5), (D_ATT,), (ATTEND_B, 1),
+    (ATTEND_B, 2), (ATTEND_B, 0), (SUM, 8), (SUM, 9), (TURN_B,), (SEND, 4), (SUM, 7), (PASS, 4), (SUM, 6),
+    (GRAD_BIAS,), (GRAD_ATT,), (SUM, 5), (SUM, 7), (SUM, 8), (GRAD_QKV, 3), (GRAD_QKV, 4), (BACK_1,), (SUM, 7),
+    (SUM, 9), (SUM, 6), (SUM, 8), (SUM, 3), (SUM, 4), (SUM, 5), (D_HID,), (SUM, 5), (SUM, 7), (GRAD_TOK,),
+    (POINTS, 0), (SUM, 4), (SUM, 6), (SUM, 3), (SUM, 4), (POINTS, 1), (SUM, 3), (GRAD_HID,), (SUM, 0), (SUM, 5),
+    (SUM, 0), (SUM, 6), (SUM, 1), (SUM, 2), (SUM, 2), (SUM, 3), (POINTS, 2), (SUM, 1), (SUM, 0), (FINISH,), (SUM, 0),
+    (SUM, 2), (SUM, 2), (SUM, 4), (SUM, 1), (SUM, 1), (POINTS, 3),
+)
+L_RES, L_ONE, L_VEC, L_BIN, L_HID = 64, 72, 73, 77, 79
+TILE = 256
+TILES = D // TILE
+SCALE = 1.0 / math.sqrt(HEAD_DIM)
+
+
+def iota(shape, dim):
+    return lax.broadcasted_iota(jnp.int32, shape, dim)
+
+
+def one_hot(cond):
+    return jnp.where(cond, 1.0, 0.0).astype(jnp.bfloat16)
+
+
+def layer_kernel(
+    points, missing, hid_w, hid_b, tok_in, res_t, tok_b, gain1, qkv_in, att_in, gain2, win_in, b_in, wout_in,
+    out_b, cot_in, rot_c, rot_a, rot_b,
+    out_o, pts_o, fb,
+    w, g, rb, fe, cot, part, pre, act, dpre, n1, n2, db, x0, x1,
+    hc, dpe, pret, q_s, kv_s, att, datt, dpj, ps, gbs, ghs, hidf, hid, vec, bin_s, sums, ptx, ptr,
+    pk, pkf, srcf, tmp,
+    cs, cr, xs, xr,
+    ag_s, ag_r, rs_s, rs_r, ar_s, ar_r, nx_s, nx_r, in_s, in_r, lo_s, tk_s, tk_r, fin_s, fin_r, pt_s, pt_r,
+):
+    f32, bf16 = jnp.float32, jnp.bfloat16
+    f = lax.axis_index("fsdp")
+    x = lax.axis_index("tp")
+    z = lax.div(f, 4)
+    zh = lax.div(z, 2)
+    l = z - 2 * zh
+    y = lax.div(f, 2) - 2 * z
+    c = f - 4 * z - 2 * y
+    m = 2 * l + c
+    mate = {"fsdp": f + 1 - 2 * c}
+    beside = {"fsdp": f + 4 - 8 * l}
+    corner = {"fsdp": f + 4 - 8 * l + 1 - 2 * c}
+    along = {"z": {"fsdp": f + 8 - 16 * zh}, "y": {"fsdp": f + 2 - 4 * y}, "x": {"tp": 1 - x}}
+    own0 = pl.multiple_of(OWN * c, OWN)
+    oth0 = pl.multiple_of(OWN * (1 - c), OWN)
+
+    def m16(v):
+        return pl.multiple_of(v, 16)
+
+    def remote(src, dst, s_sem, r_sem, to):
+        return pltpu.make_async_remote_copy(
+            src_ref=src, dst_ref=dst, send_sem=s_sem, recv_sem=r_sem, device_id=to, device_id_type=MESH
+        )
+
+    sent = []
+
+    def go(copy):
+        copy.start()
+        sent.append(copy)
+
+    barrier = pltpu.get_barrier_semaphore()
+    peers = (mate, beside, corner, along["z"], along["y"], along["x"])
+    for to in peers:
+        pl.semaphore_signal(barrier, inc=1, device_id=to, device_id_type=MESH)
+
+    part[0:80, 0:640] = tok_in[...].astype(f32)
+    part[80:160, 0:640] = att_in[...].astype(f32)
+    part[160:240, 0:640] = qkv_in[0].astype(f32)
+    part[240:320, 0:640] = qkv_in[1].astype(f32)
+    part[0:80, 640:1280] = qkv_in[2].astype(f32)
+    srcf[...] = jnp.zeros(srcf.shape, f32)
+    srcf[0:32, 0:80] = res_t[...].astype(f32)
+    for i, v in enumerate((gain1, gain2, out_b, tok_b)):
+        srcf[32 + i : 33 + i, 0:80] = v[...].astype(f32)
+    tmp[0:1, 0:160] = b_in[...].astype(f32)
+    srcf[36:37, 0:80] = tmp[0:1, 0:80]
+    srcf[37:38, 0:80] = tmp[0:1, 80:160]
+    srcf[40:80, 0:64] = hid_w[...].astype(f32)
+    src = srcf[...].astype(bf16)
+    row = iota((80, 128), 0)
+    lane = iota((80, 128), 1)
+    for q in range(4):
+        col = 160 * q
+        pkf[:, 0:160] = part[0:80, col : col + 160]
+        pkf[:, 160:320] = part[80:160, col : col + 160]
+        pkf[:, 320:384] = jnp.zeros((80, 64), f32)
+        place = (row < 32) & (row >= 8 * q) & (row < 8 * q + 8) & (lane == L_RES + row - 8 * q)
+        place = place | ((row >= 32) & (row < 38) & (lane == L_VEC + row - 32))
+        place = place | ((row >= 40) & (lane == L_HID + row - 40))
+        pkf[:, 256:384] = pkf[:, 256:384] + dot_rows(src, one_hot(place))[0:80]
+        pkf[64:65, 256 + L_HID : 256 + L_HID + 40] = hid_b[...].astype(f32)
+        pkf[:, 384:544] = part[160:240, col : col + 160]
+        pkf[:, 544:704] = part[240:320, col : col + 160]
+        pkf[:, 704:864] = part[0:80, 640 + col : 800 + col]
+        pkf[:, 864:896] = jnp.zeros((80, 32), f32)
+        pk[q] = pkf[...].astype(bf16)
+
+    pl.semaphore_wait(barrier, len(peers))
+
+    def cols(k, h):
+        first, apart, width, _ = CHUNKS[k]
+        return pl.ds(pl.multiple_of(first + apart * h, 128), width)
+
+    def piece(k, member):
+        first, _, width, at = CHUNKS[k]
+        if at < 896:
+            return pk.at[member, :, at : at + width]
+        src, base = (win_in, 896) if at < 1536 else (wout_in, 1536)
+        return src.at[:, pl.ds(pl.multiple_of(640 * member + at - base, 128), width)]
+
+    group = ((mate, 2 * l + 1 - c), (beside, 2 - 2 * l + c), (corner, 3 - 2 * l - c))
+    home = w.at[pl.ds(m16(HALF * f), HALF)]
+    locals_in = {}
+
+    def rows_of(to):
+        return pl.ds(m16(HALF * to["fsdp"]), HALF)
+
+    def g_first(k):
+        dst = w.at[pl.ds(m16(HALF * f), HALF), cols(k, x)]
+        for i, (to, member) in enumerate(group):
+            go(remote(piece(k, member), dst, in_s.at[k, i], in_r.at[k, i], to))
+        locals_in[k] = pltpu.make_async_copy(piece(k, m), dst, lo_s.at[k])
+        locals_in[k].start()
+
+    w4 = w.reshape(4, 2, 160, C_ALL)
+    g4 = g.reshape(4, 2, 160, C_ALL)
+
+    def block(ref, k, flips):
+        zz = 1 - zh if "z" in flips else zh
+        yy = 1 - y if "y" in flips else y
+        h = 1 - x if "x" in flips else x
+        return ref.at[pl.ds(2 * zz, 2), yy, :, cols(k, h)]
+
+    def g_send(k, i, flips, axis):
+        ref = block(w4, k, flips)
+        go(remote(ref, ref, ag_s.at[k, i], ag_r.at[k, i], along[axis]))
+
+    def g_recv(k, i, flips):
+        ref = block(w4, k, flips)
+        remote(ref, ref, ag_s.at[k, i], ag_r.at[k, i], along[flips[-1]]).wait_recv()
+
+    def g_own(k):
+        a, b, d = GATHER_ORDER[k]
+        locals_in[k].wait()
+        for i, (to, member) in enumerate(group):
+            ref = w.at[rows_of(to), cols(k, x)]
+            remote(ref, ref, in_s.at[k, i], in_r.at[k, i], to).wait_recv()
+        g_send(k, 0, "", a)
+        g_send(k, 1, "", b)
+        g_send(k, 3, "", d)
+
+    def g_second(k):
+        a, b, d = GATHER_ORDER[k]
+        g_recv(k, 0, a)
+        g_send(k, 2, a, b)
+        g_send(k, 4, a, d)
+
+    def g_third(k):
+        a, b, d = GATHER_ORDER[k]
+        g_recv(k, 1, b)
+        g_send(k, 5, b, d)
+        g_recv(k, 2, a + b)
+        g_send(k, 6, a + b, d)
+
+    def g_done(k):
+        a, b, d = GATHER_ORDER[k]
+        g_recv(k, 3, d)
+        g_recv(k, 4, a + d)
+        g_recv(k, 5, b + d)
+        g_recv(k, 6, a + b + d)
+
+    def s_buf(k, i):
+        _, _, width, at = CHUNKS[k]
+        return rb.at[i, :, :, at : at + width]
+
+    def s_send(k, i, flips, axis):
+        go(remote(block(g4, k, flips), s_buf(k, i), rs_s.at[k, i], rs_r.at[k, i], along[axis]))
+
+    def s_add(k, i, flips, axis):
+        ref = s_buf(k, i)
+        remote(ref, ref, rs_s.at[k, i], rs_r.at[k, i], along[axis]).wait_recv()
+        _, _, width, at = CHUNKS[k]
+        zz = 1 - zh if "z" in flips else zh
+        yy = 1 - y if "y" in flips else y
+        there = cols(k, 1 - x if "x" in flips else x)
+
+        def step(j, carry):
+            half = lax.div(j, 2)
+            inside = 80 * (j - 2 * half)
+            here = pl.ds(m16(640 * zz + 320 * half + 160 * yy + inside), 80)
+            g[here, there] = g[here, there] + rb[i, half, pl.ds(m16(inside), 80), at : at + width]
+            return carry
+
+        lax.fori_loop(0, 4, step, 0)
+
+    def s_start(k):
+        a, b, d = SUM_ORDER[k]
+        s_send(k, 0, a + b + d, a)
+        s_send(k, 1, a + b, a)
+        s_send(k, 2, a + d, a)
+        s_send(k, 3, a, a)
+        s_at[k] = 0
+
+    def s_step(k):
+        a, b, d = SUM_ORDER[k]
+        stage = s_at[k]
+        if stage == 0:
+            s_add(k, 0, b + d, a)
+            s_send(k, 4, b + d, b)
+            s_add(k, 1, b, a)
+            s_send(k, 5, b, b)
+        elif stage == 1:
+            s_add(k, 2, d, a)
+            s_add(k, 4, d, b)
+            s_send(k, 6, d, d)
+        elif stage == 2:
+            s_add(k, 3, "", a)
+            s_add(k, 5, "", b)
+        else:
+            s_add(k, 6, "", d)
+            _, _, width, at = CHUNKS[k]
+            for i, (to, member) in enumerate(group):
+                src = g.at[rows_of(to), cols(k, x)]
+                go(remote(src, fb.at[m, :, at : at + width], fin_s.at[k, i], fin_r.at[k, i], to))
+            fb[m, :, at : at + width] = g[pl.ds(m16(HALF * f), HALF), cols(k, x)]
+            del s_at[k]
+            return
+        s_at[k] = stage + 1
+
+    s_at = {}
+
+    def ar_tile(i):
+        return slice(TILE * i, TILE * i + TILE)
+
+    def ar_begin(a):
+        left, lo, width = operands[a]
+        b = a % 2
+        if a >= 2:
+            for i in range(TILES):
+                done = cs.at[b, :, ar_tile(i)]
+                remote(done, done, ar_s.at[a - 2, 0, i], ar_r.at[a - 2, 0, i], mate).wait_send()
+        for i in range(TILES):
+            part[:, ar_tile(i)] = dot_last(left[...], w[ar_tile(i), lo : lo + width])
+            cs[b, :, ar_tile(i)] = part[pl.ds(oth0, OWN), ar_tile(i)].astype(bf16)
+            copy = remote(cs.at[b, :, ar_tile(i)], cr.at[b, :, ar_tile(i)], ar_s.at[a, 0, i], ar_r.at[a, 0, i], mate)
+            copy.start()
+            if a >= 3:
+                sent.append(copy)
+
+    def ar_mid(a):
+        b = a % 2
+        if a >= 2:
+            for i in range(TILES):
+                done = xs.at[b, :, ar_tile(i)]
+                remote(done, done, ar_s.at[a - 2, 1, i], ar_r.at[a - 2, 1, i], beside).wait_send()
+        for i in range(TILES):
+            here = cr.at[b, :, ar_tile(i)]
+            remote(here, here, ar_s.at[a, 0, i], ar_r.at[a, 0, i], mate).wait_recv()
+            xs[b, :, ar_tile(i)] = (
+                part[pl.ds(own0, OWN), ar_tile(i)] + cr[b, :, ar_tile(i)].astype(f32)
+            ).astype(bf16)
+            copy = remote(
+                xs.at[b, :, ar_tile(i)], xr.at[a % 3, :, ar_tile(i)], ar_s.at[a, 1, i], ar_r.at[a, 1, i], beside
+            )
+            copy.start()
+            if a >= 3:
+                sent.append(copy)
+
+    def ar_end(a):
+        for i in range(TILES):
+            here = xr.at[a % 3, :, ar_tile(i)]
+            remote(here, here, ar_s.at[a, 1, i], ar_r.at[a, 1, i], beside).wait_recv()
+
+    def summed(a, rows):
+        return xs[a % 2, rows, :].astype(f32) + xr[a % 3, rows, :].astype(f32)
+
+    def own_rows(body, first=0, count=OWN, size=32):
+        def step(j, carry):
+            start = m16(first + size * j)
+            body(pl.ds(start, size), pl.ds(m16(own0 + start), size))
+            return carry
+
+        lax.fori_loop(0, count // size, step, 0)
+
+    def share(j, ref):
+        rows = ref.at[pl.ds(own0, OWN)]
+        go(remote(rows, rows, nx_s.at[j], nx_r.at[j], mate))
+
+    def shared(j, ref):
+        rows = ref.at[pl.ds(oth0, OWN)]
+        remote(rows, rows, nx_s.at[j], nx_r.at[j], mate).wait_recv()
+
+    def rms(v):
+        return lax.rsqrt(jnp.mean(v * v, axis=-1, keepdims=True) + 1e-06)
+
+    def fold(v):
+        return jnp.sum(v.reshape(v.shape[0] // 8, 8, v.shape[1]), axis=0)
+
+    def tiles_loop(count, body):
+        def step(i, carry):
+            body(pl.ds(pl.multiple_of(TILE * i, TILE), TILE), i)
+            return carry
+
+        lax.fori_loop(0, count, step, 0)
+
+    def grad_block(k, left, right, base):
+        first, apart, width, _ = CHUNKS[k]
+
+        def body(rows, i):
+            for h in (0, 1):
+                lo = first - base + apart * h
+                g[rows, first + apart * h : first + apart * h + width] = dot_rows(
+                    left[:, rows], right[:, lo : lo + width]
+                ).astype(bf16)
+
+        tiles_loop(TILES, body)
+
+    def slab(h):
+        return slice(256 + 384 * h, 384 + 384 * h)
+
+    spread = one_hot(lax.div(iota((OWN, 12), 0), CTXLEN) == iota((OWN, 12), 1))
+    right_patch = lax.div(iota((OWN, 512), 1), PL) == (iota((OWN, 512), 0) & (CTXLEN - 1))
+    lane_of = iota((512, 128), 1)
+    place_of = iota((512, 128), 0) & (PL - 1)
+    mine0 = m16(own0 + PART * l)
+    cot_part = cot_in.at[pl.ds(m16(PART * x), PART)]
+    cot_copy = pltpu.make_async_copy(cot_part, cot.at[pl.ds(mine0, PART)], lo_s.at[len(CHUNKS)])
+    lane768 = iota((TOK, 768), 1)
+    lane384 = jnp.where(lane768 >= 384, lane768 - 384, lane768)
+    units = lane384 < 160
+    resids = (lane384 >= 256 + L_RES) & (lane384 < 256 + L_RES + 8)
+    de = act
+
+    def tokens_here(j, ref):
+        for i, (to, member) in enumerate(group):
+            cc = 1 - c if i != 1 else c
+            ll = l if i == 0 else 1 - l
+            rows = ref.at[pl.ds(m16(OWN * cc + PART * ll), PART)]
+            remote(rows, rows, tk_s.at[j, i], tk_r.at[j, i], to).wait_recv()
+
+    def features():
+        keep = 1.0 - missing[...].astype(f32)
+        seen = dot_plain(spread, (points[...].astype(f32) * keep).astype(bf16))
+        gone = dot_plain(spread, missing[...].astype(f32).astype(bf16))
+        feats = dot_plain(jnp.where(right_patch, seen, 0.0).astype(bf16), one_hot(lane_of == place_of))
+        feats = feats + dot_plain(jnp.where(right_patch, gone, 0.0).astype(bf16), one_hot(lane_of == place_of + PL))
+        ptx[0:OWN, :] = jnp.where(iota((OWN, 128), 1) == 2 * PL, 1.0, feats)
+        fe[pl.ds(mine0, PART), :] = ptx[pl.ds(m16(PART * x), PART), :].astype(bf16)
+        for i, (to, member) in enumerate(group):
+            rows = fe.at[pl.ds(mine0, PART)]
+            go(remote(rows, rows, tk_s.at[0, i], tk_r.at[0, i], to))
+        sums[...] = jnp.zeros(sums.shape, f32)
+        hidf[...] = jnp.zeros(hidf.shape, f32)
+
+    def cot_out():
+        cot_copy.start()
+        for i, (to, member) in enumerate(group):
+            go(remote(cot_part, cot.at[pl.ds(mine0, PART)], tk_s.at[1, i], tk_r.at[1, i], to))
+
+    def cot_here():
+        cot_copy.wait()
+        tokens_here(1, cot)
+
+    def tokenize():
+        for h in (0, 1):
+            for j in range(4):
+                rows = pl.ds(m16(320 * m + 80 * j), 80)
+                tmp[:, 0:128] = w[rows, slab(h)].astype(f32)
+                hidf[0:72, 384 * h + 40 * j : 384 * h + 40 * j + 40] = tmp[0:72, L_HID : L_HID + 40]
+            row = iota((128, 128), 0)
+            lane = iota((128, 128), 1)
+            chosen = (lane >= L_RES) & (lane < L_RES + 8) & (row == PL * h + 8 * m + lane - L_RES)
+            hidf[:, slab(h)] = jnp.where(chosen, 1.0, 0.0)
+        hid[...] = hidf[...].astype(bf16)
+        tokens_here(0, fe)
+        pret[...] = dot_plain(fe[...], hid[...])
+        v = pret[...]
+        hc[...] = jnp.where(
+            units, v * jax.nn.sigmoid(v), jnp.where(resids, v, jnp.where(lane384 == 256 + L_ONE, 1.0, 0.0))
+        ).astype(bf16)
+
+    def vectors():
+        row16 = iota((16, 128), 0)
+        lane16 = iota((16, 128), 1)
+        vec[...] = dot_last(one_hot((row16 < 4) & (lane16 == L_VEC + row16)), w[:, slab(0)])
+        for h in (0, 1):
+            pair = dot_last(one_hot((row16 < 2) & (lane16 == L_BIN + row16)), w[pl.ds(m16(320 * m), 320), slab(h)])
+            tmp[0:16, 0:320] = pair
+            for j in range(4):
+                at = 640 * h + 160 * j
+                bin_s[0:1, at : at + 80] = tmp[0:1, 80 * j : 80 * j + 80]
+                bin_s[0:1, at + 80 : at + 160] = tmp[1:2, 80 * j : 80 * j + 80]
+
+    def first_norm():
+        ar_end(0)
+
+        def body(rows, mine):
+            v = summed(0, rows) + vec[3:4, :]
+            x0[rows, :] = v
+            n1[mine, :] = (v * rms(v) * vec[0:1, :]).astype(bf16)
+
+        own_rows(body)
+        share(0, n1)
+
+    def project():
+        shared(0, n1)
+
+        def body(cols, i):
+            part[:, cols] = dot_plain(n1[...], w[:, pl.ds(pl.multiple_of(C_QKV + TILE * i, TILE), TILE)])
+
+        tiles_loop(4, body)
+
+    def turn():
+        def body(j, carry):
+            rows = pl.ds(m16(16 * j), 16)
+            v = part[rows, 0:1024]
+            v = v * rot_c[...] + pltpu.roll(v, 984, 1) * rot_a[...] + pltpu.roll(v, 40, 1) * rot_b[...]
+            for h in (0, 1):
+                one = v[:, 512 * h : 512 * h + 512]
+                q_s[h, rows, :] = one[:, 0:256].astype(bf16)
+                kv_s[h, rows, :] = pltpu.roll(one, 352, 1)[:, 0:384].astype(bf16)
+            return carry
+
+        lax.fori_loop(0, TOK // 16, body, 0)
+
+    def stacked(v, first):
+        head = iota(v.shape, 1)
+        return jnp.concatenate(
+            [
+                jnp.where((head >= first + HEAD_DIM * h) & (head < first + HEAD_DIM * h + HEAD_DIM), v, jnp.zeros_like(v))
+                for h in (0, 1)
+            ],
+            axis=0,
+        )
+
+    def side(v):
+        return jnp.concatenate([v[0:128], v[128:256]], axis=1)
+
+    def attend(b):
+        rows = slice(128 * b, 128 * b + 128)
+        qi = iota((256, 128), 0) & 127
+        kj = iota((256, 128), 1)
+        allowed = ((qi >> 4) == (kj >> 4)) & (kj <= qi)
+        for h in (0, 1):
+            kv = kv_s[h, rows, :]
+            scores = dot_last(stacked(q_s[h, rows, :], 0), kv[:, 0:256]) * SCALE
+            scores = jnp.where(allowed, scores, -1e30)
+            e = jnp.exp(scores - jnp.max(scores, axis=-1, keepdims=True))
+            probs = e * (1.0 / jnp.sum(e, axis=-1, keepdims=True))
+            ps[512 * b + 256 * h : 512 * b + 256 * h + 256, :] = probs
+            att[rows, 384 * h : 384 * h + 384] = dot_plain(side(probs.astype(bf16)), stacked(kv, 160)).astype(bf16)
+
+    def second_norm():
+        ar_end(1)
+
+        def body(rows, mine):
+            v = x0[rows, :] + summed(1, rows)
+            x1[rows, :] = v
+            n2[mine, :] = (v * rms(v) * vec[1:2, :]).astype(bf16)
+
+        own_rows(body)
+        share(1, n2)
+
+    def inner():
+        shared(1, n2)
+
+        def body(cols, i):
+            v = dot_plain(n2[...], w[:, pl.ds(pl.multiple_of(C_IN + TILE * i, 128), TILE)]) + bin_s[0:1, cols]
+            pre[:, cols] = v
+            act[:, cols] = (v * jax.nn.sigmoid(v)).astype(bf16)
+
+        tiles_loop(TILES, body)
+
+    def outer_back():
+        def body(cols, i):
+            v = pre[:, cols]
+            s = jax.nn.sigmoid(v)
+            d = dot_plain(cot[...], w[:, pl.ds(pl.multiple_of(C_OUT + TILE * i, 128), TILE)])
+            dpre[:, cols] = (d * (s * (1.0 + v * (1.0 - s)))).astype(bf16)
+
+        tiles_loop(TILES, body)
+
+    def second_back():
+        ar_end(2)
+
+        def body(rows, mine):
+            dn = summed(2, rows)
+            v = x1[rows, :]
+            r = rms(v)
+            xh = v * r
+            scaled = dn * vec[1:2, :]
+            inside = jnp.mean(scaled * xh, axis=-1, keepdims=True)
+            ct = cot[mine, :].astype(f32)
+            d = ct + r * (scaled - xh * inside)
+            pre[rows, :] = d
+            db[mine, :] = d.astype(bf16)
+            sums[8:16, :] += fold(dn * xh)
+            sums[16:24, :] += fold(ct)
+
+        own_rows(body)
+        share(2, db)
+
+    def attended_back():
+        shared(2, db)
+
+        def body(cols, i):
+            datt[:, cols] = dot_plain(db[...], w[:, cols]).astype(bf16)
+
+        tiles_loop(3, body)
+
+    def attend_back(b):
+        rows = slice(128 * b, 128 * b + 128)
+        for h in (0, 1):
+            probs = ps[512 * b + 256 * h : 512 * b + 256 * h + 256, :]
+            kv = kv_s[h, rows, :]
+            heads_d = stacked(datt[rows, 384 * h : 384 * h + 384], 160)
+            dp = dot_last(heads_d, kv)
+            ds = (probs * (dp - jnp.sum(probs * dp, axis=-1, keepdims=True))).astype(bf16)
+            part[rows, 512 * h : 512 * h + 256] = dot_plain(side(ds), stacked(kv[:, 0:256], 0)) * SCALE
+            dv = dot_rows(probs.astype(bf16), heads_d)
+            dk = dot_rows(ds, stacked(q_s[h, rows, :], 0)) * SCALE
+            dkv = jnp.concatenate([dv[:, 0:256] + dk, dv[:, 256:384]], axis=1)
+            part[rows, 512 * h + 160 : 512 * h + 512] = dkv[:, 0:352]
+
+    def turn_back():
+        def body(j, carry):
+            rows = pl.ds(m16(16 * j), 16)
+            v = part[rows, 0:1024]
+            v = v * rot_c[...] - pltpu.roll(v, 984, 1) * rot_a[...] - pltpu.roll(v, 40, 1) * rot_b[...]
+            dpj[rows, :] = v.astype(bf16)
+            return carry
+
+        lax.fori_loop(0, TOK // 16, body, 0)
+
+    def finish():
+        ar_end(3)
+
+        def body(rows, mine):
+            start = rows.start - PART * l + PART * x
+            out_o[pl.ds(m16(start), 32), :] = (x1[rows, :] + summed(3, rows) + vec[2:3, :]).astype(bf16)
+
+        own_rows(body, PART * l, PART)
+        ref = out_o.at[pl.ds(m16(PART * x), PART)]
+        go(remote(ref, ref, pt_s.at[3], pt_r.at[3], along["x"]))
+
+    def grad_out(k):
+        grad_block(k, cot, act, C_OUT)
+        s_start(k)
+
+    def grad_in(k):
+        grad_block(k, n2, dpre, C_IN)
+        s_start(k)
+
+    def grad_qkv(k):
+        grad_block(k, n1, dpj, C_QKV)
+        s_start(k)
+
+    def grad_att():
+        def body(rows, i):
+            g[rows, 0:768] = dot_rows(db[:, rows], att[...]).astype(bf16)
+
+        tiles_loop(TILES, body)
+
+    def grad_bias():
+        ones = one_hot((iota((TOK, 128), 1) >= L_BIN) & (iota((TOK, 128), 1) < L_BIN + 2))
+
+        def body(rows, i):
+            gbs[rows, :] = dot_rows(dpre[:, rows], ones)
+
+        tiles_loop(TILES, body)
+
+    def first_back():
+        ar_end(4)
+
+        def body(rows, mine):
+            dn = summed(4, rows)
+            v = x0[rows, :]
+            r = rms(v)
+            xh = v * r
+            scaled = dn * vec[0:1, :]
+            inside = jnp.mean(scaled * xh, axis=-1, keepdims=True)
+            d = pre[rows, :] + r * (scaled - xh * inside)
+            de[mine, :] = d.astype(bf16)
+            sums[0:8, :] += fold(dn * xh)
+
+        own_rows(body)
+        share(3, de)
+
+    def hidden_back():
+        shared(3, de)
+        v = pret[...]
+        s = jax.nn.sigmoid(v)
+        d = dot_plain(de[...], w[:, 0:768])
+        dpe[...] = jnp.where(units, d * (s * (1.0 + v * (1.0 - s))), jnp.where(resids, d, 0.0)).astype(bf16)
+
+    def grad_tok():
+        row32 = iota((32, 128), 0)
+        pick = one_hot((row32 < 24) & (iota((32, 128), 1) == L_VEC + (row32 >> 3)))
+
+        def body(rows, i):
+            both = g[rows, 0:768].astype(f32) + dot_rows(de[:, rows], hc[...])
+            columns = dot_rows(sums[:, rows].astype(bf16), pick)
+            for h in (0, 1):
+                g[rows, 384 * h : 384 * h + 256] = both[:, 384 * h : 384 * h + 256].astype(bf16)
+                g[rows, slab(h)] = (both[:, slab(h)] + columns).astype(bf16)
+
+        tiles_loop(TILES, body)
+        s_start(0)
+        s_start(1)
+
+    def grad_hidden():
+        ghs[...] = dot_rows(fe[...], dpe[...])
+        lane = iota((80, 128), 1)
+        for h in (0, 1):
+            for j in range(4):
+                at = 640 * h + 160 * j
+                tmp[:, 0:128] = jnp.where(lane == L_BIN, gbs[at : at + 80, :], 0.0) + jnp.where(
+                    lane == L_BIN + 1, gbs[at + 80 : at + 160, :], 0.0
+                )
+                tmp[:, L_HID : L_HID + 40] = ghs[0:80, 384 * h + 40 * j : 384 * h + 40 * j + 40]
+                rows = pl.ds(m16(320 * m + 80 * j), 80)
+                g[rows, slab(h)] = (g[rows, slab(h)].astype(f32) + tmp[:, 0:128]).astype(bf16)
+        s_start(2)
+
+    def points_back(stage):
+        theirs = m16(PART * (1 - l))
+        mine = m16(PART * l)
+        half = pl.ds(m16(PART * x), PART)
+        if stage == 0:
+            ptx[...] = dot_last(dpe[...], hid[...])
+            go(remote(ptx.at[pl.ds(oth0, OWN)], ptr.at[0], pt_s.at[0], pt_r.at[0], mate))
+        elif stage == 1:
+            remote(ptr.at[0], ptr.at[0], pt_s.at[0], pt_r.at[0], mate).wait_recv()
+            ptr[1] = ptx[pl.ds(own0, OWN), :] + ptr[0]
+            go(remote(ptr.at[1, pl.ds(theirs, PART)], ptr.at[2, pl.ds(theirs, PART)], pt_s.at[1], pt_r.at[1], beside))
+        elif stage == 2:
+            there = ptr.at[2, pl.ds(mine, PART)]
+            remote(there, there, pt_s.at[1], pt_r.at[1], beside).wait_recv()
+            ptr[3, half, :] = ptr[1, pl.ds(mine, PART), :] + ptr[2, pl.ds(mine, PART), :]
+            go(remote(ptr.at[3, half], ptr.at[3, half], pt_s.at[2], pt_r.at[2], along["x"]))
+        else:
+            there = ptr.at[3, pl.ds(m16(PART * (1 - x)), PART)]
+            remote(there, there, pt_s.at[2], pt_r.at[2], along["x"]).wait_recv()
+            wide = dot_last(ptr[3].astype(bf16), one_hot(lane_of == place_of))
+            wide = jnp.where(right_patch, wide, 0.0).astype(bf16)
+            pts_o[...] = dot_rows(spread, wide) * (1.0 - missing[...].astype(f32))
+
+    operands = ((hc, 0, 768), (att, 0, 768), (dpre, C_IN, 1280), (act, C_OUT, 1280), (dpj, C_QKV, 1024))
+    steps = (
+        g_first, g_own, g_second, g_third, g_done, s_step, features, cot_out, cot_here, tokenize, vectors,
+        first_norm, project, turn, attend, second_norm, inner, grad_out, outer_back, grad_in, second_back,
+        attended_back, attend_back, turn_back, finish, grad_qkv, grad_att, grad_bias, first_back, hidden_back,
+        grad_tok, grad_hidden, points_back, ar_begin, ar_mid,
+    )
+    for name, *which in PLAN:
+        steps[name](*which)
+
+    there = out_o.at[pl.ds(m16(PART * (1 - x)), PART)]
+    remote(there, there, pt_s.at[3], pt_r.at[3], along["x"]).wait_recv()
+    for k, (_, _, width, at) in enumerate(CHUNKS):
+        for i, (to, member) in enumerate(group):
+            there = fb.at[member, :, at : at + width]
+            remote(there, there, fin_s.at[k, i], fin_r.at[k, i], to).wait_recv()
+    for copy in sent:
+        copy.wait_send()
+
+
+def unpack_kernel(
+    out_i, pts_i, fb,
+    out_o, pts_o, hw_o, hb_o, tok_o, res_o, tokb_o, gain1_o, qkv_o, att_o, gain2_o, in_o, inb_o, outw_o, outb_o,
+):
+    f32 = jnp.float32
+    out_o[...] = out_i[...]
+    pts_o[...] = pts_i[...]
+    turned = []
+    hidden = jnp.zeros((8, 128), f32)
+    for q in range(4):
+        at = slice(160 * q, 160 * q + 160)
+        lead = fb[q, :, 0:384].astype(f32)
+        tok_o[:, at] = lead[:, 0:160]
+        att_o[:, at] = lead[:, 160:320]
+        tile = lead[:, 256:384]
+        hidden = hidden + tile[64:72]
+        t = jnp.transpose(jnp.concatenate([tile, jnp.zeros((48, 128), f32)], axis=0))
+        turned.append(t)
+        res_o[8 * q : 8 * q + 8, :] = t[L_RES : L_RES + 8, 0:80]
+        qkv = fb[q, :, 384:896].astype(f32)
+        for j in range(3):
+            qkv_o[j, :, at] = qkv[:, 160 * j : 160 * j + 160]
+        in_o[:, 640 * q : 640 * q + 640] = fb[q, :, 896:1536].astype(f32)
+        outw_o[:, 640 * q : 640 * q + 640] = fb[q, :, 1536:2176].astype(f32)
+    both = turned[0] + turned[1]
+    every = both + turned[2] + turned[3]
+    tokb_o[...] = turned[0][L_ONE : L_ONE + 1, 0:80]
+    gain1_o[...] = both[L_VEC : L_VEC + 1, 0:80]
+    gain2_o[...] = both[L_VEC + 1 : L_VEC + 2, 0:80]
+    outb_o[...] = both[L_VEC + 2 : L_VEC + 3, 0:80]
+    inb_o[:, 0:80] = every[L_BIN : L_BIN + 1, 0:80]
+    inb_o[:, 80:160] = every[L_BIN + 1 : L_BIN + 2, 0:80]
+    hw_o[...] = every[L_HID : L_HID + 40, 0:64]
+    hb_o[...] = hidden[0:1, L_HID : L_HID + 40]
+
+
+def rotary_lanes():
+    lanes = np.arange(1024) % 512
+    inside = lanes % HEAD_DIM
+    turned = lanes < 320
+    freqs = 10000.0 ** (-2.0 * (inside % 40) / HEAD_DIM)
+    angles = np.arange(CTXLEN)[:, None] * freqs[None, :]
+    cosine = np.where(turned, np.cos(angles), 1.0)
+    sine = np.where(turned, np.sin(angles), 0.0)
+    lower = np.where(inside < 40, -sine, 0.0)
+    upper = np.where(inside >= 40, sine, 0.0)
+    return [np.asarray(t, np.float32) for t in (cosine, lower, upper)]
+
+
+def fast_body(
+    points, missing, tok_hidden_w, tok_hidden_b, tok_out_w, tok_res_w, tok_out_b, attn_gain, qkv_w, attn_out_w,
+    mlp_gain, mlp_in_w, mlp_in_b, mlp_out_w, mlp_out_b, cotangent,
+):
+    f32, bf16 = jnp.float32, jnp.bfloat16
+    any_space = pl.BlockSpec(memory_space=pl.ANY)
+    vmem = pl.BlockSpec(memory_space=pltpu.VMEM)
+
+    def sems(*shape):
+        return pltpu.SemaphoreType.DMA(shape)
+
+    def like(*shape):
+        return jax.ShapeDtypeStruct(shape, f32)
+
+    chunks = len(CHUNKS)
+    specs = [vmem] * 19
+    specs[11] = specs[13] = specs[15] = any_space
+    out, pts, packed = pl.pallas_call(
+        layer_kernel,
+        out_shape=(
+            jax.ShapeDtypeStruct((OWN, D), bf16),
+            like(12, 512),
+            jax.ShapeDtypeStruct((4, HALF, C_ONE), bf16),
+        ),
+        in_specs=specs,
+        out_specs=[vmem] * 3,
+        scratch_shapes=[
+            pltpu.VMEM((D, C_ALL), bf16),
+            pltpu.VMEM((D, C_ALL), bf16),
+            pltpu.VMEM((7, 2, 160, C_ONE), bf16),
+            pltpu.VMEM((TOK, 128), bf16),
+            pltpu.VMEM((TOK, D), bf16),
+            pltpu.VMEM((TOK, D), f32),
+            pltpu.VMEM((TOK, D), f32),
+            pltpu.VMEM((TOK, D), bf16),
+            pltpu.VMEM((TOK, D), bf16),
+            pltpu.VMEM((TOK, D), bf16),
+            pltpu.VMEM((TOK, D), bf16),
+            pltpu.VMEM((TOK, D), bf16),
+            pltpu.VMEM((OWN, D), f32),
+            pltpu.VMEM((OWN, D), f32),
+            pltpu.VMEM((TOK, 768), bf16),
+            pltpu.VMEM((TOK, 768), bf16),
+            pltpu.VMEM((TOK, 768), f32),
+            pltpu.VMEM((2, TOK, 256), bf16),
+            pltpu.VMEM((2, TOK, 384), bf16),
+            pltpu.VMEM((TOK, 768), bf16),
+            pltpu.VMEM((TOK, 768), bf16),
+            pltpu.VMEM((TOK, 1024), bf16),
+            pltpu.VMEM((1536, 128), f32),
+            pltpu.VMEM((D, 128), f32),
+            pltpu.VMEM((128, 768), f32),
+            pltpu.VMEM((128, 768), f32),
+            pltpu.VMEM((128, 768), bf16),
+            pltpu.VMEM((16, D), f32),
+            pltpu.VMEM((8, D), f32),
+            pltpu.VMEM((32, D), f32),
+            pltpu.VMEM((TOK, 128), f32),
+            pltpu.VMEM((4, OWN, 128), f32),
+            pltpu.VMEM((4, HALF, 896), bf16),
+            pltpu.VMEM((HALF, 896), f32),
+            pltpu.VMEM((HALF, 128), f32),
+            pltpu.VMEM((HALF, 384), f32),
+            pltpu.VMEM((2, OWN, D), bf16),
+            pltpu.VMEM((2, OWN, D), bf16),
+            pltpu.VMEM((2, OWN, D), bf16),
+            pltpu.VMEM((3, OWN, D), bf16),
+            sems(chunks, 7), sems(chunks, 7), sems(chunks, 7), sems(chunks, 7),
+            sems(5, 2, TILES), sems(5, 2, TILES),
+            sems(4), sems(4), sems(chunks, 3), sems(chunks, 3), sems(chunks + 1), sems(2, 3), sems(2, 3),
+            sems(chunks, 3), sems(chunks, 3), sems(4), sems(4),
+        ],
+        compiler_params=pltpu.CompilerParams(
+            collective_id=0, has_side_effects=True, vmem_limit_bytes=64 * 1024 * 1024 - 512 * 1024
+        ),
+        cost_estimate=pl.CostEstimate(flops=13 * 10**9, bytes_accessed=10**7, transcendentals=10**6),
+    )(
+        points, missing, tok_hidden_w[0], tok_hidden_b, tok_out_w, tok_res_w.T, tok_out_b[None], attn_gain[None],
+        qkv_w.transpose(1, 0, 2), attn_out_w, mlp_gain[None], mlp_in_w, mlp_in_b, mlp_out_w, mlp_out_b[None],
+        cotangent, *[jnp.asarray(t) for t in rotary_lanes()],
+    )
+    (
+        output, points_grad, hidden_w, hidden_b, tok, res_t, tok_b, gain1, qkv, att, gain2, inner, inner_b, outer,
+        outer_b,
+    ) = pl.pallas_call(
+        unpack_kernel,
+        out_shape=(
+            jax.ShapeDtypeStruct((OWN, D), bf16),
+            like(12, 512), like(40, 64), like(1, 40), like(HALF, 640), like(32, HALF), like(1, HALF), like(1, HALF),
+            like(3, HALF, 640), like(HALF, 640), like(1, HALF), like(HALF, 2560), like(1, 160), like(HALF, 2560),
+            like(1, HALF),
+        ),
+        in_specs=[vmem] * 3,
+        out_specs=[vmem] * 15,
+        compiler_params=pltpu.CompilerParams(vmem_limit_bytes=32 * 1024 * 1024),
+    )(out, pts, packed)
+    return (
+        output, points_grad, hidden_w[None], hidden_b, tok, res_t.T, tok_b[0], gain1[0], qkv.transpose(1, 0, 2), att,
+        gain2[0], inner, inner_b, outer, outer_b[0],
+    )
+
+
 def solution(mesh):
     placed = (
         P("fsdp", None),
@@ -311,8 +1168,9 @@
         P("fsdp"),
         P("fsdp", None),
     )
+    small_slice = mesh.shape["fsdp"] == 16 and mesh.shape["tp"] == 2
     return jax.shard_map(
-        body,
+        fast_body if small_slice else body,
         mesh=mesh,
         in_specs=placed,
         out_specs=(

time: 1230 us -> 220 us (0.18)
  waiting for transfers between devices: 906 us -> 0 us
  Pallas kernels: 0 us -> 216 us
  blocking collectives: 167 us -> 0 us
  matrix products: 75.1 us -> 0 us
  local copies, waits for them, and re-layouts: 45.8 us -> 3.12 us
  between operations: 18 us -> 0.67 us
  other arithmetic: 14.2 us -> 0 us
    reduce_scatter x4 -> x0, waiting for transfers between devices: 402 us -> none  [the longest x1 143 us: body(): lax.psum_scatter(grad_inner, 'fsdp', scatter_dimension=0, tiled=True)]
    pallas_call x0 -> x2, Pallas kernels: none -> 216 us  [the longest x1 214 us: fast_body(): pl.pallas_call(layer_kernel, out_shape=(jax.ShapeDtypeStruct((OWN, D), bf...]
    all_gather x5 -> x0, waiting for transfers between devices: 203 us -> none  [the longest x1 64.2 us: body(): lax.all_gather(mlp_in_w, 'fsdp', axis=0, tiled=True)]
    unnamed x21 -> x0, waiting for transfers between devices: 194 us -> none
    unnamed x2 -> x0, blocking collectives: 121 us -> none
    psum x4 -> x0, waiting for transfers between devices: 106 us -> none  [the longest x1 37.3 us: body(): lax.psum(dot_last(activation, outer_full).astype(jnp.bfloat16), 'tp')]
    dot_general x26 -> x0, matrix products: 73.9 us -> none  [the longest x6 28.8 us: dot_rows(): lax.dot_general(left, right, (((0,), (0,)), ((), ())), preferred_element_...]
    all_gather x2 -> x0, blocking collectives: 37.5 us -> none  [the longest x1 19.7 us: body(): lax.all_gather(tok_hidden_w, 'fsdp', axis=1, tiled=True)]
  transfers between devices with their start and end apart: 17 -> 0, of which waited for: 15 -> 0; matrix products, arithmetic and copies ran while one was open for 8% -> 0% of each run, Pallas kernels for 0% -> 0%
where the time goes in v2:
time: 220 us
  Pallas kernels  216 us (98%)
  local copies, waits for them, and re-layouts  3.12 us (1%)
    pallas_call x1, Pallas kernels, fast_body(): pl.pallas_call(layer_kernel, out_shape=(jax.ShapeDtypeStruct((OWN, D), bf...  214 us

profile of v2, /device:TPU:0, one launch (start us, length us, event | category | flops | bytes accessed | tf_op | source)
XLA Modules:
  0.0 219.6 jit_solution(3063372264133773916)
XLA Ops:
  0.7 213.8 %shard_map.298 = (bf16[192,1280]{1,0:T(8,128)(2,1)}, f32[12,512]{1,0:T(8,128)}, bf16[4,80,2176]{2,1,0:T(8,128)(2,1)}) custom-call(bf16[12,512]{1,0:T(8,128)(2,1)} %points.1, s32[12,512]{1,0:T(8,128)} %missing.1, bf16[40,64]{1,0:T(8,128)(2,1)} %bitcast.18, bf16[1,40]{1,0:T(2,128)(2,1)} %hid_b.1, bf16[80,640]{1,0:T(8,128)(2,1)} %tok_in.1, ...), custom_call_target="tpu_custom_call" | custom-call | flops 12999999488 | bytes 10000000 | tf_op jit(solution)/shard_map/pallas_call | solution.py:1067
  214.5 0.0 copy-start
  214.5 1.3 copy-done
  215.8 0.0 copy-start.1
  215.8 1.0 copy-done.1
  216.9 0.0 copy-start.2
  216.9 0.8 copy-done.2
  217.6 2.0 shard_map.299
Async XLA Ops:
  214.5 1.3 copy-start
  215.8 1.0 copy-start.1
  216.9 0.8 copy-start.2

commit v3 on v2

--- a/solution.py
+++ b/solution.py
@@ -300,44 +300,52 @@
 OWN = 192
 PART = 96
 HALF = 80
-C_SL, C_QKV, C_IN, C_OUT, C_ALL, C_ONE = 0, 768, 1792, 3072, 4352, 2176
+C_QKV, C_IN, C_OUT, C_ALL, C_ONE = 512, 1792, 2432, 3072, 2176
+C_MLP = 896
+BOTH = 2 * TOK
+MLP_TILES = ((0, 256), (256, 256), (512, 128))
+SPLIT = 640
 CHUNKS = (
-    (0, 384, 128, 0),
-    (128, 384, 128, 128),
-    (256, 384, 128, 256),
-    (768, 512, 256, 384),
-    (1024, 512, 256, 640),
-    (1792, 640, 256, 896),
-    (2048, 640, 384, 1152),
-    (3072, 640, 256, 1536),
-    (3328, 640, 256, 1792),
-    (3584, 640, 128, 2048),
+    (0, 256, 128, 0),
+    (128, 256, 128, 128),
+    (512, 640, 256, 256),
+    (768, 640, 256, 512),
+    (1024, 640, 128, 768),
+    (1792, 0, 256, 896),
+    (2048, 0, 384, 1152),
+    (2432, 0, 256, 1536),
+    (2688, 0, 256, 1792),
+    (2944, 0, 128, 2048),
 )
-GATHER_ORDER = ("zxy", "zyx", "zxy", "zyx", "zxy", "zyx", "zxy", "zyx", "zxy", "zyx")
-SUM_ORDER = ("yxz", "xyz", "yxz", "xyz", "yxz", "xyz", "yxz", "xyz", "yxz", "xyz")
+GATHER_ORDER = ("zxy", "zyx", "zxy", "zyx", "zxy", "zy", "zy", "zy", "zy", "zy")
+SUM_ORDER = ("yxz", "xyz", "yxz", "xyz", "yxz", "yz", "yz", "yz", "yz", "yz")
 (
     FIRST, OWNED, SECOND, THIRD, HERE, SUM, FEATS, COT, COT_HERE, TOKENS, VECTORS, NORM_1, PROJECT, TURN, ATTEND,
-    NORM_2, INNER, GRAD_OUT, OUTER, GRAD_IN, BACK_2, D_ATT, ATTEND_B, TURN_B, FINISH, GRAD_QKV, GRAD_ATT,
-    GRAD_BIAS, BACK_1, D_HID, GRAD_TOK, GRAD_HID, POINTS, SEND, PASS,
-) = range(35)
+    NORM_2, INNER, GRAD_OUT, OUTER, GRAD_IN, BACK_2, D_ATT, ATTEND_B, TURN_B, FINISH, GRAD_QKV, GRAD_BIAS, BACK_1,
+    D_HID, GRAD_TOK, GRAD_HID, POINTS, SEND, PASS, COT_PASS, NORM_PASS, CROSS, HIDDEN,
+) = range(38)
 PLAN = (
-    (FIRST, 2), (FIRST, 5), (FIRST, 1), (OWNED, 2), (FIRST, 0), (OWNED, 5), (OWNED, 1), (FIRST, 3), (OWNED, 0),
-    (FIRST, 4), (OWNED, 3), (FIRST, 6), (OWNED, 4), (SECOND, 2), (SECOND, 1), (FIRST, 8), (THIRD, 2), (SECOND, 0),
-    (THIRD, 1), (FIRST, 7), (THIRD, 0), (OWNED, 6), (FEATS,), (HERE, 0), (HERE, 2), (SECOND, 5), (HERE, 1), (TOKENS,),
-    (FIRST, 9), (SECOND, 3), (SEND, 0), (PASS, 0), (SECOND, 4), (OWNED, 7), (THIRD, 3), (OWNED, 8), (THIRD, 4),
-    (VECTORS,), (SECOND, 6), (COT,), (NORM_1,), (HERE, 4), (OWNED, 9), (THIRD, 5), (HERE, 3), (PROJECT,), (SECOND, 7),
-    (TURN,), (THIRD, 6), (SECOND, 8), (ATTEND, 0), (ATTEND, 1), (ATTEND, 2), (SEND, 1), (PASS, 1), (THIRD, 7),
-    (HERE, 5), (SECOND, 9), (NORM_2,), (THIRD, 8), (THIRD, 9), (HERE, 6), (INNER,), (COT_HERE,), (GRAD_OUT, 9),
-    (GRAD_OUT, 8), (HERE, 9), (GRAD_OUT, 7), (HERE, 7), (HERE, 8), (OUTER,), (SEND, 2), (PASS, 2), (SUM, 9),
-    (SEND, 3), (GRAD_IN, 6), (SUM, 8), (SUM, 9), (PASS, 3), (BACK_2,), (GRAD_IN, 5), (D_ATT,), (ATTEND_B, 1),
-    (ATTEND_B, 2), (ATTEND_B, 0), (SUM, 8), (SUM, 9), (TURN_B,), (SEND, 4), (SUM, 7), (PASS, 4), (SUM, 6),
-    (GRAD_BIAS,), (GRAD_ATT,), (SUM, 5), (SUM, 7), (SUM, 8), (GRAD_QKV, 3), (GRAD_QKV, 4), (BACK_1,), (SUM, 7),
-    (SUM, 9), (SUM, 6), (SUM, 8), (SUM, 3), (SUM, 4), (SUM, 5), (D_HID,), (SUM, 5), (SUM, 7), (GRAD_TOK,),
-    (POINTS, 0), (SUM, 4), (SUM, 6), (SUM, 3), (SUM, 4), (POINTS, 1), (SUM, 3), (GRAD_HID,), (SUM, 0), (SUM, 5),
-    (SUM, 0), (SUM, 6), (SUM, 1), (SUM, 2), (SUM, 2), (SUM, 3), (POINTS, 2), (SUM, 1), (SUM, 0), (FINISH,), (SUM, 0),
-    (SUM, 2), (SUM, 2), (SUM, 4), (SUM, 1), (SUM, 1), (POINTS, 3),
+    (FIRST, 0), (FIRST, 4), (FIRST, 2), (FIRST, 1), (OWNED, 0), (FIRST, 3), (OWNED, 1), (FIRST, 7), (OWNED, 3),
+    (FIRST, 5), (OWNED, 4), (SECOND, 0), (FIRST, 8), (SECOND, 1), (OWNED, 2), (FEATS,), (COT,), (THIRD, 1),
+    (THIRD, 0), (SECOND, 4), (SECOND, 3), (SECOND, 2), (HERE, 0), (OWNED, 5), (FIRST, 6), (HERE, 1), (HIDDEN,),
+    (TOKENS, 1), (THIRD, 4), (OWNED, 7), (TOKENS, 0), (FIRST, 9), (SEND, 0, 1), (THIRD, 2), (SEND, 0, 0),
+    (PASS, 0, 1), (THIRD, 3), (OWNED, 6), (SECOND, 5), (PASS, 0, 0), (OWNED, 8), (VECTORS,), (HERE, 3), (HERE, 4),
+    (NORM_1, 1), (SECOND, 7), (HERE, 2), (PROJECT, 1), (TURN, 1), (ATTEND, 1), (SEND, 1, 1), (PASS, 1, 1),
+    (NORM_1, 0), (SECOND, 6), (COT_PASS,), (OWNED, 9), (PROJECT, 0), (TURN, 0), (ATTEND, 0), (SEND, 1, 0), (HERE, 5),
+    (PASS, 1, 0), (SECOND, 8), (NORM_2, 1), (SECOND, 9), (NORM_2, 0), (COT_HERE,), (HERE, 6), (NORM_PASS, 1),
+    (INNER, 0, 1), (HERE, 7), (HERE, 8), (INNER, 1, 1), (HERE, 9), (OUTER, 1), (SEND, 2, 1), (SEND, 3, 1),
+    (NORM_PASS, 0), (CROSS, 2, 1), (INNER, 0, 0), (INNER, 1, 0), (GRAD_OUT, 7), (OUTER, 0), (SEND, 2, 0),
+    (PASS, 2, 1), (CROSS, 2, 0), (CROSS, 3, 1), (GRAD_IN, 5), (SUM, 7), (GRAD_IN, 6), (PASS, 2, 0), (BACK_2, 1),
+    (SEND, 3, 0), (SUM, 5), (D_ATT, 1), (ATTEND_B, 1), (GRAD_OUT, 8), (PASS, 3, 1), (TURN_B, 1), (SEND, 4, 1),
+    (BACK_2, 0), (GRAD_OUT, 9), (GRAD_BIAS,), (CROSS, 3, 0), (D_ATT, 0), (SUM, 6), (PASS, 4, 1), (ATTEND_B, 0),
+    (TURN_B, 0), (SUM, 6), (SUM, 7), (SEND, 4, 0), (GRAD_QKV, 4), (SUM, 5), (PASS, 4, 0), (GRAD_QKV, 3),
+    (GRAD_QKV, 2), (BACK_1, 1), (SUM, 4), (SUM, 8), (SUM, 9), (PASS, 3, 0), (D_HID, 1), (BACK_1, 0), (D_HID, 0),
+    (SUM, 3), (POINTS, 0), (SUM, 2), (SUM, 4), (SUM, 5), (GRAD_TOK,), (SUM, 2), (SUM, 7), (GRAD_HID,), (SUM, 8),
+    (SUM, 4), (POINTS, 1), (SUM, 2), (SUM, 3), (SUM, 4), (SUM, 9), (SUM, 6), (SUM, 3), (SUM, 0), (SUM, 1), (SUM, 0),
+    (SUM, 8), (SUM, 1), (FINISH,), (SUM, 3), (SUM, 0), (SUM, 1), (POINTS, 2), (SUM, 2), (SUM, 0), (SUM, 1), (SUM, 9),
+    (POINTS, 3),
 )
-L_RES, L_ONE, L_VEC, L_BIN, L_HID = 64, 72, 73, 77, 79
+L_RES, L_ONE, L_VEC, L_BIN, L_HID = 32, 40, 41, 45, 47
 TILE = 256
 TILES = D // TILE
 SCALE = 1.0 / math.sqrt(HEAD_DIM)
@@ -355,10 +363,10 @@
     points, missing, hid_w, hid_b, tok_in, res_t, tok_b, gain1, qkv_in, att_in, gain2, win_in, b_in, wout_in,
     out_b, cot_in, rot_c, rot_a, rot_b,
     out_o, pts_o, fb,
-    w, g, rb, fe, cot, part, pre, act, dpre, n1, n2, db, x0, x1,
-    hc, dpe, pret, q_s, kv_s, att, datt, dpj, ps, gbs, ghs, hidf, hid, vec, bin_s, sums, ptx, ptr,
+    w, g, rb, rbm, fe, cot, part, pre, act, dpre, n1, n2, db, de, x0, x1, x2,
+    hc, dpe, pret, q_s, k_s, v_s, att, datt, dpj, ps, gbs, ghs, hidf, hid, vec, bin_s, sums, ptx, ptr,
     pk, pkf, srcf, tmp,
-    cs, cr, xs, xr,
+    part3, cs, cr, ys, yr, xs, xr,
     ag_s, ag_r, rs_s, rs_r, ar_s, ar_r, nx_s, nx_r, in_s, in_r, lo_s, tk_s, tk_r, fin_s, fin_r, pt_s, pt_r,
 ):
     f32, bf16 = jnp.float32, jnp.bfloat16
@@ -374,8 +382,8 @@
     beside = {"fsdp": f + 4 - 8 * l}
     corner = {"fsdp": f + 4 - 8 * l + 1 - 2 * c}
     along = {"z": {"fsdp": f + 8 - 16 * zh}, "y": {"fsdp": f + 2 - 4 * y}, "x": {"tp": 1 - x}}
-    own0 = pl.multiple_of(OWN * c, OWN)
-    oth0 = pl.multiple_of(OWN * (1 - c), OWN)
+    own0 = pl.multiple_of(PART * c, PART)
+    oth0 = pl.multiple_of(PART * (1 - c), PART)
 
     def m16(v):
         return pl.multiple_of(v, 16)
@@ -415,17 +423,16 @@
     for q in range(4):
         col = 160 * q
         pkf[:, 0:160] = part[0:80, col : col + 160]
-        pkf[:, 160:320] = part[80:160, col : col + 160]
-        pkf[:, 320:384] = jnp.zeros((80, 64), f32)
+        pkf[:, 160:256] = jnp.zeros((80, 96), f32)
         place = (row < 32) & (row >= 8 * q) & (row < 8 * q + 8) & (lane == L_RES + row - 8 * q)
         place = place | ((row >= 32) & (row < 38) & (lane == L_VEC + row - 32))
         place = place | ((row >= 40) & (lane == L_HID + row - 40))
-        pkf[:, 256:384] = pkf[:, 256:384] + dot_rows(src, one_hot(place))[0:80]
-        pkf[64:65, 256 + L_HID : 256 + L_HID + 40] = hid_b[...].astype(f32)
-        pkf[:, 384:544] = part[160:240, col : col + 160]
-        pkf[:, 544:704] = part[240:320, col : col + 160]
-        pkf[:, 704:864] = part[0:80, 640 + col : 800 + col]
-        pkf[:, 864:896] = jnp.zeros((80, 32), f32)
+        pkf[:, 128:256] = pkf[:, 128:256] + dot_rows(src, one_hot(place))[0:80]
+        pkf[64:65, 128 + L_HID : 128 + L_HID + 40] = hid_b[...].astype(f32)
+        pkf[:, 256:416] = part[160:240, col : col + 160]
+        pkf[:, 416:576] = part[240:320, col : col + 160]
+        pkf[:, 576:736] = part[0:80, 640 + col : 800 + col]
+        pkf[:, 736:896] = part[80:160, col : col + 160]
         pk[q] = pkf[...].astype(bf16)
 
     pl.semaphore_wait(barrier, len(peers))
@@ -473,20 +480,19 @@
         remote(ref, ref, ag_s.at[k, i], ag_r.at[k, i], along[flips[-1]]).wait_recv()
 
     def g_own(k):
-        a, b, d = GATHER_ORDER[k]
+        order = GATHER_ORDER[k]
         locals_in[k].wait()
         for i, (to, member) in enumerate(group):
             ref = w.at[rows_of(to), cols(k, x)]
             remote(ref, ref, in_s.at[k, i], in_r.at[k, i], to).wait_recv()
-        g_send(k, 0, "", a)
-        g_send(k, 1, "", b)
-        g_send(k, 3, "", d)
+        for axis, i in zip(order, (0, 1, 3)):
+            g_send(k, i, "", axis)
 
     def g_second(k):
-        a, b, d = GATHER_ORDER[k]
+        a, *rest = GATHER_ORDER[k]
         g_recv(k, 0, a)
-        g_send(k, 2, a, b)
-        g_send(k, 4, a, d)
+        for axis, i in zip(rest, (2, 4)):
+            g_send(k, i, a, axis)
 
     def g_third(k):
         a, b, d = GATHER_ORDER[k]
@@ -496,15 +502,20 @@
         g_send(k, 6, a + b, d)
 
     def g_done(k):
-        a, b, d = GATHER_ORDER[k]
+        order = GATHER_ORDER[k]
+        if len(order) == 2:
+            g_recv(k, 1, order[1])
+            g_recv(k, 2, order)
+            return
+        a, b, d = order
         g_recv(k, 3, d)
         g_recv(k, 4, a + d)
         g_recv(k, 5, b + d)
-        g_recv(k, 6, a + b + d)
+        g_recv(k, 6, order)
 
     def s_buf(k, i):
         _, _, width, at = CHUNKS[k]
-        return rb.at[i, :, :, at : at + width]
+        return rb.at[i, :, :, at : at + width] if at < C_MLP else rbm.at[i, :, :, at - C_MLP : at - C_MLP + width]
 
     def s_send(k, i, flips, axis):
         go(remote(block(g4, k, flips), s_buf(k, i), rs_s.at[k, i], rs_r.at[k, i], along[axis]))
@@ -521,22 +532,44 @@
             half = lax.div(j, 2)
             inside = 80 * (j - 2 * half)
             here = pl.ds(m16(640 * zz + 320 * half + 160 * yy + inside), 80)
-            g[here, there] = g[here, there] + rb[i, half, pl.ds(m16(inside), 80), at : at + width]
+            rows = pl.ds(m16(inside), 80)
+            if at < C_MLP:
+                came = rb[i, half, rows, at : at + width]
+            else:
+                came = rbm[i, half, rows, at - C_MLP : at - C_MLP + width]
+            g[here, there] = g[here, there] + came
             return carry
 
         lax.fori_loop(0, 4, step, 0)
 
     def s_start(k):
-        a, b, d = SUM_ORDER[k]
-        s_send(k, 0, a + b + d, a)
-        s_send(k, 1, a + b, a)
-        s_send(k, 2, a + d, a)
-        s_send(k, 3, a, a)
+        a, b, *last = SUM_ORDER[k]
+        if last:
+            d = last[0]
+            s_send(k, 0, a + b + d, a)
+            s_send(k, 1, a + b, a)
+            s_send(k, 2, a + d, a)
+            s_send(k, 3, a, a)
+        else:
+            s_send(k, 0, a + b, a)
+            s_send(k, 1, a, a)
         s_at[k] = 0
 
     def s_step(k):
-        a, b, d = SUM_ORDER[k]
+        a, b, *last = SUM_ORDER[k]
         stage = s_at[k]
+        s_at[k] = stage + 1
+        if not last:
+            if stage == 0:
+                s_add(k, 0, b, a)
+                s_send(k, 2, b, b)
+            elif stage == 1:
+                s_add(k, 1, "", a)
+            else:
+                s_add(k, 2, "", b)
+                s_out(k)
+            return
+        d = last[0]
         if stage == 0:
             s_add(k, 0, b + d, a)
             s_send(k, 4, b + d, b)
@@ -551,77 +584,116 @@
             s_add(k, 5, "", b)
         else:
             s_add(k, 6, "", d)
-            _, _, width, at = CHUNKS[k]
-            for i, (to, member) in enumerate(group):
-                src = g.at[rows_of(to), cols(k, x)]
-                go(remote(src, fb.at[m, :, at : at + width], fin_s.at[k, i], fin_r.at[k, i], to))
-            fb[m, :, at : at + width] = g[pl.ds(m16(HALF * f), HALF), cols(k, x)]
-            del s_at[k]
-            return
-        s_at[k] = stage + 1
+            s_out(k)
+
+    def s_out(k):
+        _, _, width, at = CHUNKS[k]
+        for i, (to, member) in enumerate(group):
+            src = g.at[rows_of(to), cols(k, x)]
+            go(remote(src, fb.at[m, :, at : at + width], fin_s.at[k, i], fin_r.at[k, i], to))
+        fb[m, :, at : at + width] = g[pl.ds(m16(HALF * f), HALF), cols(k, x)]
 
     s_at = {}
 
     def ar_tile(i):
-        return slice(TILE * i, TILE * i + TILE)
-
-    def ar_begin(a):
-        left, lo, width = operands[a]
-        b = a % 2
+        return slice(SPLIT * i, SPLIT * i + SPLIT)
+
+    def cs_ref(a, p, i):
+        rows = OWN if a in (2, 3) else PART
+        return cs.at[a % 2, p, 0:rows, ar_tile(i)], cr.at[a % 2, p, 0:rows, ar_tile(i)]
+
+    def total(a):
+        return part3 if a == 3 else part
+
+    def ar_begin(a, p):
         if a >= 2:
-            for i in range(TILES):
-                done = cs.at[b, :, ar_tile(i)]
-                remote(done, done, ar_s.at[a - 2, 0, i], ar_r.at[a - 2, 0, i], mate).wait_send()
-        for i in range(TILES):
-            part[:, ar_tile(i)] = dot_last(left[...], w[ar_tile(i), lo : lo + width])
-            cs[b, :, ar_tile(i)] = part[pl.ds(oth0, OWN), ar_tile(i)].astype(bf16)
-            copy = remote(cs.at[b, :, ar_tile(i)], cr.at[b, :, ar_tile(i)], ar_s.at[a, 0, i], ar_r.at[a, 0, i], mate)
+            for i in range(2):
+                done, there = cs_ref(a - 2, p, i)
+                remote(done, there, ar_s.at[a - 2, 0, p, i], ar_r.at[a - 2, 0, p, i], mate).wait_send()
+        for i in range(2):
+            for n, first in enumerate((0, TOK) if a in (2, 3) else (0,)):
+                rows = slice(first + OWN * p, first + OWN * p + OWN)
+                value = None
+                for left, lo, col, width in operands[a]:
+                    more = dot_last(left[rows, lo : lo + width], w[ar_tile(i), col : col + width])
+                    value = more if value is None else value + more
+                total(a)[rows, ar_tile(i)] = value
+                away = pl.ds(m16(first + OWN * p + oth0), PART)
+                cs[a % 2, p, PART * n : PART * n + PART, ar_tile(i)] = total(a)[away, ar_tile(i)].astype(bf16)
+            src, there = cs_ref(a, p, i)
+            copy = remote(src, there, ar_s.at[a, 0, p, i], ar_r.at[a, 0, p, i], mate)
             copy.start()
             if a >= 3:
                 sent.append(copy)
 
-    def ar_mid(a):
+    def ar_cross(a, p):
+        b = a - 2
+        near = pl.ds(m16(TOK * x + OWN * p + own0), PART)
+        far = pl.ds(m16(TOK * (1 - x) + OWN * p + own0), PART)
+        for i in range(2):
+            _, here = cs_ref(a, p, i)
+            remote(here, here, ar_s.at[a, 0, p, i], ar_r.at[a, 0, p, i], mate).wait_recv()
+            came = cr[a % 2, p, pl.ds(m16(PART * (1 - x)), PART), ar_tile(i)].astype(f32)
+            ys[b, p, :, ar_tile(i)] = (total(a)[far, ar_tile(i)] + came).astype(bf16)
+            go(remote(
+                ys.at[b, p, :, ar_tile(i)], yr.at[b, p, :, ar_tile(i)], ar_s.at[a, 2, p, i], ar_r.at[a, 2, p, i],
+                along["x"],
+            ))
+            total(a)[near, ar_tile(i)] = total(a)[near, ar_tile(i)] + cr[
+                a % 2, p, pl.ds(m16(PART * x), PART), ar_tile(i)
+            ].astype(f32)
+
+    def ar_mid(a, p):
         b = a % 2
         if a >= 2:
-            for i in range(TILES):
-                done = xs.at[b, :, ar_tile(i)]
-                remote(done, done, ar_s.at[a - 2, 1, i], ar_r.at[a - 2, 1, i], beside).wait_send()
-        for i in range(TILES):
-            here = cr.at[b, :, ar_tile(i)]
-            remote(here, here, ar_s.at[a, 0, i], ar_r.at[a, 0, i], mate).wait_recv()
-            xs[b, :, ar_tile(i)] = (
-                part[pl.ds(own0, OWN), ar_tile(i)] + cr[b, :, ar_tile(i)].astype(f32)
-            ).astype(bf16)
+            for i in range(2):
+                done = xs.at[b, p, :, ar_tile(i)]
+                remote(done, done, ar_s.at[a - 2, 1, p, i], ar_r.at[a - 2, 1, p, i], beside).wait_send()
+        for i in range(2):
+            if a in (2, 3):
+                here = yr.at[a - 2, p, :, ar_tile(i)]
+                remote(here, here, ar_s.at[a, 2, p, i], ar_r.at[a, 2, p, i], along["x"]).wait_recv()
+                mine = total(a)[pl.ds(m16(TOK * x + OWN * p + own0), PART), ar_tile(i)]
+                came = yr[a - 2, p, :, ar_tile(i)]
+            else:
+                _, here = cs_ref(a, p, i)
+                remote(here, here, ar_s.at[a, 0, p, i], ar_r.at[a, 0, p, i], mate).wait_recv()
+                mine = part[pl.ds(m16(OWN * p + own0), PART), ar_tile(i)]
+                came = cr[b, p, 0:PART, ar_tile(i)]
+            xs[b, p, :, ar_tile(i)] = (mine + came.astype(f32)).astype(bf16)
             copy = remote(
-                xs.at[b, :, ar_tile(i)], xr.at[a % 3, :, ar_tile(i)], ar_s.at[a, 1, i], ar_r.at[a, 1, i], beside
+                xs.at[b, p, :, ar_tile(i)], xr.at[a % 3, p, :, ar_tile(i)], ar_s.at[a, 1, p, i], ar_r.at[a, 1, p, i],
+                beside,
             )
             copy.start()
             if a >= 3:
                 sent.append(copy)
 
-    def ar_end(a):
-        for i in range(TILES):
-            here = xr.at[a % 3, :, ar_tile(i)]
-            remote(here, here, ar_s.at[a, 1, i], ar_r.at[a, 1, i], beside).wait_recv()
-
-    def summed(a, rows):
-        return xs[a % 2, rows, :].astype(f32) + xr[a % 3, rows, :].astype(f32)
-
-    def own_rows(body, first=0, count=OWN, size=32):
+    def ar_end(a, p):
+        for i in range(2):
+            here = xr.at[a % 3, p, :, ar_tile(i)]
+            remote(here, here, ar_s.at[a, 1, p, i], ar_r.at[a, 1, p, i], beside).wait_recv()
+
+    def summed(a, p, rows):
+        return xs[a % 2, p, rows, :].astype(f32) + xr[a % 3, p, rows, :].astype(f32)
+
+    def own_rows(body):
         def step(j, carry):
-            start = m16(first + size * j)
-            body(pl.ds(start, size), pl.ds(m16(own0 + start), size))
+            body(pl.multiple_of(32 * j, 32))
             return carry
 
-        lax.fori_loop(0, count // size, step, 0)
-
-    def share(j, ref):
-        rows = ref.at[pl.ds(own0, OWN)]
-        go(remote(rows, rows, nx_s.at[j], nx_r.at[j], mate))
-
-    def shared(j, ref):
-        rows = ref.at[pl.ds(oth0, OWN)]
-        remote(rows, rows, nx_s.at[j], nx_r.at[j], mate).wait_recv()
+        lax.fori_loop(0, PART // 32, step, 0)
+
+    def at32(start):
+        return pl.ds(m16(start), 32)
+
+    def share(j, p, ref, first=0, to=None):
+        rows = ref.at[pl.ds(m16(first + OWN * p + own0), PART)]
+        go(remote(rows, rows, nx_s.at[j, p], nx_r.at[j, p], mate if to is None else to))
+
+    def shared(j, p, ref, first=0, start=None, to=None):
+        rows = ref.at[pl.ds(m16(first + OWN * p + (oth0 if start is None else start)), PART)]
+        remote(rows, rows, nx_s.at[j, p], nx_r.at[j, p], mate if to is None else to).wait_recv()
 
     def rms(v):
         return lax.rsqrt(jnp.mean(v * v, axis=-1, keepdims=True) + 1e-06)
@@ -636,40 +708,23 @@
 
         lax.fori_loop(0, count, step, 0)
 
-    def grad_block(k, left, right, base):
-        first, apart, width, _ = CHUNKS[k]
-
-        def body(rows, i):
-            for h in (0, 1):
-                lo = first - base + apart * h
-                g[rows, first + apart * h : first + apart * h + width] = dot_rows(
-                    left[:, rows], right[:, lo : lo + width]
-                ).astype(bf16)
-
-        tiles_loop(TILES, body)
-
     def slab(h):
-        return slice(256 + 384 * h, 384 + 384 * h)
+        return slice(128 + 256 * h, 256 + 256 * h)
 
     spread = one_hot(lax.div(iota((OWN, 12), 0), CTXLEN) == iota((OWN, 12), 1))
     right_patch = lax.div(iota((OWN, 512), 1), PL) == (iota((OWN, 512), 0) & (CTXLEN - 1))
     lane_of = iota((512, 128), 1)
     place_of = iota((512, 128), 0) & (PL - 1)
-    mine0 = m16(own0 + PART * l)
-    cot_part = cot_in.at[pl.ds(m16(PART * x), PART)]
-    cot_copy = pltpu.make_async_copy(cot_part, cot.at[pl.ds(mine0, PART)], lo_s.at[len(CHUNKS)])
-    lane768 = iota((TOK, 768), 1)
-    lane384 = jnp.where(lane768 >= 384, lane768 - 384, lane768)
-    units = lane384 < 160
-    resids = (lane384 >= 256 + L_RES) & (lane384 < 256 + L_RES + 8)
-    de = act
-
-    def tokens_here(j, ref):
-        for i, (to, member) in enumerate(group):
-            cc = 1 - c if i != 1 else c
-            ll = l if i == 0 else 1 - l
-            rows = ref.at[pl.ds(m16(OWN * cc + PART * ll), PART)]
-            remote(rows, rows, tk_s.at[j, i], tk_r.at[j, i], to).wait_recv()
+    mine0 = m16(OWN * l + own0)
+    cot_part = cot_in.reshape(2, PART, D)
+    cot_rows = cot.reshape(2, TOK, D)
+    cot_copy = pltpu.make_async_copy(cot_part, cot_rows.at[:, pl.ds(mine0, PART)], lo_s.at[len(CHUNKS)])
+    lane512 = iota((OWN, 512), 1) & 255
+    units = lane512 < 160
+    resids = (lane512 >= 128 + L_RES) & (lane512 < 128 + L_RES + 8)
+
+    def part_rows(p, first=0):
+        return slice(first + OWN * p, first + OWN * p + OWN)
 
     def features():
         keep = 1.0 - missing[...].astype(f32)
@@ -687,303 +742,341 @@
 
     def cot_out():
         cot_copy.start()
-        for i, (to, member) in enumerate(group):
-            go(remote(cot_part, cot.at[pl.ds(mine0, PART)], tk_s.at[1, i], tk_r.at[1, i], to))
+        for i, to in enumerate((mate, beside)):
+            go(remote(cot_part, cot_rows.at[:, pl.ds(mine0, PART)], tk_s.at[1, i], tk_r.at[1, i], to))
+
+    def cot_pass():
+        rows = cot_rows.at[:, pl.ds(m16(OWN * (1 - l) + own0), PART)]
+        remote(rows, rows, tk_s.at[1, 1], tk_r.at[1, 1], beside).wait_recv()
+        go(remote(rows, rows, tk_s.at[1, 2], tk_r.at[1, 2], mate))
 
     def cot_here():
         cot_copy.wait()
-        tokens_here(1, cot)
-
-    def tokenize():
+        for i, ll in ((0, l), (2, 1 - l)):
+            rows = cot_rows.at[:, pl.ds(m16(OWN * ll + oth0), PART)]
+            remote(rows, rows, tk_s.at[1, i], tk_r.at[1, i], mate).wait_recv()
+
+    def hidden():
         for h in (0, 1):
             for j in range(4):
                 rows = pl.ds(m16(320 * m + 80 * j), 80)
                 tmp[:, 0:128] = w[rows, slab(h)].astype(f32)
-                hidf[0:72, 384 * h + 40 * j : 384 * h + 40 * j + 40] = tmp[0:72, L_HID : L_HID + 40]
+                hidf[0:72, 256 * h + 40 * j : 256 * h + 40 * j + 40] = tmp[0:72, L_HID : L_HID + 40]
             row = iota((128, 128), 0)
             lane = iota((128, 128), 1)
             chosen = (lane >= L_RES) & (lane < L_RES + 8) & (row == PL * h + 8 * m + lane - L_RES)
-            hidf[:, slab(h)] = jnp.where(chosen, 1.0, 0.0)
+            hidf[:, slab(h)] = jnp.where(chosen, 1.0, hidf[:, slab(h)])
         hid[...] = hidf[...].astype(bf16)
-        tokens_here(0, fe)
-        pret[...] = dot_plain(fe[...], hid[...])
-        v = pret[...]
-        hc[...] = jnp.where(
-            units, v * jax.nn.sigmoid(v), jnp.where(resids, v, jnp.where(lane384 == 256 + L_ONE, 1.0, 0.0))
+        for i, (to, member) in enumerate(group):
+            cc = 1 - c if i != 1 else c
+            ll = l if i == 0 else 1 - l
+            rows = fe.at[pl.ds(m16(OWN * ll + PART * cc), PART)]
+            remote(rows, rows, tk_s.at[0, i], tk_r.at[0, i], to).wait_recv()
+
+    def tokenize(p):
+        v = dot_plain(fe[part_rows(p), :], hid[...])
+        pret[part_rows(p), :] = v
+        hc[part_rows(p), :] = jnp.where(
+            units, v * jax.nn.sigmoid(v), jnp.where(resids, v, jnp.where(lane512 == 128 + L_ONE, 1.0, 0.0))
         ).astype(bf16)
 
     def vectors():
         row16 = iota((16, 128), 0)
         lane16 = iota((16, 128), 1)
         vec[...] = dot_last(one_hot((row16 < 4) & (lane16 == L_VEC + row16)), w[:, slab(0)])
+        own_slab = pl.ds(pl.multiple_of(128 + 256 * x, 128), 128)
+        pair = dot_last(one_hot((row16 < 2) & (lane16 == L_BIN + row16)), w[pl.ds(m16(320 * m), 320), own_slab])
+        tmp[0:16, 0:320] = pair
+        for j in range(4):
+            at = 160 * j
+            bin_s[0:1, at : at + 80] = tmp[0:1, 80 * j : 80 * j + 80]
+            bin_s[0:1, at + 80 : at + 160] = tmp[1:2, 80 * j : 80 * j + 80]
+
+    def first_norm(p):
+        ar_end(0, p)
+
+        def body(start):
+            v = summed(0, p, pl.ds(start, 32)) + vec[3:4, :]
+            x0[at32(PART * p + start), :] = v
+            n1[at32(OWN * p + own0 + start), :] = (v * rms(v) * vec[0:1, :]).astype(bf16)
+
+        own_rows(body)
+        share(0, p, n1)
+
+    def project(p):
+        shared(0, p, n1)
+        rows = part_rows(p)
         for h in (0, 1):
-            pair = dot_last(one_hot((row16 < 2) & (lane16 == L_BIN + row16)), w[pl.ds(m16(320 * m), 320), slab(h)])
-            tmp[0:16, 0:320] = pair
-            for j in range(4):
-                at = 640 * h + 160 * j
-                bin_s[0:1, at : at + 80] = tmp[0:1, 80 * j : 80 * j + 80]
-                bin_s[0:1, at + 80 : at + 160] = tmp[1:2, 80 * j : 80 * j + 80]
-
-    def first_norm():
-        ar_end(0)
-
-        def body(rows, mine):
-            v = summed(0, rows) + vec[3:4, :]
-            x0[rows, :] = v
-            n1[mine, :] = (v * rms(v) * vec[0:1, :]).astype(bf16)
-
-        own_rows(body)
-        share(0, n1)
-
-    def project():
-        shared(0, n1)
-
-        def body(cols, i):
-            part[:, cols] = dot_plain(n1[...], w[:, pl.ds(pl.multiple_of(C_QKV + TILE * i, TILE), TILE)])
-
-        tiles_loop(4, body)
-
-    def turn():
+            for lo in (0, 256):
+                col = C_QKV + 640 * h + lo
+                part[rows, 512 * h + lo : 512 * h + lo + 256] = dot_plain(n1[rows, :], w[:, col : col + 256])
+
+    def turn(p):
         def body(j, carry):
-            rows = pl.ds(m16(16 * j), 16)
-            v = part[rows, 0:1024]
-            v = v * rot_c[...] + pltpu.roll(v, 984, 1) * rot_a[...] + pltpu.roll(v, 40, 1) * rot_b[...]
+            rows = pl.ds(m16(OWN * p + 48 * j), 48)
             for h in (0, 1):
-                one = v[:, 512 * h : 512 * h + 512]
-                q_s[h, rows, :] = one[:, 0:256].astype(bf16)
-                kv_s[h, rows, :] = pltpu.roll(one, 352, 1)[:, 0:384].astype(bf16)
+                v = part[rows, 512 * h : 512 * h + 512]
+                v = v * rot_c[...] + pltpu.roll(v, 472, 1) * rot_a[...] + pltpu.roll(v, 40, 1) * rot_b[...]
+                q_s[h, rows, :] = v[:, 0:256].astype(bf16)
+                k_s[h, rows, :] = pltpu.roll(v, 352, 1)[:, 0:256].astype(bf16)
+                v_s[h, rows, :] = pltpu.roll(v, 288, 1)[:, 0:256].astype(bf16)
             return carry
 
-        lax.fori_loop(0, TOK // 16, body, 0)
+        lax.fori_loop(0, OWN // 48, body, 0)
+
+    def one_head(v, first, i):
+        lane = iota(v.shape, 1)
+        inside = (lane >= first + HEAD_DIM * i) & (lane < first + HEAD_DIM * i + HEAD_DIM)
+        return jnp.where(inside, v, jnp.zeros_like(v))
 
     def stacked(v, first):
-        head = iota(v.shape, 1)
-        return jnp.concatenate(
-            [
-                jnp.where((head >= first + HEAD_DIM * h) & (head < first + HEAD_DIM * h + HEAD_DIM), v, jnp.zeros_like(v))
-                for h in (0, 1)
-            ],
-            axis=0,
-        )
-
-    def side(v):
-        return jnp.concatenate([v[0:128], v[128:256]], axis=1)
-
-    def attend(b):
-        rows = slice(128 * b, 128 * b + 128)
-        qi = iota((256, 128), 0) & 127
-        kj = iota((256, 128), 1)
+        return jnp.concatenate([one_head(v, first, 0), one_head(v, first, 1)], axis=0)
+
+    def by_head(probs, v, first):
+        return dot_plain(probs[0:OWN], one_head(v, first, 0)) + dot_plain(probs[OWN:TOK], one_head(v, first, 1))
+
+    def attend(p):
+        rows = part_rows(p)
+        qi = iota((TOK, OWN), 0)
+        qi = jnp.where(qi >= OWN, qi - OWN, qi)
+        kj = iota((TOK, OWN), 1)
         allowed = ((qi >> 4) == (kj >> 4)) & (kj <= qi)
         for h in (0, 1):
-            kv = kv_s[h, rows, :]
-            scores = dot_last(stacked(q_s[h, rows, :], 0), kv[:, 0:256]) * SCALE
+            scores = dot_last(stacked(q_s[h, rows, :], 0), k_s[h, rows, :]) * SCALE
             scores = jnp.where(allowed, scores, -1e30)
             e = jnp.exp(scores - jnp.max(scores, axis=-1, keepdims=True))
             probs = e * (1.0 / jnp.sum(e, axis=-1, keepdims=True))
-            ps[512 * b + 256 * h : 512 * b + 256 * h + 256, :] = probs
-            att[rows, 384 * h : 384 * h + 384] = dot_plain(side(probs.astype(bf16)), stacked(kv, 160)).astype(bf16)
-
-    def second_norm():
-        ar_end(1)
-
-        def body(rows, mine):
-            v = x0[rows, :] + summed(1, rows)
-            x1[rows, :] = v
-            n2[mine, :] = (v * rms(v) * vec[1:2, :]).astype(bf16)
+            ps[p, h] = probs
+            att[rows, 256 * h : 256 * h + 256] = by_head(probs.astype(bf16), v_s[h, rows, :], 96).astype(bf16)
+
+    def second_norm(p):
+        ar_end(1, p)
+
+        def body(start):
+            own = at32(PART * p + start)
+            v = x0[own, :] + summed(1, p, pl.ds(start, 32))
+            x1[own, :] = v
+            n2[at32(TOK * x + OWN * p + own0 + start), :] = (v * rms(v) * vec[1:2, :]).astype(bf16)
 
         own_rows(body)
-        share(1, n2)
-
-    def inner():
-        shared(1, n2)
-
-        def body(cols, i):
-            v = dot_plain(n2[...], w[:, pl.ds(pl.multiple_of(C_IN + TILE * i, 128), TILE)]) + bin_s[0:1, cols]
-            pre[:, cols] = v
-            act[:, cols] = (v * jax.nn.sigmoid(v)).astype(bf16)
-
-        tiles_loop(TILES, body)
-
-    def outer_back():
-        def body(cols, i):
-            v = pre[:, cols]
-            s = jax.nn.sigmoid(v)
-            d = dot_plain(cot[...], w[:, pl.ds(pl.multiple_of(C_OUT + TILE * i, 128), TILE)])
-            dpre[:, cols] = (d * (s * (1.0 + v * (1.0 - s)))).astype(bf16)
-
-        tiles_loop(TILES, body)
-
-    def second_back():
-        ar_end(2)
-
-        def body(rows, mine):
-            dn = summed(2, rows)
-            v = x1[rows, :]
-            r = rms(v)
-            xh = v * r
-            scaled = dn * vec[1:2, :]
-            inside = jnp.mean(scaled * xh, axis=-1, keepdims=True)
-            ct = cot[mine, :].astype(f32)
-            d = ct + r * (scaled - xh * inside)
-            pre[rows, :] = d
-            db[mine, :] = d.astype(bf16)
-            sums[8:16, :] += fold(dn * xh)
+        share(1, p, n2, TOK * x, along["x"])
+        share(4, p, n2, TOK * x)
+
+    def norm_pass(p):
+        far = TOK * (1 - x)
+        shared(1, p, n2, far, own0, along["x"])
+        rows = n2.at[pl.ds(m16(far + OWN * p + own0), PART)]
+        go(remote(rows, rows, nx_s.at[5, p], nx_r.at[5, p], mate))
+
+    def inner(which, p):
+        first = TOK * (x if which == 0 else 1 - x)
+        shared(4 if which == 0 else 5, p, n2, first)
+        rows = pl.ds(m16(first + OWN * p), OWN)
+        for lo, width in MLP_TILES:
+            at = slice(lo, lo + width)
+            v = dot_plain(n2[rows, :], w[:, C_IN + lo : C_IN + lo + width]) + bin_s[0:1, at]
+            pre[rows, at] = v
+            act[rows, at] = (v * jax.nn.sigmoid(v)).astype(bf16)
+
+    def outer_back(p):
+        for first in (0, TOK):
+            rows = part_rows(p, first)
+            for lo, width in MLP_TILES:
+                at = slice(lo, lo + width)
+                v = pre[rows, at]
+                s = jax.nn.sigmoid(v)
+                d = dot_plain(cot[rows, :], w[:, C_OUT + lo : C_OUT + lo + width])
+                dpre[rows, at] = (d * (s * (1.0 + v * (1.0 - s)))).astype(bf16)
+
+    def norm_back(dn, v, gain):
+        r = rms(v)
+        xh = v * r
+        scaled = dn * gain
+        inside = jnp.mean(scaled * xh, axis=-1, keepdims=True)
+        return r * (scaled - xh * inside), fold(dn * xh)
+
+    def second_back(p):
+        ar_end(2, p)
+
+        def body(start):
+            own = at32(PART * p + start)
+            d, by_gain = norm_back(summed(2, p, pl.ds(start, 32)), x1[own, :], vec[1:2, :])
+            ct = cot[at32(TOK * x + OWN * p + own0 + start), :].astype(f32)
+            d = ct + d
+            x2[own, :] = d
+            db[at32(OWN * p + own0 + start), :] = d.astype(bf16)
+            sums[8:16, :] += by_gain
             sums[16:24, :] += fold(ct)
 
         own_rows(body)
-        share(2, db)
-
-    def attended_back():
-        shared(2, db)
-
-        def body(cols, i):
-            datt[:, cols] = dot_plain(db[...], w[:, cols]).astype(bf16)
-
-        tiles_loop(3, body)
-
-    def attend_back(b):
-        rows = slice(128 * b, 128 * b + 128)
+        share(2, p, db)
+
+    def attended_back(p):
+        shared(2, p, db)
+        rows = part_rows(p)
         for h in (0, 1):
-            probs = ps[512 * b + 256 * h : 512 * b + 256 * h + 256, :]
-            kv = kv_s[h, rows, :]
-            heads_d = stacked(datt[rows, 384 * h : 384 * h + 384], 160)
-            dp = dot_last(heads_d, kv)
+            col = C_QKV + 640 * h + 384
+            datt[rows, 256 * h : 256 * h + 256] = dot_plain(db[rows, :], w[:, col : col + 256]).astype(bf16)
+
+    def attend_back(p):
+        rows = part_rows(p)
+        for h in (0, 1):
+            probs = ps[p, h]
+            heads_d = stacked(datt[rows, 256 * h : 256 * h + 256], 96)
+            dp = dot_last(heads_d, v_s[h, rows, :])
             ds = (probs * (dp - jnp.sum(probs * dp, axis=-1, keepdims=True))).astype(bf16)
-            part[rows, 512 * h : 512 * h + 256] = dot_plain(side(ds), stacked(kv[:, 0:256], 0)) * SCALE
+            part[rows, 512 * h : 512 * h + 256] = by_head(ds, k_s[h, rows, :], 0) * SCALE
+            part[rows, 512 * h + 160 : 512 * h + 416] = dot_rows(ds, stacked(q_s[h, rows, :], 0)) * SCALE
             dv = dot_rows(probs.astype(bf16), heads_d)
-            dk = dot_rows(ds, stacked(q_s[h, rows, :], 0)) * SCALE
-            dkv = jnp.concatenate([dv[:, 0:256] + dk, dv[:, 256:384]], axis=1)
-            part[rows, 512 * h + 160 : 512 * h + 512] = dkv[:, 0:352]
-
-    def turn_back():
+            dv = jnp.concatenate([dv, jnp.zeros((OWN, 128), f32)], axis=1)
+            part[rows, 512 * h + 320 : 512 * h + 512] = dv[:, 96:288]
+
+    def turn_back(p):
         def body(j, carry):
-            rows = pl.ds(m16(16 * j), 16)
-            v = part[rows, 0:1024]
-            v = v * rot_c[...] - pltpu.roll(v, 984, 1) * rot_a[...] - pltpu.roll(v, 40, 1) * rot_b[...]
-            dpj[rows, :] = v.astype(bf16)
+            rows = pl.ds(m16(OWN * p + 48 * j), 48)
+            for h in (0, 1):
+                v = part[rows, 512 * h : 512 * h + 512]
+                v = v * rot_c[...] - pltpu.roll(v, 472, 1) * rot_a[...] - pltpu.roll(v, 40, 1) * rot_b[...]
+                dpj[rows, 512 * h : 512 * h + 512] = v.astype(bf16)
             return carry
 
-        lax.fori_loop(0, TOK // 16, body, 0)
+        lax.fori_loop(0, OWN // 48, body, 0)
 
     def finish():
-        ar_end(3)
-
-        def body(rows, mine):
-            start = rows.start - PART * l + PART * x
-            out_o[pl.ds(m16(start), 32), :] = (x1[rows, :] + summed(3, rows) + vec[2:3, :]).astype(bf16)
-
-        own_rows(body, PART * l, PART)
+        ar_end(3, 0)
+        ar_end(3, 1)
+
+        def body(start):
+            rows = pl.ds(start, 32)
+            v = xs[1, l, rows, :].astype(f32) + xr[0, l, rows, :].astype(f32)
+            out_o[at32(PART * x + start), :] = (x1[at32(PART * l + start), :] + v + vec[2:3, :]).astype(bf16)
+
+        own_rows(body)
         ref = out_o.at[pl.ds(m16(PART * x), PART)]
         go(remote(ref, ref, pt_s.at[3], pt_r.at[3], along["x"]))
 
+    def grad_mlp(k, left, right, base):
+        first, _, width, _ = CHUNKS[k]
+
+        def body(rows, i):
+            lo = first - base
+            g[rows, first : first + width] = dot_rows(left[:, rows], right[:, lo : lo + width]).astype(bf16)
+
+        tiles_loop(TILES, body)
+        s_start(k)
+
     def grad_out(k):
-        grad_block(k, cot, act, C_OUT)
+        grad_mlp(k, cot, act, C_OUT)
+
+    def grad_in(k):
+        grad_mlp(k, n2, dpre, C_IN)
+
+    def grad_qkv(k):
+        first, apart, width, _ = CHUNKS[k]
+
+        def body(rows, i):
+            for h in (0, 1):
+                for lo in range(first - C_QKV, first - C_QKV + width, 128):
+                    value = None
+                    if lo < 512:
+                        value = dot_rows(n1[:, rows], dpj[:, 512 * h + lo : 512 * h + lo + 128])
+                    if lo >= 384:
+                        more = dot_rows(db[:, rows], att[:, 256 * h + lo - 384 : 256 * h + lo - 256])
+                        value = more if value is None else value + more
+                    col = C_QKV + apart * h + lo
+                    g[rows, col : col + 128] = value.astype(bf16)
+
+        tiles_loop(TILES, body)
         s_start(k)
 
-    def grad_in(k):
-        grad_block(k, n2, dpre, C_IN)
-        s_start(k)
-
-    def grad_qkv(k):
-        grad_block(k, n1, dpj, C_QKV)
-        s_start(k)
-
-    def grad_att():
-        def body(rows, i):
-            g[rows, 0:768] = dot_rows(db[:, rows], att[...]).astype(bf16)
-
-        tiles_loop(TILES, body)
-
     def grad_bias():
-        ones = one_hot((iota((TOK, 128), 1) >= L_BIN) & (iota((TOK, 128), 1) < L_BIN + 2))
-
-        def body(rows, i):
-            gbs[rows, :] = dot_rows(dpre[:, rows], ones)
-
-        tiles_loop(TILES, body)
-
-    def first_back():
-        ar_end(4)
-
-        def body(rows, mine):
-            dn = summed(4, rows)
-            v = x0[rows, :]
-            r = rms(v)
-            xh = v * r
-            scaled = dn * vec[0:1, :]
-            inside = jnp.mean(scaled * xh, axis=-1, keepdims=True)
-            d = pre[rows, :] + r * (scaled - xh * inside)
-            de[mine, :] = d.astype(bf16)
-            sums[0:8, :] += fold(dn * xh)
+        ones = one_hot((iota((BOTH, 128), 1) >= L_BIN) & (iota((BOTH, 128), 1) < L_BIN + 2))
+        for lo, width in MLP_TILES:
+            gbs[lo : lo + width, :] = dot_rows(dpre[:, lo : lo + width], ones)
+
+    def first_back(p):
+        ar_end(4, p)
+
+        def body(start):
+            own = at32(PART * p + start)
+            d, by_gain = norm_back(summed(4, p, pl.ds(start, 32)), x0[own, :], vec[0:1, :])
+            de[at32(OWN * p + own0 + start), :] = (x2[own, :] + d).astype(bf16)
+            sums[0:8, :] += by_gain
 
         own_rows(body)
-        share(3, de)
-
-    def hidden_back():
-        shared(3, de)
-        v = pret[...]
+        share(3, p, de)
+
+    def hidden_back(p):
+        shared(3, p, de)
+        rows = part_rows(p)
+        v = pret[rows, :]
         s = jax.nn.sigmoid(v)
-        d = dot_plain(de[...], w[:, 0:768])
-        dpe[...] = jnp.where(units, d * (s * (1.0 + v * (1.0 - s))), jnp.where(resids, d, 0.0)).astype(bf16)
+        d = dot_plain(de[rows, :], w[:, 0:512])
+        dpe[rows, :] = jnp.where(units, d * (s * (1.0 + v * (1.0 - s))), jnp.where(resids, d, 0.0)).astype(bf16)
 
     def grad_tok():
         row32 = iota((32, 128), 0)
         pick = one_hot((row32 < 24) & (iota((32, 128), 1) == L_VEC + (row32 >> 3)))
 
         def body(rows, i):
-            both = g[rows, 0:768].astype(f32) + dot_rows(de[:, rows], hc[...])
+            both = dot_rows(de[:, rows], hc[...])
             columns = dot_rows(sums[:, rows].astype(bf16), pick)
             for h in (0, 1):
-                g[rows, 384 * h : 384 * h + 256] = both[:, 384 * h : 384 * h + 256].astype(bf16)
+                g[rows, 256 * h : 256 * h + 128] = both[:, 256 * h : 256 * h + 128].astype(bf16)
                 g[rows, slab(h)] = (both[:, slab(h)] + columns).astype(bf16)
 
         tiles_loop(TILES, body)
         s_start(0)
-        s_start(1)
 
     def grad_hidden():
         ghs[...] = dot_rows(fe[...], dpe[...])
         lane = iota((80, 128), 1)
         for h in (0, 1):
             for j in range(4):
-                at = 640 * h + 160 * j
-                tmp[:, 0:128] = jnp.where(lane == L_BIN, gbs[at : at + 80, :], 0.0) + jnp.where(
-                    lane == L_BIN + 1, gbs[at + 80 : at + 160, :], 0.0
+                at = 160 * j
+                tmp[:, 0:128] = jnp.where((lane == L_BIN) & (x == h), gbs[at : at + 80, :], 0.0) + jnp.where(
+                    (lane == L_BIN + 1) & (x == h), gbs[at + 80 : at + 160, :], 0.0
                 )
-                tmp[:, L_HID : L_HID + 40] = ghs[0:80, 384 * h + 40 * j : 384 * h + 40 * j + 40]
+                tmp[:, L_HID : L_HID + 40] = ghs[0:80, 256 * h + 40 * j : 256 * h + 40 * j + 40]
                 rows = pl.ds(m16(320 * m + 80 * j), 80)
                 g[rows, slab(h)] = (g[rows, slab(h)].astype(f32) + tmp[:, 0:128]).astype(bf16)
-        s_start(2)
+        s_start(1)
 
     def points_back(stage):
-        theirs = m16(PART * (1 - l))
-        mine = m16(PART * l)
-        half = pl.ds(m16(PART * x), PART)
         if stage == 0:
             ptx[...] = dot_last(dpe[...], hid[...])
-            go(remote(ptx.at[pl.ds(oth0, OWN)], ptr.at[0], pt_s.at[0], pt_r.at[0], mate))
+            away = ptx.reshape(2, OWN, 128).at[:, pl.ds(oth0, PART)]
+            go(remote(away, ptr.at[0], pt_s.at[0], pt_r.at[0], mate))
         elif stage == 1:
             remote(ptr.at[0], ptr.at[0], pt_s.at[0], pt_r.at[0], mate).wait_recv()
-            ptr[1] = ptx[pl.ds(own0, OWN), :] + ptr[0]
-            go(remote(ptr.at[1, pl.ds(theirs, PART)], ptr.at[2, pl.ds(theirs, PART)], pt_s.at[1], pt_r.at[1], beside))
+            for p in (0, 1):
+                ptr[1, p] = ptx[pl.ds(m16(OWN * p + own0), PART), :] + ptr[0, p]
+            go(remote(ptr.at[1, 1 - l], ptr.at[2, 1 - l], pt_s.at[1], pt_r.at[1], beside))
         elif stage == 2:
-            there = ptr.at[2, pl.ds(mine, PART)]
+            there = ptr.at[2, l]
             remote(there, there, pt_s.at[1], pt_r.at[1], beside).wait_recv()
-            ptr[3, half, :] = ptr[1, pl.ds(mine, PART), :] + ptr[2, pl.ds(mine, PART), :]
-            go(remote(ptr.at[3, half], ptr.at[3, half], pt_s.at[2], pt_r.at[2], along["x"]))
+            ptr[3, x] = ptr[1, l] + ptr[2, l]
+            go(remote(ptr.at[3, x], ptr.at[3, x], pt_s.at[2], pt_r.at[2], along["x"]))
         else:
-            there = ptr.at[3, pl.ds(m16(PART * (1 - x)), PART)]
+            there = ptr.at[3, 1 - x]
             remote(there, there, pt_s.at[2], pt_r.at[2], along["x"]).wait_recv()
-            wide = dot_last(ptr[3].astype(bf16), one_hot(lane_of == place_of))
+            every = ptr[3].reshape(OWN, 128).astype(bf16)
+            wide = dot_last(every, one_hot(lane_of == place_of))
             wide = jnp.where(right_patch, wide, 0.0).astype(bf16)
             pts_o[...] = dot_rows(spread, wide) * (1.0 - missing[...].astype(f32))
 
-    operands = ((hc, 0, 768), (att, 0, 768), (dpre, C_IN, 1280), (act, C_OUT, 1280), (dpj, C_QKV, 1024))
+    operands = (
+        ((hc, 0, 0, 512),),
+        ((att, 0, 896, 256), (att, 256, 1536, 256)),
+        ((dpre, 0, C_IN, 640),),
+        ((act, 0, C_OUT, 640),),
+        ((dpj, 0, 512, 512), (dpj, 512, 1152, 512)),
+    )
     steps = (
         g_first, g_own, g_second, g_third, g_done, s_step, features, cot_out, cot_here, tokenize, vectors,
         first_norm, project, turn, attend, second_norm, inner, grad_out, outer_back, grad_in, second_back,
-        attended_back, attend_back, turn_back, finish, grad_qkv, grad_att, grad_bias, first_back, hidden_back,
-        grad_tok, grad_hidden, points_back, ar_begin, ar_mid,
+        attended_back, attend_back, turn_back, finish, grad_qkv, grad_bias, first_back, hidden_back, grad_tok,
+        grad_hidden, points_back, ar_begin, ar_mid, cot_pass, norm_pass, ar_cross, hidden,
     )
     for name, *which in PLAN:
         steps[name](*which)
@@ -1009,17 +1102,17 @@
     hidden = jnp.zeros((8, 128), f32)
     for q in range(4):
         at = slice(160 * q, 160 * q + 160)
-        lead = fb[q, :, 0:384].astype(f32)
+        lead = fb[q, :, 0:256].astype(f32)
         tok_o[:, at] = lead[:, 0:160]
-        att_o[:, at] = lead[:, 160:320]
-        tile = lead[:, 256:384]
+        tile = lead[:, 128:256]
         hidden = hidden + tile[64:72]
         t = jnp.transpose(jnp.concatenate([tile, jnp.zeros((48, 128), f32)], axis=0))
         turned.append(t)
         res_o[8 * q : 8 * q + 8, :] = t[L_RES : L_RES + 8, 0:80]
-        qkv = fb[q, :, 384:896].astype(f32)
+        qkv = fb[q, :, 256:896].astype(f32)
         for j in range(3):
             qkv_o[j, :, at] = qkv[:, 160 * j : 160 * j + 160]
+        att_o[:, at] = qkv[:, 480:640]
         in_o[:, 640 * q : 640 * q + 640] = fb[q, :, 896:1536].astype(f32)
         outw_o[:, 640 * q : 640 * q + 640] = fb[q, :, 1536:2176].astype(f32)
     both = turned[0] + turned[1]
@@ -1035,11 +1128,11 @@
 
 
 def rotary_lanes():
-    lanes = np.arange(1024) % 512
+    lanes = np.arange(512)
     inside = lanes % HEAD_DIM
     turned = lanes < 320
     freqs = 10000.0 ** (-2.0 * (inside % 40) / HEAD_DIM)
-    angles = np.arange(CTXLEN)[:, None] * freqs[None, :]
+    angles = (np.arange(48) % CTXLEN)[:, None] * freqs[None, :]
     cosine = np.where(turned, np.cos(angles), 1.0)
     sine = np.where(turned, np.sin(angles), 0.0)
     lower = np.where(inside < 40, -sine, 0.0)
@@ -1076,47 +1169,54 @@
         scratch_shapes=[
             pltpu.VMEM((D, C_ALL), bf16),
             pltpu.VMEM((D, C_ALL), bf16),
-            pltpu.VMEM((7, 2, 160, C_ONE), bf16),
+            pltpu.VMEM((7, 2, 160, C_MLP), bf16),
+            pltpu.VMEM((3, 2, 160, C_ONE - C_MLP), bf16),
             pltpu.VMEM((TOK, 128), bf16),
+            pltpu.VMEM((BOTH, D), bf16),
+            pltpu.VMEM((BOTH, D), f32),
+            pltpu.VMEM((BOTH, 640), f32),
+            pltpu.VMEM((BOTH, 640), bf16),
+            pltpu.VMEM((BOTH, 640), bf16),
             pltpu.VMEM((TOK, D), bf16),
-            pltpu.VMEM((TOK, D), f32),
-            pltpu.VMEM((TOK, D), f32),
-            pltpu.VMEM((TOK, D), bf16),
-            pltpu.VMEM((TOK, D), bf16),
-            pltpu.VMEM((TOK, D), bf16),
+            pltpu.VMEM((BOTH, D), bf16),
             pltpu.VMEM((TOK, D), bf16),
             pltpu.VMEM((TOK, D), bf16),
             pltpu.VMEM((OWN, D), f32),
             pltpu.VMEM((OWN, D), f32),
-            pltpu.VMEM((TOK, 768), bf16),
-            pltpu.VMEM((TOK, 768), bf16),
-            pltpu.VMEM((TOK, 768), f32),
+            pltpu.VMEM((OWN, D), f32),
+            pltpu.VMEM((TOK, 512), bf16),
+            pltpu.VMEM((TOK, 512), bf16),
+            pltpu.VMEM((TOK, 512), f32),
             pltpu.VMEM((2, TOK, 256), bf16),
-            pltpu.VMEM((2, TOK, 384), bf16),
-            pltpu.VMEM((TOK, 768), bf16),
-            pltpu.VMEM((TOK, 768), bf16),
+            pltpu.VMEM((2, TOK, 256), bf16),
+            pltpu.VMEM((2, TOK, 256), bf16),
+            pltpu.VMEM((TOK, 512), bf16),
+            pltpu.VMEM((TOK, 512), bf16),
             pltpu.VMEM((TOK, 1024), bf16),
-            pltpu.VMEM((1536, 128), f32),
-            pltpu.VMEM((D, 128), f32),
-            pltpu.VMEM((128, 768), f32),
-            pltpu.VMEM((128, 768), f32),
-            pltpu.VMEM((128, 768), bf16),
+            pltpu.VMEM((2, 2, TOK, OWN), f32),
+            pltpu.VMEM((640, 128), f32),
+            pltpu.VMEM((128, 512), f32),
+            pltpu.VMEM((128, 512), f32),
+            pltpu.VMEM((128, 512), bf16),
             pltpu.VMEM((16, D), f32),
-            pltpu.VMEM((8, D), f32),
+            pltpu.VMEM((8, 640), f32),
             pltpu.VMEM((32, D), f32),
             pltpu.VMEM((TOK, 128), f32),
-            pltpu.VMEM((4, OWN, 128), f32),
+            pltpu.VMEM((4, 2, PART, 128), f32),
             pltpu.VMEM((4, HALF, 896), bf16),
             pltpu.VMEM((HALF, 896), f32),
             pltpu.VMEM((HALF, 128), f32),
             pltpu.VMEM((HALF, 384), f32),
-            pltpu.VMEM((2, OWN, D), bf16),
-            pltpu.VMEM((2, OWN, D), bf16),
-            pltpu.VMEM((2, OWN, D), bf16),
-            pltpu.VMEM((3, OWN, D), bf16),
+            pltpu.VMEM((BOTH, D), f32),
+            pltpu.VMEM((2, 2, OWN, D), bf16),
+            pltpu.VMEM((2, 2, OWN, D), bf16),
+            pltpu.VMEM((2, 2, PART, D), bf16),
+            pltpu.VMEM((2, 2, PART, D), bf16),
+            pltpu.VMEM((2, 2, PART, D), bf16),
+            pltpu.VMEM((3, 2, PART, D), bf16),
             sems(chunks, 7), sems(chunks, 7), sems(chunks, 7), sems(chunks, 7),
-            sems(5, 2, TILES), sems(5, 2, TILES),
-            sems(4), sems(4), sems(chunks, 3), sems(chunks, 3), sems(chunks + 1), sems(2, 3), sems(2, 3),
+            sems(5, 3, 2, 2), sems(5, 3, 2, 2),
+            sems(6, 2), sems(6, 2), sems(chunks, 3), sems(chunks, 3), sems(chunks + 1), sems(2, 3), sems(2, 3),
             sems(chunks, 3), sems(chunks, 3), sems(4), sems(4),
         ],
         compiler_params=pltpu.CompilerParams(

time: 220 us -> 196 us (0.89)
  Pallas kernels: 216 us -> 192 us
    pallas_call x1, Pallas kernels: 214 us -> 190 us  [fast_body(): pl.pallas_call(layer_kernel, out_shape=(jax.ShapeDtypeStruct((OWN, D), bf...]
where the time goes in v3:
time: 196 us
  Pallas kernels  192 us (98%)
  local copies, waits for them, and re-layouts  3.12 us (2%)
    pallas_call x1, Pallas kernels, fast_body(): pl.pallas_call(layer_kernel, out_shape=(jax.ShapeDtypeStruct((OWN, D), bf...  190 us

profile of v3, /device:TPU:0, one launch (start us, length us, event | category | flops | bytes accessed | tf_op | source)
XLA Modules:
  0.0 195.7 jit_solution(12301305655639404143)
XLA Ops:
  0.7 190.0 %shard_map.298 = (bf16[192,1280]{1,0:T(8,128)(2,1)}, f32[12,512]{1,0:T(8,128)}, bf16[4,80,2176]{2,1,0:T(8,128)(2,1)}) custom-call(bf16[12,512]{1,0:T(8,128)(2,1)} %points.1, s32[12,512]{1,0:T(8,128)} %missing.1, bf16[40,64]{1,0:T(8,128)(2,1)} %bitcast.18, bf16[1,40]{1,0:T(2,128)(2,1)} %hid_b.1, bf16[80,640]{1,0:T(8,128)(2,1)} %tok_in.1, ...), custom_call_target="tpu_custom_call" | custom-call | flops 12999999488 | bytes 10000000 | tf_op jit(solution)/shard_map/pallas_call | solution.py:1160
  190.6 0.0 copy-start
  190.6 1.3 copy-done
  192.0 0.0 copy-start.1
  192.0 1.0 copy-done.1
  193.0 0.0 copy-start.2
  193.0 0.8 copy-done.2
  193.7 1.9 shard_map.299
Async XLA Ops:
  190.6 1.3 copy-start
  192.0 1.0 copy-start.1
  193.0 0.8 copy-start.2

commit v4 on v3

--- a/solution.py
+++ b/solution.py
@@ -317,33 +317,32 @@
     (2688, 0, 256, 1792),
     (2944, 0, 128, 2048),
 )
-GATHER_ORDER = ("zxy", "zyx", "zxy", "zyx", "zxy", "zy", "zy", "zy", "zy", "zy")
-SUM_ORDER = ("yxz", "xyz", "yxz", "xyz", "yxz", "yz", "yz", "yz", "yz", "yz")
+GATHER_ORDER = ("zxy", "zyx", "zyx", "zyx", "zxy", "zy", "zy", "zy", "zy", "zy")
+SUM_ORDER = ("xyz", "xyz", "yxz", "xyz", "xyz", "yz", "yz", "yz", "yz", "yz")
 (
     FIRST, OWNED, SECOND, THIRD, HERE, SUM, FEATS, COT, COT_HERE, TOKENS, VECTORS, NORM_1, PROJECT, TURN, ATTEND,
     NORM_2, INNER, GRAD_OUT, OUTER, GRAD_IN, BACK_2, D_ATT, ATTEND_B, TURN_B, FINISH, GRAD_QKV, GRAD_BIAS, BACK_1,
     D_HID, GRAD_TOK, GRAD_HID, POINTS, SEND, PASS, COT_PASS, NORM_PASS, CROSS, HIDDEN,
 ) = range(38)
 PLAN = (
-    (FIRST, 0), (FIRST, 4), (FIRST, 2), (FIRST, 1), (OWNED, 0), (FIRST, 3), (OWNED, 1), (FIRST, 7), (OWNED, 3),
-    (FIRST, 5), (OWNED, 4), (SECOND, 0), (FIRST, 8), (SECOND, 1), (OWNED, 2), (FEATS,), (COT,), (THIRD, 1),
-    (THIRD, 0), (SECOND, 4), (SECOND, 3), (SECOND, 2), (HERE, 0), (OWNED, 5), (FIRST, 6), (HERE, 1), (HIDDEN,),
-    (TOKENS, 1), (THIRD, 4), (OWNED, 7), (TOKENS, 0), (FIRST, 9), (SEND, 0, 1), (THIRD, 2), (SEND, 0, 0),
-    (PASS, 0, 1), (THIRD, 3), (OWNED, 6), (SECOND, 5), (PASS, 0, 0), (OWNED, 8), (VECTORS,), (HERE, 3), (HERE, 4),
-    (NORM_1, 1), (SECOND, 7), (HERE, 2), (PROJECT, 1), (TURN, 1), (ATTEND, 1), (SEND, 1, 1), (PASS, 1, 1),
-    (NORM_1, 0), (SECOND, 6), (COT_PASS,), (OWNED, 9), (PROJECT, 0), (TURN, 0), (ATTEND, 0), (SEND, 1, 0), (HERE, 5),
-    (PASS, 1, 0), (SECOND, 8), (NORM_2, 1), (SECOND, 9), (NORM_2, 0), (COT_HERE,), (HERE, 6), (NORM_PASS, 1),
-    (INNER, 0, 1), (HERE, 7), (HERE, 8), (INNER, 1, 1), (HERE, 9), (OUTER, 1), (SEND, 2, 1), (SEND, 3, 1),
-    (NORM_PASS, 0), (CROSS, 2, 1), (INNER, 0, 0), (INNER, 1, 0), (GRAD_OUT, 7), (OUTER, 0), (SEND, 2, 0),
-    (PASS, 2, 1), (CROSS, 2, 0), (CROSS, 3, 1), (GRAD_IN, 5), (SUM, 7), (GRAD_IN, 6), (PASS, 2, 0), (BACK_2, 1),
-    (SEND, 3, 0), (SUM, 5), (D_ATT, 1), (ATTEND_B, 1), (GRAD_OUT, 8), (PASS, 3, 1), (TURN_B, 1), (SEND, 4, 1),
-    (BACK_2, 0), (GRAD_OUT, 9), (GRAD_BIAS,), (CROSS, 3, 0), (D_ATT, 0), (SUM, 6), (PASS, 4, 1), (ATTEND_B, 0),
-    (TURN_B, 0), (SUM, 6), (SUM, 7), (SEND, 4, 0), (GRAD_QKV, 4), (SUM, 5), (PASS, 4, 0), (GRAD_QKV, 3),
-    (GRAD_QKV, 2), (BACK_1, 1), (SUM, 4), (SUM, 8), (SUM, 9), (PASS, 3, 0), (D_HID, 1), (BACK_1, 0), (D_HID, 0),
-    (SUM, 3), (POINTS, 0), (SUM, 2), (SUM, 4), (SUM, 5), (GRAD_TOK,), (SUM, 2), (SUM, 7), (GRAD_HID,), (SUM, 8),
-    (SUM, 4), (POINTS, 1), (SUM, 2), (SUM, 3), (SUM, 4), (SUM, 9), (SUM, 6), (SUM, 3), (SUM, 0), (SUM, 1), (SUM, 0),
-    (SUM, 8), (SUM, 1), (FINISH,), (SUM, 3), (SUM, 0), (SUM, 1), (POINTS, 2), (SUM, 2), (SUM, 0), (SUM, 1), (SUM, 9),
-    (POINTS, 3),
+    (FIRST, 1), (FIRST, 0), (FIRST, 3), (OWNED, 1), (FIRST, 2), (OWNED, 0), (OWNED, 3), (FIRST, 5), (OWNED, 2),
+    (FEATS,), (FIRST, 4), (SECOND, 1), (COT,), (THIRD, 1), (SECOND, 0), (OWNED, 5), (FIRST, 8), (THIRD, 0), (HERE, 1),
+    (FIRST, 6), (SECOND, 3), (OWNED, 4), (HERE, 0), (HIDDEN,), (TOKENS, 1), (SECOND, 2), (FIRST, 7), (OWNED, 8),
+    (TOKENS, 0), (SEND, 0, 1), (THIRD, 3), (OWNED, 6), (PASS, 0, 1), (SEND, 0, 0), (SECOND, 4), (THIRD, 2),
+    (VECTORS,), (THIRD, 4), (PASS, 0, 0), (HERE, 3), (NORM_1, 1), (SECOND, 5), (OWNED, 7), (HERE, 2), (PROJECT, 1),
+    (TURN, 1), (HERE, 4), (ATTEND, 1), (FIRST, 9), (SEND, 1, 1), (PASS, 1, 1), (SECOND, 8), (NORM_1, 0), (SECOND, 6),
+    (COT_PASS, 0), (PROJECT, 0), (OWNED, 9), (TURN, 0), (ATTEND, 0), (SEND, 1, 0), (PASS, 1, 0), (COT_PASS, 1),
+    (NORM_2, 1), (SECOND, 7), (SECOND, 9), (HERE, 6), (COT_HERE,), (NORM_2, 0), (HERE, 5), (INNER, 0, 1),
+    (NORM_PASS, 1), (HERE, 9), (HERE, 7), (HERE, 8), (INNER, 1, 1), (OUTER, 1), (SEND, 2, 1), (INNER, 0, 0),
+    (NORM_PASS, 0), (CROSS, 2, 1), (INNER, 1, 0), (GRAD_OUT, 7), (OUTER, 0), (SEND, 2, 0), (PASS, 2, 1),
+    (CROSS, 2, 0), (SEND, 3, 1), (GRAD_IN, 5), (SUM, 7), (GRAD_IN, 6), (CROSS, 3, 1), (PASS, 2, 0), (BACK_2, 1),
+    (SEND, 3, 0), (D_ATT, 1), (ATTEND_B, 1), (TURN_B, 1), (SEND, 4, 1), (SUM, 5), (CROSS, 3, 0), (PASS, 4, 1),
+    (BACK_2, 0), (GRAD_OUT, 8), (D_ATT, 0), (GRAD_QKV, 4), (ATTEND_B, 0), (SUM, 6), (TURN_B, 0), (SEND, 4, 0),
+    (GRAD_OUT, 9), (PASS, 4, 0), (GRAD_QKV, 3), (SUM, 4), (SUM, 8), (SUM, 8), (BACK_1, 1), (SUM, 7), (GRAD_QKV, 2),
+    (SUM, 9), (SUM, 7), (D_HID, 1), (SUM, 4), (PASS, 3, 0), (BACK_1, 0), (SUM, 5), (GRAD_BIAS,), (SUM, 2), (SUM, 6),
+    (D_HID, 0), (SUM, 3), (POINTS, 0), (GRAD_TOK,), (SUM, 2), (POINTS, 1), (GRAD_HID,), (SUM, 5), (SUM, 2), (FINISH,),
+    (SUM, 3), (SUM, 4), (SUM, 4), (SUM, 0), (SUM, 6), (SUM, 0), (SUM, 0), (SUM, 1), (SUM, 8), (SUM, 1), (SUM, 2),
+    (SUM, 3), (SUM, 9), (SUM, 3), (SUM, 1), (SUM, 0), (POINTS, 2), (SUM, 9), (SUM, 1), (POINTS, 3),
 )
 L_RES, L_ONE, L_VEC, L_BIN, L_HID = 32, 40, 41, 45, 47
 TILE = 256
@@ -366,8 +365,9 @@
     w, g, rb, rbm, fe, cot, part, pre, act, dpre, n1, n2, db, de, x0, x1, x2,
     hc, dpe, pret, q_s, k_s, v_s, att, datt, dpj, ps, gbs, ghs, hidf, hid, vec, bin_s, sums, ptx, ptr,
     pk, pkf, srcf, tmp,
-    part3, cs, cr, ys, yr, xs, xr,
-    ag_s, ag_r, rs_s, rs_r, ar_s, ar_r, nx_s, nx_r, in_s, in_r, lo_s, tk_s, tk_r, fin_s, fin_r, pt_s, pt_r,
+    part3, ob, cs, cr, ys, yr, xs, xr,
+    ag_s, ag_r, rs_s, rs_r, cs_s, cs_r, xs_s, xs_r, ys_s, ys_r, nx_s, nx_r, in_s, in_r, lo_s, tk_s, tk_r,
+    fin_s, fin_r, pt_s, pt_r, keep_s,
 ):
     f32, bf16 = jnp.float32, jnp.bfloat16
     f = lax.axis_index("fsdp")
@@ -398,6 +398,12 @@
     def go(copy):
         copy.start()
         sent.append(copy)
+
+    def came(ref, sem):
+        remote(ref, ref, sem, sem, mate).wait_recv()
+
+    def left(ref, sem):
+        remote(ref, ref, sem, sem, mate).wait_send()
 
     barrier = pltpu.get_barrier_semaphore()
     peers = (mate, beside, corner, along["z"], along["y"], along["x"])
@@ -457,8 +463,8 @@
 
     def g_first(k):
         dst = w.at[pl.ds(m16(HALF * f), HALF), cols(k, x)]
-        for i, (to, member) in enumerate(group):
-            go(remote(piece(k, member), dst, in_s.at[k, i], in_r.at[k, i], to))
+        for to, member in group:
+            remote(piece(k, member), dst, in_s.at[0], in_r.at[k], to).start()
         locals_in[k] = pltpu.make_async_copy(piece(k, m), dst, lo_s.at[k])
         locals_in[k].start()
 
@@ -471,20 +477,22 @@
         h = 1 - x if "x" in flips else x
         return ref.at[pl.ds(2 * zz, 2), yy, :, cols(k, h)]
 
+    wide = sum(1 for chunk in CHUNKS if chunk[3] < C_MLP)
+
+    def g_sem(k, i):
+        return ag_r.at[4 * k + min(i, 3) if k < wide else 4 * wide + 2 * (k - wide) + min(i, 1)]
+
     def g_send(k, i, flips, axis):
         ref = block(w4, k, flips)
-        go(remote(ref, ref, ag_s.at[k, i], ag_r.at[k, i], along[axis]))
+        remote(ref, ref, ag_s.at[0 if k < wide else 1], g_sem(k, i), along[axis]).start()
 
     def g_recv(k, i, flips):
-        ref = block(w4, k, flips)
-        remote(ref, ref, ag_s.at[k, i], ag_r.at[k, i], along[flips[-1]]).wait_recv()
+        came(block(w4, k, flips), g_sem(k, i))
 
     def g_own(k):
         order = GATHER_ORDER[k]
         locals_in[k].wait()
-        for i, (to, member) in enumerate(group):
-            ref = w.at[rows_of(to), cols(k, x)]
-            remote(ref, ref, in_s.at[k, i], in_r.at[k, i], to).wait_recv()
+        came(w.at[0 : 3 * HALF, 0 : CHUNKS[k][2]], in_r.at[k])
         for axis, i in zip(order, (0, 1, 3)):
             g_send(k, i, "", axis)
 
@@ -502,27 +510,24 @@
         g_send(k, 6, a + b, d)
 
     def g_done(k):
-        order = GATHER_ORDER[k]
-        if len(order) == 2:
-            g_recv(k, 1, order[1])
-            g_recv(k, 2, order)
-            return
-        a, b, d = order
-        g_recv(k, 3, d)
-        g_recv(k, 4, a + d)
-        g_recv(k, 5, b + d)
-        g_recv(k, 6, order)
+        _, _, width, at = CHUNKS[k]
+        if k < wide:
+            came(rb.at[0:4, :, :, at : at + width], g_sem(k, 3))
+        else:
+            came(rbm.at[0:2, :, :, at - C_MLP : at - C_MLP + width], g_sem(k, 1))
 
     def s_buf(k, i):
         _, _, width, at = CHUNKS[k]
         return rb.at[i, :, :, at : at + width] if at < C_MLP else rbm.at[i, :, :, at - C_MLP : at - C_MLP + width]
 
+    def s_sem(k, i):
+        return rs_r.at[7 * k + i if k < wide else 7 * wide + 3 * (k - wide) + i]
+
     def s_send(k, i, flips, axis):
-        go(remote(block(g4, k, flips), s_buf(k, i), rs_s.at[k, i], rs_r.at[k, i], along[axis]))
+        remote(block(g4, k, flips), s_buf(k, i), rs_s.at[0 if k < wide else 1], s_sem(k, i), along[axis]).start()
 
     def s_add(k, i, flips, axis):
-        ref = s_buf(k, i)
-        remote(ref, ref, rs_s.at[k, i], rs_r.at[k, i], along[axis]).wait_recv()
+        came(s_buf(k, i), s_sem(k, i))
         _, _, width, at = CHUNKS[k]
         zz = 1 - zh if "z" in flips else zh
         yy = 1 - y if "y" in flips else y
@@ -534,10 +539,10 @@
             here = pl.ds(m16(640 * zz + 320 * half + 160 * yy + inside), 80)
             rows = pl.ds(m16(inside), 80)
             if at < C_MLP:
-                came = rb[i, half, rows, at : at + width]
+                more = rb[i, half, rows, at : at + width]
             else:
-                came = rbm[i, half, rows, at - C_MLP : at - C_MLP + width]
-            g[here, there] = g[here, there] + came
+                more = rbm[i, half, rows, at - C_MLP : at - C_MLP + width]
+            g[here, there] = g[here, there] + more
             return carry
 
         lax.fori_loop(0, 4, step, 0)
@@ -588,10 +593,10 @@
 
     def s_out(k):
         _, _, width, at = CHUNKS[k]
-        for i, (to, member) in enumerate(group):
-            src = g.at[rows_of(to), cols(k, x)]
-            go(remote(src, fb.at[m, :, at : at + width], fin_s.at[k, i], fin_r.at[k, i], to))
-        fb[m, :, at : at + width] = g[pl.ds(m16(HALF * f), HALF), cols(k, x)]
+        dst = fb.at[m, :, at : at + width]
+        for to, member in group:
+            remote(g.at[rows_of(to), cols(k, x)], dst, fin_s.at[0], fin_r.at[0], to).start()
+        pltpu.make_async_copy(g.at[pl.ds(m16(HALF * f), HALF), cols(k, x)], dst, keep_s.at[0]).start()
 
     s_at = {}
 
@@ -607,24 +612,19 @@
 
     def ar_begin(a, p):
         if a >= 2:
-            for i in range(2):
-                done, there = cs_ref(a - 2, p, i)
-                remote(done, there, ar_s.at[a - 2, 0, p, i], ar_r.at[a - 2, 0, p, i], mate).wait_send()
+            left(cs.at[a % 2, p, 0 : OWN if a == 4 else PART, :], cs_s.at[a - 2, p])
         for i in range(2):
             for n, first in enumerate((0, TOK) if a in (2, 3) else (0,)):
                 rows = slice(first + OWN * p, first + OWN * p + OWN)
                 value = None
-                for left, lo, col, width in operands[a]:
-                    more = dot_last(left[rows, lo : lo + width], w[ar_tile(i), col : col + width])
+                for ref, lo, col, width in operands[a]:
+                    more = dot_last(ref[rows, lo : lo + width], w[ar_tile(i), col : col + width])
                     value = more if value is None else value + more
                 total(a)[rows, ar_tile(i)] = value
                 away = pl.ds(m16(first + OWN * p + oth0), PART)
                 cs[a % 2, p, PART * n : PART * n + PART, ar_tile(i)] = total(a)[away, ar_tile(i)].astype(bf16)
             src, there = cs_ref(a, p, i)
-            copy = remote(src, there, ar_s.at[a, 0, p, i], ar_r.at[a, 0, p, i], mate)
-            copy.start()
-            if a >= 3:
-                sent.append(copy)
+            remote(src, there, cs_s.at[a, p], cs_r.at[a, p, i], mate).start()
 
     def ar_cross(a, p):
         b = a - 2
@@ -632,47 +632,50 @@
         far = pl.ds(m16(TOK * (1 - x) + OWN * p + own0), PART)
         for i in range(2):
             _, here = cs_ref(a, p, i)
-            remote(here, here, ar_s.at[a, 0, p, i], ar_r.at[a, 0, p, i], mate).wait_recv()
-            came = cr[a % 2, p, pl.ds(m16(PART * (1 - x)), PART), ar_tile(i)].astype(f32)
-            ys[b, p, :, ar_tile(i)] = (total(a)[far, ar_tile(i)] + came).astype(bf16)
-            go(remote(
-                ys.at[b, p, :, ar_tile(i)], yr.at[b, p, :, ar_tile(i)], ar_s.at[a, 2, p, i], ar_r.at[a, 2, p, i],
-                along["x"],
-            ))
+            came(here, cs_r.at[a, p, i])
+            more = cr[a % 2, p, pl.ds(m16(PART * (1 - x)), PART), ar_tile(i)].astype(f32)
+            ys[b, p, :, ar_tile(i)] = (total(a)[far, ar_tile(i)] + more).astype(bf16)
+            remote(
+                ys.at[b, p, :, ar_tile(i)], yr.at[b, p, :, ar_tile(i)], ys_s.at[0], ys_r.at[b, p, i], along["x"]
+            ).start()
             total(a)[near, ar_tile(i)] = total(a)[near, ar_tile(i)] + cr[
                 a % 2, p, pl.ds(m16(PART * x), PART), ar_tile(i)
             ].astype(f32)
 
+    def fold_out():
+        for p in (0, 1):
+            left(xs.at[1, p], xs_s.at[1, p])
+        for i in range(2):
+            for p in (0, 1):
+                came(yr.at[1, p, :, ar_tile(i)], ys_r.at[1, p, i])
+            mine = part3[pl.ds(m16(TOK * x + OWN * (1 - l) + own0), PART), ar_tile(i)]
+            xs[1, 0, :, ar_tile(i)] = (mine + yr[1, 1 - l, :, ar_tile(i)].astype(f32)).astype(bf16)
+            remote(
+                xs.at[1, 0, :, ar_tile(i)], xr.at[0, 0, :, ar_tile(i)], xs_s.at[3, 0], xs_r.at[3, 0], beside
+            ).start()
+
     def ar_mid(a, p):
+        if a == 3:
+            return fold_out()
         b = a % 2
         if a >= 2:
-            for i in range(2):
-                done = xs.at[b, p, :, ar_tile(i)]
-                remote(done, done, ar_s.at[a - 2, 1, p, i], ar_r.at[a - 2, 1, p, i], beside).wait_send()
+            left(xs.at[b, p], xs_s.at[a - 2, p])
         for i in range(2):
-            if a in (2, 3):
-                here = yr.at[a - 2, p, :, ar_tile(i)]
-                remote(here, here, ar_s.at[a, 2, p, i], ar_r.at[a, 2, p, i], along["x"]).wait_recv()
-                mine = total(a)[pl.ds(m16(TOK * x + OWN * p + own0), PART), ar_tile(i)]
-                came = yr[a - 2, p, :, ar_tile(i)]
+            if a == 2:
+                came(yr.at[0, p, :, ar_tile(i)], ys_r.at[0, p, i])
+                mine = part[pl.ds(m16(TOK * x + OWN * p + own0), PART), ar_tile(i)]
+                more = yr[0, p, :, ar_tile(i)]
             else:
-                _, here = cs_ref(a, p, i)
-                remote(here, here, ar_s.at[a, 0, p, i], ar_r.at[a, 0, p, i], mate).wait_recv()
+                came(cs_ref(a, p, i)[1], cs_r.at[a, p, i])
                 mine = part[pl.ds(m16(OWN * p + own0), PART), ar_tile(i)]
-                came = cr[b, p, 0:PART, ar_tile(i)]
-            xs[b, p, :, ar_tile(i)] = (mine + came.astype(f32)).astype(bf16)
-            copy = remote(
-                xs.at[b, p, :, ar_tile(i)], xr.at[a % 3, p, :, ar_tile(i)], ar_s.at[a, 1, p, i], ar_r.at[a, 1, p, i],
-                beside,
-            )
-            copy.start()
-            if a >= 3:
-                sent.append(copy)
+                more = cr[b, p, 0:PART, ar_tile(i)]
+            xs[b, p, :, ar_tile(i)] = (mine + more.astype(f32)).astype(bf16)
+            remote(
+                xs.at[b, p, :, ar_tile(i)], xr.at[a % 3, p, :, ar_tile(i)], xs_s.at[a, p], xs_r.at[a, p], beside
+            ).start()
 
     def ar_end(a, p):
-        for i in range(2):
-            here = xr.at[a % 3, p, :, ar_tile(i)]
-            remote(here, here, ar_s.at[a, 1, p, i], ar_r.at[a, 1, p, i], beside).wait_recv()
+        came(xr.at[a % 3, p], xs_r.at[a, p])
 
     def summed(a, p, rows):
         return xs[a % 2, p, rows, :].astype(f32) + xr[a % 3, p, rows, :].astype(f32)
@@ -689,11 +692,10 @@
 
     def share(j, p, ref, first=0, to=None):
         rows = ref.at[pl.ds(m16(first + OWN * p + own0), PART)]
-        go(remote(rows, rows, nx_s.at[j, p], nx_r.at[j, p], mate if to is None else to))
-
-    def shared(j, p, ref, first=0, start=None, to=None):
-        rows = ref.at[pl.ds(m16(first + OWN * p + (oth0 if start is None else start)), PART)]
-        remote(rows, rows, nx_s.at[j, p], nx_r.at[j, p], mate if to is None else to).wait_recv()
+        remote(rows, rows, nx_s.at[0], nx_r.at[j, p], mate if to is None else to).start()
+
+    def shared(j, p, ref, first=0, start=None):
+        came(ref.at[pl.ds(m16(first + OWN * p + (oth0 if start is None else start)), PART)], nx_r.at[j, p])
 
     def rms(v):
         return lax.rsqrt(jnp.mean(v * v, axis=-1, keepdims=True) + 1e-06)
@@ -734,27 +736,34 @@
         feats = feats + dot_plain(jnp.where(right_patch, gone, 0.0).astype(bf16), one_hot(lane_of == place_of + PL))
         ptx[0:OWN, :] = jnp.where(iota((OWN, 128), 1) == 2 * PL, 1.0, feats)
         fe[pl.ds(mine0, PART), :] = ptx[pl.ds(m16(PART * x), PART), :].astype(bf16)
-        for i, (to, member) in enumerate(group):
+        for to, member in group:
             rows = fe.at[pl.ds(mine0, PART)]
-            go(remote(rows, rows, tk_s.at[0, i], tk_r.at[0, i], to))
+            remote(rows, rows, tk_s.at[0], tk_r.at[0], to).start()
         sums[...] = jnp.zeros(sums.shape, f32)
         hidf[...] = jnp.zeros(hidf.shape, f32)
 
     def cot_out():
         cot_copy.start()
-        for i, to in enumerate((mate, beside)):
-            go(remote(cot_part, cot_rows.at[:, pl.ds(mine0, PART)], tk_s.at[1, i], tk_r.at[1, i], to))
-
-    def cot_pass():
-        rows = cot_rows.at[:, pl.ds(m16(OWN * (1 - l) + own0), PART)]
-        remote(rows, rows, tk_s.at[1, 1], tk_r.at[1, 1], beside).wait_recv()
-        go(remote(rows, rows, tk_s.at[1, 2], tk_r.at[1, 2], mate))
+        dst = cot_rows.at[:, pl.ds(mine0, PART)]
+        remote(cot_part, dst, tk_s.at[1], tk_r.at[1], mate).start()
+        remote(cot_part.at[x], cot_rows.at[x, pl.ds(mine0, PART)], tk_s.at[1], tk_r.at[2], beside).start()
+
+    def cot_pass(stage):
+        here = pl.ds(m16(OWN * (1 - l) + own0), PART)
+        near, far = cot_rows.at[x, here], cot_rows.at[1 - x, here]
+        if stage == 0:
+            came(near, tk_r.at[2])
+            remote(near, near, tk_s.at[1], tk_r.at[3], along["x"]).start()
+            remote(near, near, tk_s.at[1], tk_r.at[4], mate).start()
+        else:
+            came(far, tk_r.at[3])
+            remote(far, far, tk_s.at[1], tk_r.at[5], mate).start()
 
     def cot_here():
         cot_copy.wait()
-        for i, ll in ((0, l), (2, 1 - l)):
-            rows = cot_rows.at[:, pl.ds(m16(OWN * ll + oth0), PART)]
-            remote(rows, rows, tk_s.at[1, i], tk_r.at[1, i], mate).wait_recv()
+        came(cot_rows.at[:, pl.ds(m16(OWN * l + oth0), PART)], tk_r.at[1])
+        for i, xx in ((4, x), (5, 1 - x)):
+            came(cot_rows.at[xx, pl.ds(m16(OWN * (1 - l) + oth0), PART)], tk_r.at[i])
 
     def hidden():
         for h in (0, 1):
@@ -767,11 +776,7 @@
             chosen = (lane >= L_RES) & (lane < L_RES + 8) & (row == PL * h + 8 * m + lane - L_RES)
             hidf[:, slab(h)] = jnp.where(chosen, 1.0, hidf[:, slab(h)])
         hid[...] = hidf[...].astype(bf16)
-        for i, (to, member) in enumerate(group):
-            cc = 1 - c if i != 1 else c
-            ll = l if i == 0 else 1 - l
-            rows = fe.at[pl.ds(m16(OWN * ll + PART * cc), PART)]
-            remote(rows, rows, tk_s.at[0, i], tk_r.at[0, i], to).wait_recv()
+        came(fe.at[0 : 3 * PART], tk_r.at[0])
 
     def tokenize(p):
         v = dot_plain(fe[part_rows(p), :], hid[...])
@@ -864,9 +869,9 @@
 
     def norm_pass(p):
         far = TOK * (1 - x)
-        shared(1, p, n2, far, own0, along["x"])
+        shared(1, p, n2, far, own0)
         rows = n2.at[pl.ds(m16(far + OWN * p + own0), PART)]
-        go(remote(rows, rows, nx_s.at[5, p], nx_r.at[5, p], mate))
+        remote(rows, rows, nx_s.at[0], nx_r.at[5, p], mate).start()
 
     def inner(which, p):
         first = TOK * (x if which == 0 else 1 - x)
@@ -944,16 +949,17 @@
 
     def finish():
         ar_end(3, 0)
-        ar_end(3, 1)
 
         def body(start):
             rows = pl.ds(start, 32)
-            v = xs[1, l, rows, :].astype(f32) + xr[0, l, rows, :].astype(f32)
-            out_o[at32(PART * x + start), :] = (x1[at32(PART * l + start), :] + v + vec[2:3, :]).astype(bf16)
+            v = part3[at32(TOK * x + OWN * l + own0 + start), :] + yr[1, l, rows, :].astype(f32)
+            v = v + xr[0, 0, rows, :].astype(f32)
+            ob[rows, :] = (x1[at32(PART * l + start), :] + v + vec[2:3, :]).astype(bf16)
 
         own_rows(body)
         ref = out_o.at[pl.ds(m16(PART * x), PART)]
-        go(remote(ref, ref, pt_s.at[3], pt_r.at[3], along["x"]))
+        go(remote(ob, ref, pt_s.at[3], pt_r.at[3], along["x"]))
+        pltpu.make_async_copy(ob, ref, keep_s.at[1]).start()
 
     def grad_mlp(k, left, right, base):
         first, _, width, _ = CHUNKS[k]
@@ -1081,26 +1087,39 @@
     for name, *which in PLAN:
         steps[name](*which)
 
-    there = out_o.at[pl.ds(m16(PART * (1 - x)), PART)]
-    remote(there, there, pt_s.at[3], pt_r.at[3], along["x"]).wait_recv()
-    for k, (_, _, width, at) in enumerate(CHUNKS):
-        for i, (to, member) in enumerate(group):
-            there = fb.at[member, :, at : at + width]
-            remote(there, there, fin_s.at[k, i], fin_r.at[k, i], to).wait_recv()
+    came(out_o.at[pl.ds(m16(PART * (1 - x)), PART)], pt_r.at[3])
+    came(fb.at[0:3], fin_r.at[0])
+    pltpu.make_async_copy(g.at[0:HALF, 0:C_ONE], fb.at[m], keep_s.at[0]).wait()
+    pltpu.make_async_copy(ob, out_o.at[pl.ds(m16(PART * x), PART)], keep_s.at[1]).wait()
+    for ref, sem in (
+        (rb, ag_s.at[0]), (rbm, ag_s.at[1]), (rb, rs_s.at[0]), (rbm, rs_s.at[1]),
+        (w.at[0 : 3 * HALF, 0:C_ONE], in_s.at[0]), (g.at[0 : 3 * HALF, 0:C_ONE], fin_s.at[0]),
+        (cs.at[1, 0], cs_s.at[3, 0]), (cs.at[1, 1], cs_s.at[3, 1]),
+        (cs.at[0, 0, 0:PART], cs_s.at[4, 0]), (cs.at[0, 1, 0:PART], cs_s.at[4, 1]),
+        (xs.at[1, 0], xs_s.at[3, 0]), (xs.at[0, 0], xs_s.at[4, 0]), (xs.at[0, 1], xs_s.at[4, 1]),
+        (ys, ys_s.at[0]), (w.at[0 : 12 * PART, 0:D], nx_s.at[0]),
+        (fe.at[0 : 3 * PART], tk_s.at[0]), (cot.at[0 : 6 * PART], tk_s.at[1]),
+    ):
+        left(ref, sem)
     for copy in sent:
         copy.wait_send()
 
 
 def unpack_kernel(
-    out_i, pts_i, fb,
+    out_i, pts_i, fb_i,
     out_o, pts_o, hw_o, hb_o, tok_o, res_o, tokb_o, gain1_o, qkv_o, att_o, gain2_o, in_o, inb_o, outw_o, outb_o,
+    fb, sem,
 ):
     f32 = jnp.float32
-    out_o[...] = out_i[...]
+    copies = [pltpu.make_async_copy(fb_i.at[q], fb.at[q], sem.at[q]) for q in range(4)]
+    copies.append(pltpu.make_async_copy(out_i, out_o, sem.at[4]))
+    for copy in copies:
+        copy.start()
     pts_o[...] = pts_i[...]
     turned = []
     hidden = jnp.zeros((8, 128), f32)
     for q in range(4):
+        copies[q].wait()
         at = slice(160 * q, 160 * q + 160)
         lead = fb[q, :, 0:256].astype(f32)
         tok_o[:, at] = lead[:, 0:160]
@@ -1125,6 +1144,7 @@
     inb_o[:, 80:160] = every[L_BIN + 1 : L_BIN + 2, 0:80]
     hw_o[...] = every[L_HID : L_HID + 40, 0:64]
     hb_o[...] = hidden[0:1, L_HID : L_HID + 40]
+    copies[4].wait()
 
 
 def rotary_lanes():
@@ -1155,6 +1175,7 @@
         return jax.ShapeDtypeStruct(shape, f32)
 
     chunks = len(CHUNKS)
+    wide = sum(1 for chunk in CHUNKS if chunk[3] < C_MLP)
     specs = [vmem] * 19
     specs[11] = specs[13] = specs[15] = any_space
     out, pts, packed = pl.pallas_call(
@@ -1165,7 +1186,7 @@
             jax.ShapeDtypeStruct((4, HALF, C_ONE), bf16),
         ),
         in_specs=specs,
-        out_specs=[vmem] * 3,
+        out_specs=[any_space, vmem, any_space],
         scratch_shapes=[
             pltpu.VMEM((D, C_ALL), bf16),
             pltpu.VMEM((D, C_ALL), bf16),
@@ -1208,16 +1229,17 @@
             pltpu.VMEM((HALF, 128), f32),
             pltpu.VMEM((HALF, 384), f32),
             pltpu.VMEM((BOTH, D), f32),
+            pltpu.VMEM((PART, D), bf16),
             pltpu.VMEM((2, 2, OWN, D), bf16),
             pltpu.VMEM((2, 2, OWN, D), bf16),
             pltpu.VMEM((2, 2, PART, D), bf16),
             pltpu.VMEM((2, 2, PART, D), bf16),
             pltpu.VMEM((2, 2, PART, D), bf16),
             pltpu.VMEM((3, 2, PART, D), bf16),
-            sems(chunks, 7), sems(chunks, 7), sems(chunks, 7), sems(chunks, 7),
-            sems(5, 3, 2, 2), sems(5, 3, 2, 2),
-            sems(6, 2), sems(6, 2), sems(chunks, 3), sems(chunks, 3), sems(chunks + 1), sems(2, 3), sems(2, 3),
-            sems(chunks, 3), sems(chunks, 3), sems(4), sems(4),
+            sems(2), sems(4 * wide + 2 * (chunks - wide)), sems(2), sems(7 * wide + 3 * (chunks - wide)),
+            sems(5, 2), sems(5, 2, 2), sems(5, 2), sems(5, 2), sems(1), sems(2, 2, 2),
+            sems(1), sems(6, 2), sems(1), sems(chunks), sems(chunks + 1), sems(2), sems(6),
+            sems(1), sems(1), sems(4), sems(4), sems(2),
         ],
         compiler_params=pltpu.CompilerParams(
             collective_id=0, has_side_effects=True, vmem_limit_bytes=64 * 1024 * 1024 - 512 * 1024
@@ -1239,8 +1261,9 @@
             like(3, HALF, 640), like(HALF, 640), like(1, HALF), like(HALF, 2560), like(1, 160), like(HALF, 2560),
             like(1, HALF),
         ),
-        in_specs=[vmem] * 3,
-        out_specs=[vmem] * 15,
+        in_specs=[any_space, vmem, any_space],
+        out_specs=[any_space] + [vmem] * 14,
+        scratch_shapes=[pltpu.VMEM((4, HALF, C_ONE), bf16), sems(5)],
         compiler_params=pltpu.CompilerParams(vmem_limit_bytes=32 * 1024 * 1024),
     )(out, pts, packed)
     return (

time: 196 us -> 180 us (0.918)
  Pallas kernels: 192 us -> 176 us
    pallas_call x1, Pallas kernels: 190 us -> 173 us  [fast_body(): pl.pallas_call(layer_kernel, out_shape=(jax.ShapeDtypeStruct((OWN, D), bf...]
where the time goes in v4:
time: 180 us
  Pallas kernels  176 us (98%)
  local copies, waits for them, and re-layouts  3.12 us (2%)
    pallas_call x1, Pallas kernels, fast_body(): pl.pallas_call(layer_kernel, out_shape=(jax.ShapeDtypeStruct((OWN, D), bf...  173 us

profile of v4, /device:TPU:0, one launch (start us, length us, event | category | flops | bytes accessed | tf_op | source)
XLA Modules:
  0.0 179.6 jit_solution(18260991548682502863)
XLA Ops:
  0.7 172.8 %shard_map.298 = (bf16[192,1280]{1,0:T(8,128)(2,1)}, f32[12,512]{1,0:T(8,128)}, bf16[4,80,2176]{2,1,0:T(8,128)(2,1)}) custom-call(bf16[12,512]{1,0:T(8,128)(2,1)} %points.1, s32[12,512]{1,0:T(8,128)} %missing.1, bf16[40,64]{1,0:T(8,128)(2,1)} %bitcast.18, bf16[1,40]{1,0:T(2,128)(2,1)} %hid_b.1, bf16[80,640]{1,0:T(8,128)(2,1)} %tok_in.1, ...), custom_call_target="tpu_custom_call" | custom-call | flops 12999999488 | bytes 10000000 | tf_op jit(solution)/shard_map/pallas_call | solution.py:1181
  173.4 0.0 copy-start
  173.4 1.3 copy-done
  174.8 0.0 copy-start.1
  174.8 1.0 copy-done.1
  175.8 0.0 copy-start.2
  175.8 0.8 copy-done.2
  176.5 2.9 %shard_map.299 = (bf16[192,1280]{1,0:T(8,128)(2,1)}, f32[12,512]{1,0:T(8,128)}, f32[40,64]{1,0:T(8,128)}, f32[1,40]{1,0:T(1,128)}, f32[80,640]{1,0:T(8,128)}, /*...) custom-call(bf16[192,1280]{1,0:T(8,128)(2,1)S(1)} %copy-done.1, ...), custom_call_target="tpu_custom_call" | custom-call | tf_op jit(solution)/shard_map/pallas_call | solution.py:1256
Async XLA Ops:
  173.4 1.3 copy-start
  174.8 1.0 copy-start.1
  175.8 0.8 copy-start.2

commit v5 on v4

--- a/solution.py
+++ b/solution.py
@@ -325,24 +325,24 @@
     D_HID, GRAD_TOK, GRAD_HID, POINTS, SEND, PASS, COT_PASS, NORM_PASS, CROSS, HIDDEN,
 ) = range(38)
 PLAN = (
-    (FIRST, 1), (FIRST, 0), (FIRST, 3), (OWNED, 1), (FIRST, 2), (OWNED, 0), (OWNED, 3), (FIRST, 5), (OWNED, 2),
-    (FEATS,), (FIRST, 4), (SECOND, 1), (COT,), (THIRD, 1), (SECOND, 0), (OWNED, 5), (FIRST, 8), (THIRD, 0), (HERE, 1),
-    (FIRST, 6), (SECOND, 3), (OWNED, 4), (HERE, 0), (HIDDEN,), (TOKENS, 1), (SECOND, 2), (FIRST, 7), (OWNED, 8),
-    (TOKENS, 0), (SEND, 0, 1), (THIRD, 3), (OWNED, 6), (PASS, 0, 1), (SEND, 0, 0), (SECOND, 4), (THIRD, 2),
-    (VECTORS,), (THIRD, 4), (PASS, 0, 0), (HERE, 3), (NORM_1, 1), (SECOND, 5), (OWNED, 7), (HERE, 2), (PROJECT, 1),
-    (TURN, 1), (HERE, 4), (ATTEND, 1), (FIRST, 9), (SEND, 1, 1), (PASS, 1, 1), (SECOND, 8), (NORM_1, 0), (SECOND, 6),
-    (COT_PASS, 0), (PROJECT, 0), (OWNED, 9), (TURN, 0), (ATTEND, 0), (SEND, 1, 0), (PASS, 1, 0), (COT_PASS, 1),
-    (NORM_2, 1), (SECOND, 7), (SECOND, 9), (HERE, 6), (COT_HERE,), (NORM_2, 0), (HERE, 5), (INNER, 0, 1),
-    (NORM_PASS, 1), (HERE, 9), (HERE, 7), (HERE, 8), (INNER, 1, 1), (OUTER, 1), (SEND, 2, 1), (INNER, 0, 0),
-    (NORM_PASS, 0), (CROSS, 2, 1), (INNER, 1, 0), (GRAD_OUT, 7), (OUTER, 0), (SEND, 2, 0), (PASS, 2, 1),
-    (CROSS, 2, 0), (SEND, 3, 1), (GRAD_IN, 5), (SUM, 7), (GRAD_IN, 6), (CROSS, 3, 1), (PASS, 2, 0), (BACK_2, 1),
-    (SEND, 3, 0), (D_ATT, 1), (ATTEND_B, 1), (TURN_B, 1), (SEND, 4, 1), (SUM, 5), (CROSS, 3, 0), (PASS, 4, 1),
-    (BACK_2, 0), (GRAD_OUT, 8), (D_ATT, 0), (GRAD_QKV, 4), (ATTEND_B, 0), (SUM, 6), (TURN_B, 0), (SEND, 4, 0),
-    (GRAD_OUT, 9), (PASS, 4, 0), (GRAD_QKV, 3), (SUM, 4), (SUM, 8), (SUM, 8), (BACK_1, 1), (SUM, 7), (GRAD_QKV, 2),
-    (SUM, 9), (SUM, 7), (D_HID, 1), (SUM, 4), (PASS, 3, 0), (BACK_1, 0), (SUM, 5), (GRAD_BIAS,), (SUM, 2), (SUM, 6),
-    (D_HID, 0), (SUM, 3), (POINTS, 0), (GRAD_TOK,), (SUM, 2), (POINTS, 1), (GRAD_HID,), (SUM, 5), (SUM, 2), (FINISH,),
-    (SUM, 3), (SUM, 4), (SUM, 4), (SUM, 0), (SUM, 6), (SUM, 0), (SUM, 0), (SUM, 1), (SUM, 8), (SUM, 1), (SUM, 2),
-    (SUM, 3), (SUM, 9), (SUM, 3), (SUM, 1), (SUM, 0), (POINTS, 2), (SUM, 9), (SUM, 1), (POINTS, 3),
+    (FIRST, 0), (FIRST, 1), (FIRST, 4), (FIRST, 9), (FIRST, 3), (OWNED, 0), (OWNED, 1), (FIRST, 8), (OWNED, 4),
+    (FIRST, 2), (FEATS,), (FIRST, 7), (FIRST, 5), (OWNED, 9), (OWNED, 3), (SECOND, 0), (FIRST, 6), (SECOND, 1),
+    (THIRD, 0), (THIRD, 1), (OWNED, 2), (OWNED, 7), (HERE, 1), (HERE, 0), (HIDDEN,), (TOKENS, 1), (SEND, 0, 1),
+    (SECOND, 4), (TOKENS, 0), (PASS, 0, 1), (SECOND, 3), (SEND, 0, 0), (OWNED, 5), (THIRD, 3), (PASS, 0, 0),
+    (SECOND, 2), (OWNED, 6), (COT,), (THIRD, 2), (VECTORS,), (HERE, 3), (NORM_1, 1), (THIRD, 4), (NORM_1, 0),
+    (HERE, 4), (HERE, 2), (PROJECT, 1), (SECOND, 5), (OWNED, 8), (PROJECT, 0), (TURN, 1), (SECOND, 7), (ATTEND, 1),
+    (SEND, 1, 1), (PASS, 1, 1), (TURN, 0), (ATTEND, 0), (SEND, 1, 0), (COT_PASS, 0), (PASS, 1, 0), (SECOND, 6),
+    (SECOND, 8), (NORM_2, 1), (SECOND, 9), (COT_PASS, 1), (NORM_2, 0), (HERE, 6), (COT_HERE,), (HERE, 7),
+    (NORM_PASS, 1), (HERE, 5), (INNER, 0, 0), (HERE, 9), (HERE, 8), (INNER, 0, 1), (INNER, 1, 1), (OUTER, 1),
+    (SEND, 2, 1), (NORM_PASS, 0), (CROSS, 2, 1), (INNER, 1, 0), (GRAD_OUT, 9), (OUTER, 0), (GRAD_IN, 6), (SEND, 2, 0),
+    (PASS, 2, 1), (SUM, 9), (CROSS, 2, 0), (SEND, 3, 1), (SEND, 3, 0), (GRAD_OUT, 7), (GRAD_OUT, 8), (PASS, 2, 0),
+    (BACK_2, 1), (SUM, 6), (CROSS, 3, 0), (CROSS, 3, 1), (D_ATT, 1), (ATTEND_B, 1), (TURN_B, 1), (SEND, 4, 1),
+    (SUM, 7), (PASS, 4, 1), (BACK_2, 0), (GRAD_IN, 5), (D_ATT, 0), (GRAD_QKV, 4), (ATTEND_B, 0), (TURN_B, 0),
+    (SEND, 4, 0), (GRAD_BIAS,), (PASS, 4, 0), (GRAD_QKV, 3), (SUM, 4), (SUM, 5), (GRAD_QKV, 2), (BACK_1, 1), (SUM, 5),
+    (SUM, 8), (PASS, 3, 0), (BACK_1, 0), (SUM, 6), (SUM, 4), (D_HID, 0), (D_HID, 1), (SUM, 6), (SUM, 3), (SUM, 2),
+    (SUM, 4), (SUM, 8), (GRAD_TOK,), (SUM, 2), (SUM, 9), (SUM, 8), (GRAD_HID,), (SUM, 7), (SUM, 7), (SUM, 2),
+    (SUM, 3), (SUM, 4), (SUM, 0), (POINTS, 0), (FINISH,), (SUM, 3), (POINTS, 1), (SUM, 0), (SUM, 2), (SUM, 1),
+    (SUM, 1), (SUM, 3), (SUM, 0), (SUM, 0), (SUM, 5), (SUM, 1), (POINTS, 2), (SUM, 1), (SUM, 9), (POINTS, 3),
 )
 L_RES, L_ONE, L_VEC, L_BIN, L_HID = 32, 40, 41, 45, 47
 TILE = 256
@@ -365,7 +365,7 @@
     w, g, rb, rbm, fe, cot, part, pre, act, dpre, n1, n2, db, de, x0, x1, x2,
     hc, dpe, pret, q_s, k_s, v_s, att, datt, dpj, ps, gbs, ghs, hidf, hid, vec, bin_s, sums, ptx, ptr,
     pk, pkf, srcf, tmp,
-    part3, ob, cs, cr, ys, yr, xs, xr,
+    part3, ob, pts_v, cs, cr, ys, yr, xs, xr,
     ag_s, ag_r, rs_s, rs_r, cs_s, cs_r, xs_s, xs_r, ys_s, ys_r, nx_s, nx_r, in_s, in_r, lo_s, tk_s, tk_r,
     fin_s, fin_r, pt_s, pt_r, keep_s,
 ):
@@ -979,18 +979,25 @@
 
     def grad_qkv(k):
         first, apart, width, _ = CHUNKS[k]
+        lo, hi = first - C_QKV, first - C_QKV + width
+        mid, cut = min(hi, 512), max(lo, 384)
 
         def body(rows, i):
             for h in (0, 1):
-                for lo in range(first - C_QKV, first - C_QKV + width, 128):
-                    value = None
-                    if lo < 512:
-                        value = dot_rows(n1[:, rows], dpj[:, 512 * h + lo : 512 * h + lo + 128])
-                    if lo >= 384:
-                        more = dot_rows(db[:, rows], att[:, 256 * h + lo - 384 : 256 * h + lo - 256])
-                        value = more if value is None else value + more
-                    col = C_QKV + apart * h + lo
-                    g[rows, col : col + 128] = value.astype(bf16)
+                col = C_QKV + apart * h
+                if lo < mid:
+                    value = dot_rows(n1[:, rows], dpj[:, 512 * h + lo : 512 * h + mid])
+                    if cut >= mid:
+                        g[rows, col + lo : col + mid] = value.astype(bf16)
+                    else:
+                        more = dot_rows(db[:, rows], att[:, 256 * h + cut - 384 : 256 * h + mid - 384])
+                        if cut > lo:
+                            g[rows, col + lo : col + cut] = value[:, 0 : cut - lo].astype(bf16)
+                        g[rows, col + cut : col + mid] = (value[:, cut - lo :] + more).astype(bf16)
+                if hi > 512:
+                    start = max(lo, 512)
+                    value = dot_rows(db[:, rows], att[:, 256 * h + start - 384 : 256 * h + hi - 384])
+                    g[rows, col + start : col + hi] = value.astype(bf16)
 
         tiles_loop(TILES, body)
         s_start(k)
@@ -1069,7 +1076,8 @@
             every = ptr[3].reshape(OWN, 128).astype(bf16)
             wide = dot_last(every, one_hot(lane_of == place_of))
             wide = jnp.where(right_patch, wide, 0.0).astype(bf16)
-            pts_o[...] = dot_rows(spread, wide) * (1.0 - missing[...].astype(f32))
+            pts_v[...] = dot_rows(spread, wide) * (1.0 - missing[...].astype(f32))
+            pltpu.make_async_copy(pts_v, pts_o, keep_s.at[2]).start()
 
     operands = (
         ((hc, 0, 0, 512),),
@@ -1091,6 +1099,7 @@
     came(fb.at[0:3], fin_r.at[0])
     pltpu.make_async_copy(g.at[0:HALF, 0:C_ONE], fb.at[m], keep_s.at[0]).wait()
     pltpu.make_async_copy(ob, out_o.at[pl.ds(m16(PART * x), PART)], keep_s.at[1]).wait()
+    pltpu.make_async_copy(pts_v, pts_o, keep_s.at[2]).wait()
     for ref, sem in (
         (rb, ag_s.at[0]), (rbm, ag_s.at[1]), (rb, rs_s.at[0]), (rbm, rs_s.at[1]),
         (w.at[0 : 3 * HALF, 0:C_ONE], in_s.at[0]), (g.at[0 : 3 * HALF, 0:C_ONE], fin_s.at[0]),
@@ -1186,7 +1195,7 @@
             jax.ShapeDtypeStruct((4, HALF, C_ONE), bf16),
         ),
         in_specs=specs,
-        out_specs=[any_space, vmem, any_space],
+        out_specs=[any_space] * 3,
         scratch_shapes=[
             pltpu.VMEM((D, C_ALL), bf16),
             pltpu.VMEM((D, C_ALL), bf16),
@@ -1230,6 +1239,7 @@
             pltpu.VMEM((HALF, 384), f32),
             pltpu.VMEM((BOTH, D), f32),
             pltpu.VMEM((PART, D), bf16),
+            pltpu.VMEM((12, 512), f32),
             pltpu.VMEM((2, 2, OWN, D), bf16),
             pltpu.VMEM((2, 2, OWN, D), bf16),
             pltpu.VMEM((2, 2, PART, D), bf16),
@@ -1239,7 +1249,7 @@
             sems(2), sems(4 * wide + 2 * (chunks - wide)), sems(2), sems(7 * wide + 3 * (chunks - wide)),
             sems(5, 2), sems(5, 2, 2), sems(5, 2), sems(5, 2), sems(1), sems(2, 2, 2),
             sems(1), sems(6, 2), sems(1), sems(chunks), sems(chunks + 1), sems(2), sems(6),
-            sems(1), sems(1), sems(4), sems(4), sems(2),
+            sems(1), sems(1), sems(4), sems(4), sems(3),
         ],
         compiler_params=pltpu.CompilerParams(
             collective_id=0, has_side_effects=True, vmem_limit_bytes=64 * 1024 * 1024 - 512 * 1024
@@ -1262,9 +1272,9 @@
             like(1, HALF),
         ),
         in_specs=[any_space, vmem, any_space],
-        out_specs=[any_space] + [vmem] * 14,
+        out_specs=[vmem] * 15,
         scratch_shapes=[pltpu.VMEM((4, HALF, C_ONE), bf16), sems(5)],
-        compiler_params=pltpu.CompilerParams(vmem_limit_bytes=32 * 1024 * 1024),
+        compiler_params=pltpu.CompilerParams(vmem_limit_bytes=63 * 1024 * 1024),
     )(out, pts, packed)
     return (
         output, points_grad, hidden_w[None], hidden_b, tok, res_t.T, tok_b[0], gain1[0], qkv.transpose(1, 0, 2), att,

time: 180 us -> 177 us (0.983)
  local copies, waits for them, and re-layouts: 3.12 us -> 0 us
    unnamed x6 -> x0, local copies, waits for them, and re-layouts: 3.12 us -> none
where the time goes in v5:
time: 177 us
  Pallas kernels  176 us (99%)
    pallas_call x1, Pallas kernels, fast_body(): pl.pallas_call(layer_kernel, out_shape=(jax.ShapeDtypeStruct((OWN, D), bf...  172 us
    pallas_call x1, Pallas kernels, fast_body(): pl.pallas_call(unpack_kernel, out_shape=(jax.ShapeDtypeStruct((OWN, D), b...  4.13 us

profile of v5, /device:TPU:0, one launch (start us, length us, event | category | flops | bytes accessed | tf_op | source)
XLA Modules:
  0.0 176.6 jit_solution(3454299836460850496)
XLA Ops:
  0.7 171.6 %shard_map.298 = (bf16[192,1280]{1,0:T(8,128)(2,1)}, f32[12,512]{1,0:T(8,128)}, bf16[4,80,2176]{2,1,0:T(8,128)(2,1)}) custom-call(bf16[12,512]{1,0:T(8,128)(2,1)} %points.1, s32[12,512]{1,0:T(8,128)} %missing.1, bf16[40,64]{1,0:T(8,128)(2,1)} %bitcast.18, bf16[1,40]{1,0:T(2,128)(2,1)} %hid_b.1, bf16[80,640]{1,0:T(8,128)(2,1)} %tok_in.1, ...), custom_call_target="tpu_custom_call" | custom-call | flops 12999999488 | bytes 10000000 | tf_op jit(solution)/shard_map/pallas_call | solution.py:1190
  172.2 4.1 %shard_map.299 = (bf16[192,1280]{1,0:T(8,128)(2,1)}, f32[12,512]{1,0:T(8,128)}, f32[40,64]{1,0:T(8,128)}, f32[1,40]{1,0:T(1,128)}, f32[80,640]{1,0:T(8,128)}, /*...) custom-call(bf16[192,1280]{1,0:T(8,128)(2,1)} %get-tuple-element.33., ...), custom_call_target="tpu_custom_call" | custom-call | tf_op jit(solution)/shard_map/pallas_call | solution.py:1266

commit v6 on v5

--- a/solution.py
+++ b/solution.py
@@ -317,7 +317,7 @@
     (2688, 0, 256, 1792),
     (2944, 0, 128, 2048),
 )
-GATHER_ORDER = ("zxy", "zyx", "zyx", "zyx", "zxy", "zy", "zy", "zy", "zy", "zy")
+GATHER_ORDER = ("zyx", "zxy", "zyx", "zyx", "zxy", "zy", "zy", "zy", "zy", "zy")
 SUM_ORDER = ("xyz", "xyz", "yxz", "xyz", "xyz", "yz", "yz", "yz", "yz", "yz")
 (
     FIRST, OWNED, SECOND, THIRD, HERE, SUM, FEATS, COT, COT_HERE, TOKENS, VECTORS, NORM_1, PROJECT, TURN, ATTEND,
@@ -325,24 +325,24 @@
     D_HID, GRAD_TOK, GRAD_HID, POINTS, SEND, PASS, COT_PASS, NORM_PASS, CROSS, HIDDEN,
 ) = range(38)
 PLAN = (
-    (FIRST, 0), (FIRST, 1), (FIRST, 4), (FIRST, 9), (FIRST, 3), (OWNED, 0), (OWNED, 1), (FIRST, 8), (OWNED, 4),
-    (FIRST, 2), (FEATS,), (FIRST, 7), (FIRST, 5), (OWNED, 9), (OWNED, 3), (SECOND, 0), (FIRST, 6), (SECOND, 1),
-    (THIRD, 0), (THIRD, 1), (OWNED, 2), (OWNED, 7), (HERE, 1), (HERE, 0), (HIDDEN,), (TOKENS, 1), (SEND, 0, 1),
-    (SECOND, 4), (TOKENS, 0), (PASS, 0, 1), (SECOND, 3), (SEND, 0, 0), (OWNED, 5), (THIRD, 3), (PASS, 0, 0),
-    (SECOND, 2), (OWNED, 6), (COT,), (THIRD, 2), (VECTORS,), (HERE, 3), (NORM_1, 1), (THIRD, 4), (NORM_1, 0),
-    (HERE, 4), (HERE, 2), (PROJECT, 1), (SECOND, 5), (OWNED, 8), (PROJECT, 0), (TURN, 1), (SECOND, 7), (ATTEND, 1),
-    (SEND, 1, 1), (PASS, 1, 1), (TURN, 0), (ATTEND, 0), (SEND, 1, 0), (COT_PASS, 0), (PASS, 1, 0), (SECOND, 6),
-    (SECOND, 8), (NORM_2, 1), (SECOND, 9), (COT_PASS, 1), (NORM_2, 0), (HERE, 6), (COT_HERE,), (HERE, 7),
-    (NORM_PASS, 1), (HERE, 5), (INNER, 0, 0), (HERE, 9), (HERE, 8), (INNER, 0, 1), (INNER, 1, 1), (OUTER, 1),
-    (SEND, 2, 1), (NORM_PASS, 0), (CROSS, 2, 1), (INNER, 1, 0), (GRAD_OUT, 9), (OUTER, 0), (GRAD_IN, 6), (SEND, 2, 0),
-    (PASS, 2, 1), (SUM, 9), (CROSS, 2, 0), (SEND, 3, 1), (SEND, 3, 0), (GRAD_OUT, 7), (GRAD_OUT, 8), (PASS, 2, 0),
-    (BACK_2, 1), (SUM, 6), (CROSS, 3, 0), (CROSS, 3, 1), (D_ATT, 1), (ATTEND_B, 1), (TURN_B, 1), (SEND, 4, 1),
-    (SUM, 7), (PASS, 4, 1), (BACK_2, 0), (GRAD_IN, 5), (D_ATT, 0), (GRAD_QKV, 4), (ATTEND_B, 0), (TURN_B, 0),
-    (SEND, 4, 0), (GRAD_BIAS,), (PASS, 4, 0), (GRAD_QKV, 3), (SUM, 4), (SUM, 5), (GRAD_QKV, 2), (BACK_1, 1), (SUM, 5),
-    (SUM, 8), (PASS, 3, 0), (BACK_1, 0), (SUM, 6), (SUM, 4), (D_HID, 0), (D_HID, 1), (SUM, 6), (SUM, 3), (SUM, 2),
-    (SUM, 4), (SUM, 8), (GRAD_TOK,), (SUM, 2), (SUM, 9), (SUM, 8), (GRAD_HID,), (SUM, 7), (SUM, 7), (SUM, 2),
-    (SUM, 3), (SUM, 4), (SUM, 0), (POINTS, 0), (FINISH,), (SUM, 3), (POINTS, 1), (SUM, 0), (SUM, 2), (SUM, 1),
-    (SUM, 1), (SUM, 3), (SUM, 0), (SUM, 0), (SUM, 5), (SUM, 1), (POINTS, 2), (SUM, 1), (SUM, 9), (POINTS, 3),
+    (FIRST, 1), (FIRST, 0), (FIRST, 3), (FIRST, 4), (OWNED, 1), (FIRST, 2), (OWNED, 0), (FIRST, 5), (FIRST, 9),
+    (OWNED, 3), (FEATS,), (FIRST, 6), (SECOND, 1), (OWNED, 4), (SECOND, 0), (THIRD, 1), (THIRD, 0), (OWNED, 2),
+    (FIRST, 8), (HERE, 1), (FIRST, 7), (SECOND, 3), (HERE, 0), (OWNED, 5), (HIDDEN,), (VECTORS,), (TOKENS, 1),
+    (SEND, 0, 1), (TOKENS, 0), (SECOND, 4), (PASS, 0, 1), (SEND, 0, 0), (THIRD, 3), (OWNED, 6), (OWNED, 7),
+    (PASS, 0, 0), (SECOND, 2), (NORM_1, 1), (THIRD, 4), (COT,), (SECOND, 5), (THIRD, 2), (OWNED, 8), (HERE, 3),
+    (HERE, 2), (PROJECT, 1), (TURN, 1), (NORM_1, 0), (HERE, 4), (ATTEND, 1), (SEND, 1, 1), (SECOND, 6), (PASS, 1, 1),
+    (PROJECT, 0), (TURN, 0), (ATTEND, 0), (SEND, 1, 0), (COT_PASS, 0), (SECOND, 8), (PASS, 1, 0), (NORM_2, 1),
+    (OWNED, 9), (HERE, 5), (COT_PASS, 1), (SECOND, 7), (NORM_2, 0), (SECOND, 9), (NORM_PASS, 1), (HERE, 6),
+    (INNER, 0, 1), (HERE, 7), (HERE, 8), (COT_HERE,), (INNER, 1, 1), (INNER, 0, 0), (HERE, 9), (OUTER, 1),
+    (NORM_PASS, 0), (SEND, 2, 1), (INNER, 1, 0), (CROSS, 2, 1), (GRAD_OUT, 7), (OUTER, 0), (SEND, 2, 0), (SEND, 3, 0),
+    (PASS, 2, 1), (CROSS, 2, 0), (GRAD_OUT, 8), (SUM, 7), (GRAD_IN, 6), (GRAD_IN, 5), (PASS, 2, 0), (BACK_2, 1),
+    (CROSS, 3, 0), (SEND, 3, 1), (D_ATT, 1), (SUM, 8), (ATTEND_B, 1), (TURN_B, 1), (SEND, 4, 1), (CROSS, 3, 1),
+    (SUM, 8), (PASS, 4, 1), (BACK_2, 0), (GRAD_OUT, 9), (SUM, 6), (D_ATT, 0), (GRAD_QKV, 4), (ATTEND_B, 0),
+    (TURN_B, 0), (SEND, 4, 0), (GRAD_QKV, 3), (PASS, 4, 0), (SUM, 5), (SUM, 4), (GRAD_QKV, 2), (GRAD_BIAS,), (SUM, 9),
+    (BACK_1, 1), (SUM, 9), (SUM, 7), (SUM, 6), (D_HID, 1), (SUM, 4), (SUM, 3), (BACK_1, 0), (PASS, 3, 0), (SUM, 6),
+    (D_HID, 0), (POINTS, 0), (SUM, 2), (SUM, 8), (GRAD_TOK,), (SUM, 2), (SUM, 9), (SUM, 7), (GRAD_HID,), (SUM, 5),
+    (SUM, 4), (FINISH,), (POINTS, 1), (SUM, 2), (SUM, 3), (SUM, 0), (SUM, 4), (SUM, 0), (SUM, 1), (SUM, 2), (SUM, 1),
+    (SUM, 5), (SUM, 0), (SUM, 1), (POINTS, 2), (SUM, 3), (SUM, 0), (SUM, 3), (SUM, 1), (POINTS, 3),
 )
 L_RES, L_ONE, L_VEC, L_BIN, L_HID = 32, 40, 41, 45, 47
 TILE = 256

time: 177 us -> 176 us (level)
  no operation moved by 1% of the time
where the time goes in v6:
time: 176 us
  Pallas kernels  175 us (99%)
    pallas_call x1, Pallas kernels, fast_body(): pl.pallas_call(layer_kernel, out_shape=(jax.ShapeDtypeStruct((OWN, D), bf...  171 us
    pallas_call x1, Pallas kernels, fast_body(): pl.pallas_call(unpack_kernel, out_shape=(jax.ShapeDtypeStruct((OWN, D), b...  4.13 us

profile of v6, /device:TPU:0, one launch (start us, length us, event | category | flops | bytes accessed | tf_op | source)
XLA Modules:
  0.0 175.9 jit_solution(4760114872723938410)
XLA Ops:
  0.7 170.9 %shard_map.298 = (bf16[192,1280]{1,0:T(8,128)(2,1)}, f32[12,512]{1,0:T(8,128)}, bf16[4,80,2176]{2,1,0:T(8,128)(2,1)}) custom-call(bf16[12,512]{1,0:T(8,128)(2,1)} %points.1, s32[12,512]{1,0:T(8,128)} %missing.1, bf16[40,64]{1,0:T(8,128)(2,1)} %bitcast.18, bf16[1,40]{1,0:T(2,128)(2,1)} %hid_b.1, bf16[80,640]{1,0:T(8,128)(2,1)} %tok_in.1, ...), custom_call_target="tpu_custom_call" | custom-call | flops 12999999488 | bytes 10000000 | tf_op jit(solution)/shard_map/pallas_call | solution.py:1190
  171.5 4.1 %shard_map.299 = (bf16[192,1280]{1,0:T(8,128)(2,1)}, f32[12,512]{1,0:T(8,128)}, f32[40,64]{1,0:T(8,128)}, f32[1,40]{1,0:T(1,128)}, f32[80,640]{1,0:T(8,128)}, /*...) custom-call(bf16[192,1280]{1,0:T(8,128)(2,1)} %get-tuple-element.33., ...), custom_call_target="tpu_custom_call" | custom-call | tf_op jit(solution)/shard_map/pallas_call | solution.py:1266

commit v7 on v6

--- a/solution.py
+++ b/solution.py
@@ -406,7 +406,7 @@
         remote(ref, ref, sem, sem, mate).wait_send()
 
     barrier = pltpu.get_barrier_semaphore()
-    peers = (mate, beside, corner, along["z"], along["y"], along["x"])
+    peers = (along["z"], corner, beside, along["y"], along["x"], mate)
     for to in peers:
         pl.semaphore_signal(barrier, inc=1, device_id=to, device_id_type=MESH)
 

time: 176 us -> 176 us (level)
  no operation moved by 1% of the time
where the time goes in v7:
time: 176 us
  Pallas kernels  175 us (99%)
    pallas_call x1, Pallas kernels, fast_body(): pl.pallas_call(layer_kernel, out_shape=(jax.ShapeDtypeStruct((OWN, D), bf...  171 us
    pallas_call x1, Pallas kernels, fast_body(): pl.pallas_call(unpack_kernel, out_shape=(jax.ShapeDtypeStruct((OWN, D), b...  4.13 us

profile of v7, /device:TPU:0, one launch (start us, length us, event | category | flops | bytes accessed | tf_op | source)
XLA Modules:
  0.0 175.9 jit_solution(3035354904013207430)
XLA Ops:
  0.7 170.9 %shard_map.298 = (bf16[192,1280]{1,0:T(8,128)(2,1)}, f32[12,512]{1,0:T(8,128)}, bf16[4,80,2176]{2,1,0:T(8,128)(2,1)}) custom-call(bf16[12,512]{1,0:T(8,128)(2,1)} %points.1, s32[12,512]{1,0:T(8,128)} %missing.1, bf16[40,64]{1,0:T(8,128)(2,1)} %bitcast.18, bf16[1,40]{1,0:T(2,128)(2,1)} %hid_b.1, bf16[80,640]{1,0:T(8,128)(2,1)} %tok_in.1, ...), custom_call_target="tpu_custom_call" | custom-call | flops 12999999488 | bytes 10000000 | tf_op jit(solution)/shard_map/pallas_call | solution.py:1190
  171.5 4.1 %shard_map.299 = (bf16[192,1280]{1,0:T(8,128)(2,1)}, f32[12,512]{1,0:T(8,128)}, f32[40,64]{1,0:T(8,128)}, f32[1,40]{1,0:T(1,128)}, f32[80,640]{1,0:T(8,128)}, /*...) custom-call(bf16[192,1280]{1,0:T(8,128)(2,1)} %get-tuple-element.33., ...), custom_call_target="tpu_custom_call" | custom-call | tf_op jit(solution)/shard_map/pallas_call | solution.py:1266
